TPU v7x, 32 devices: a whole 2x2x4 slice. The times are simulated.
32 devices in a mesh: groups: 2 (over x), feat: 8 (over z, y), rep: 2 (over core).
Axes of the slice: x: 2, y: 2, z: 4, core: 2. Of those that a mesh axis runs over, the one named last changes fastest.
Arguments:
- seed_feat: bfloat16 [4, 768, 256], P(('groups', 'rep'), 'feat'), parts along dimension 0, may hold values from -6 to 6
- hop_feat: bfloat16 [4, 768, 8, 256], P(('groups', 'rep'), 'feat'), parts along dimension 0, may hold values from -6 to 6
- frontier: bfloat16 [4, 768, 6144], P(('groups', 'rep'), 'feat'), parts along dimension 0, may hold values from -6 to 6
- nbr_index: int32 [4, 4, 8, 256], P(('groups', 'rep')), parts along dimension 0, may hold values from 0 to 6143
- hop_degree: int32 [4, 8, 256], P(('groups', 'rep')), parts along dimension 0, may hold values from 1 to 4
- seed_degree: int32 [4, 256], P(('groups', 'rep')), parts along dimension 0, may hold values from 1 to 8
- w_self: bfloat16 [768, 512], P('feat'), may hold values from -0.21875 to 0.21875
- w_neigh: bfloat16 [768, 512], P('feat'), may hold values from -0.21875 to 0.21875
- v_self: bfloat16 [512, 153], replicated, may hold values from -0.25 to 0.25
- v_neigh: bfloat16 [512, 153], replicated, may hold values from -0.25 to 0.25
- cotangent: bfloat16 [4, 256, 153], P(('groups', 'rep'), 'feat'), parts along dimension 0, may hold values from -6 to 6
Outputs:
- logits: bfloat16 [4, 256, 153], P(('groups', 'rep'), 'feat'), parts along dimension 0
- grad_w_self: float32 [1536, 512], P(('groups', 'feat')), parts along dimension 0
- grad_w_neigh: float32 [1536, 512], P(('groups', 'feat')), parts along dimension 0
- grad_v_self: float32 [1024, 153], P('groups'), parts along dimension 0
- grad_v_neigh: float32 [1024, 153], P('groups'), parts along dimension 0
There are 2 independent parts, one for each index of `groups`. A program takes and returns all parts, laid end to end along the dimension named above; an argument that names none is the same for every part. Nothing has to cross between parts.
Inputs may be any that keep to these rules, and one draw needn't show every extreme that they name: nbr_index names a column of its own half's frontier.
All inputs are finite; a program needn't handle non-finite values.
Results may differ from a plain program's by a relative error of at most 0.0075.
Values may be sent and summed in bfloat16 or wider, within the bound.
No kernel may reach another device: no remote copies, remote signals or barrier semaphores. Data moves between devices by JAX's collectives and lax.ppermute only.
A program may use at most 128 MiB of HBM per device.

v0:
```python
import jax
import jax.numpy as jnp
from jax import lax
from jax.sharding import PartitionSpec as P


def neighbour_mean(table, nbr_index, hop_degree):
    total = jnp.zeros((table.shape[0],) + nbr_index.shape[1:], jnp.float32)
    for slot_index in range(nbr_index.shape[0]):
        picked = jnp.take(table, nbr_index[slot_index], axis=1).astype(jnp.float32)
        live_slot = (hop_degree > slot_index).astype(jnp.float32)
        total = total + picked * live_slot[None]
    return (total / hop_degree.astype(jnp.float32)[None]).astype(jnp.bfloat16)


def seed_average(hop_feat, seed_degree):
    fan_count = hop_feat.shape[1]
    live_slot = (jnp.arange(fan_count, dtype=jnp.int32)[:, None] < seed_degree[None, :]).astype(
        jnp.float32
    )
    total = jnp.sum(hop_feat.astype(jnp.float32) * live_slot[None], axis=1)
    return (total / seed_degree.astype(jnp.float32)[None]).astype(jnp.bfloat16)


def project_rows(own_part, agg_part, w_self, w_neigh):
    first = jnp.einsum("fkn,fh->nkh", own_part, w_self, preferred_element_type=jnp.float32)
    second = jnp.einsum("fkn,fh->nkh", agg_part, w_neigh, preferred_element_type=jnp.float32)
    return first + second


def on_device(
    seed_feat,
    hop_feat,
    frontier,
    nbr_index,
    hop_degree,
    seed_degree,
    w_self,
    w_neigh,
    v_self,
    v_neigh,
    cotangent,
):
    hop_local = hop_feat[0]
    hop_mean = neighbour_mean(frontier[0], nbr_index[0], hop_degree[0])
    seed_mean = seed_average(hop_local, seed_degree[0])
    own_all = jnp.concatenate([seed_feat[0][:, None], hop_local], axis=1)
    agg_all = jnp.concatenate([seed_mean[:, None], hop_mean], axis=1)
    slots = own_all.shape[1]
    hidden_width = w_self.shape[1]
    owned_seeds = cotangent.shape[1]
    position = lax.axis_index("feat")
    my_degree = lax.dynamic_slice_in_dim(seed_degree[0], position * owned_seeds, owned_seeds)
    own_part = own_all
    agg_part = agg_all
    summed = lax.psum_scatter(
        project_rows(own_part, agg_part, w_self, w_neigh).reshape(
            owned_seeds * lax.axis_size("feat"), slots * hidden_width
        ),
        "feat",
        scatter_dimension=0,
        tiled=True,
    )
    pre = summed.reshape(owned_seeds, slots, hidden_width)
    sigma = jax.nn.sigmoid(pre)
    hidden = (pre * sigma).astype(jnp.bfloat16)
    fan_count = slots - 1
    live_slot = (jnp.arange(fan_count, dtype=jnp.int32)[None, :] < my_degree[:, None]).astype(
        jnp.float32
    )
    degree_f = my_degree.astype(jnp.float32)
    hidden_mean = (
        jnp.sum(hidden[:, 1:].astype(jnp.float32) * live_slot[:, :, None], axis=1)
        / degree_f[:, None]
    ).astype(jnp.bfloat16)
    seed_hidden = hidden[:, 0]
    logits = (
        jnp.dot(seed_hidden, v_self, preferred_element_type=jnp.float32)
        + jnp.dot(hidden_mean, v_neigh, preferred_element_type=jnp.float32)
    ).astype(jnp.bfloat16)
    cot_local = cotangent[0]
    over_rows = (((0,), (0,)), ((), ()))
    grad_v_self = lax.dot_general(
        seed_hidden, cot_local, over_rows, preferred_element_type=jnp.float32
    )
    grad_v_neigh = lax.dot_general(
        hidden_mean, cot_local, over_rows, preferred_element_type=jnp.float32
    )
    grad_v_self, grad_v_neigh = lax.psum((grad_v_self, grad_v_neigh), ("feat", "rep"))
    over_classes = (((1,), (1,)), ((), ()))
    back_seed = lax.dot_general(cot_local, v_self, over_classes, preferred_element_type=jnp.float32)
    back_mean = lax.dot_general(
        cot_local, v_neigh, over_classes, preferred_element_type=jnp.float32
    )
    back_hops = back_mean[:, None, :] * live_slot[:, :, None] / degree_f[:, None, None]
    back = jnp.concatenate([back_seed[:, None, :], back_hops], axis=1)
    slope = sigma * (1.0 + pre * (1.0 - sigma))
    dpre = (back * slope).astype(jnp.bfloat16)
    grad_piece = lax.all_gather(
        dpre.reshape(owned_seeds, slots * hidden_width), "feat", axis=0, tiled=True
    )
    row_count = grad_piece.shape[0]
    own_part = own_all
    agg_part = agg_all
    piece_rows = grad_piece.reshape(row_count, slots, hidden_width)
    extra_self = jnp.einsum("fkn,nkh->fh", own_part, piece_rows, preferred_element_type=jnp.float32)
    extra_neigh = jnp.einsum(
        "fkn,nkh->fh", agg_part, piece_rows, preferred_element_type=jnp.float32
    )
    grad_w_self = extra_self
    grad_w_neigh = extra_neigh
    grad_w_self, grad_w_neigh = (
        lax.psum(grad_w_self.astype(jnp.bfloat16), "rep").astype(jnp.float32),
        lax.psum(grad_w_neigh.astype(jnp.bfloat16), "rep").astype(jnp.float32),
    )
    return (logits[None], grad_w_self, grad_w_neigh, grad_v_self, grad_v_neigh)


def solution(mesh):
    placed = (
        P(("groups", "rep"), "feat", None),
        P(("groups", "rep"), "feat", None, None),
        P(("groups", "rep"), "feat", None),
        P(("groups", "rep"), None, None, None),
        P(("groups", "rep"), None, None),
        P(("groups", "rep"), None),
        P("feat", None),
        P("feat", None),
        P(),
        P(),
        P(("groups", "rep"), "feat", None),
    )
    return jax.shard_map(
        on_device,
        mesh=mesh,
        in_specs=placed,
        out_specs=(
            P(("groups", "rep"), "feat", None),
            P(("groups", "feat"), None),
            P(("groups", "feat"), None),
            P("groups", None),
            P("groups", None),
        ),
        check_vma=False,
    )
```

profile of v0, /device:TPU:0, one launch (start us, length us, event | category | flops | bytes accessed | tf_op | source)
XLA Modules:
  0.0 345.0 jit_solution(15176823551008482406)
XLA Ops:
  7.2 0.0 copy-start
  7.2 0.0 reduce-scatter.4.cloned.1.call-start
  7.2 0.8 fusion.22
  8.0 1.4 compare_and_fusion.3
  9.4 1.3 convert_bitcast_fusion.3
  10.7 1.3 convert_bitcast_fusion.4
  12.0 1.8 copy.36
  13.8 6.2 %gather_fusion = bf16[2048,96]{1,0:T(8,128)(2,1)S(1)} fusion(bf16[96,6144]{0,1:T(8,128)(2,1)S(1)} %bitcast.120, s32[2048]{0:T(1024)S(1)} %broadcast_clamp_fusion.3), kind=kCustom, calls=%fused_computation.clone | custom fusion | bytes 794624 | tf_op jit(solution)/shard_map/jit(_take)/gather | solution.py:10
  20.0 0.2 copy.38
  20.3 6.2 %gather_fusion.1 = bf16[2048,96]{1,0:T(8,128)(2,1)S(1)} fusion(bf16[96,6144]{0,1:T(8,128)(2,1)S(1)} %bitcast.121, s32[2048]{0:T(1024)S(1)} %broadcast_clamp_fusion.2), kind=kCustom, calls=%fused_computation.1.clone | custom fusion | bytes 794624 | tf_op jit(solution)/shard_map/jit(_take)/gather | solution.py:10
  26.5 0.2 copy.40
  26.7 6.2 %gather_fusion.2 = bf16[2048,96]{1,0:T(8,128)(2,1)S(1)} fusion(bf16[96,6144]{0,1:T(8,128)(2,1)S(1)} %bitcast.122, s32[2048]{0:T(1024)S(1)} %broadcast_clamp_fusion.1), kind=kCustom, calls=%fused_computation.2.clone | custom fusion | bytes 794624 | tf_op jit(solution)/shard_map/jit(_take)/gather | solution.py:10
  32.9 1.0 copy.42
  33.9 0.0 copy-start.6
  33.9 6.2 %gather_fusion.3 = bf16[2048,96]{1,0:T(8,128)(2,1)S(1)} fusion(bf16[96,6144]{0,1:T(8,128)(2,1)S(1)} %bitcast.123, s32[2048]{0:T(1024)S(1)} %broadcast_clamp_fusion), kind=kCustom, calls=%fused_computation.3.clone | custom fusion | bytes 794624 | tf_op jit(solution)/shard_map/jit(_take)/gather | solution.py:10
  40.1 0.0 copy-start.11
  40.1 0.2 copy.44
  40.3 0.1 copy.83
  40.4 0.1 multiply_reduce_fusion
  40.6 0.4 copy-done.11
  41.0 0.0 copy-start.10
  41.1 0.8 fusion.4
  41.9 0.1 copy-done.3
  42.0 0.6 divide_convert_fusion
  42.6 3.0 add_bitcast_fusion
  45.6 6.1 %copy.45 = f32[256,9,512]{0,2,1:T(8,128)} copy(f32[256,9,512]{2,0,1:T(8,128)} %add_bitcast_fusion) | data formatting | bytes 9437184 | tf_op jit(solution)/shard_map/add | solution.py:28
  51.7 6.1 %copy.64 = f32[256,4608]{1,0:T(8,128)} copy(f32[256,4608]{0,1:T(8,128)} %bitcast.126) | data formatting | bytes 9437184
  57.8 0.0 reduce-scatter.4.cloned.1.call-update
  57.8 0.0 all-gather.2.cloned.1.call-start
  57.9 0.6 copy-done.4
  58.5 0.1 convolution_bitcast_fusion.2
  58.6 0.1 copy.47
  58.7 0.6 fusion.30
  59.3 0.7 fusion.18
  60.0 0.1 fusion.15
  60.1 95.8 %reduce-scatter.4.cloned.1.call-done = f32[32,4608]{1,0:T(8,128)} async-done(((f32[256,4608]{1,0:T(8,128)}), f32[32,4608]{1,0:T(8,128)}) %reduce-scatter.4.cloned.1.call-update) | async-done | bytes 589840 | tf_op jit(solution)/shard_map/reduce_scatter | solution.py:56
  155.9 1.7 copy.65
  157.6 2.4 copy.63
  160.0 1.5 multiply_convert_fusion
  161.5 1.1 multiply_divide_fusion
  162.6 0.0 copy-start.5
  162.6 0.2 pad_maximum_fusion
  162.8 0.3 copy.71
  163.2 0.9 multiply_convert_fusion.1
  164.1 0.0 all-gather.2.cloned.1.call-update
  164.1 0.0 all-reduce.7.cloned.1.call-start
  164.2 1.0 fusion.12
  165.2 50.9 %all-gather.2.cloned.1.call-done = bf16[256,4608]{1,0:T(8,128)(2,1)} async-done(((bf16[32,4608]{1,0:T(8,128)(2,1)}), bf16[256,4608]{1,0:T(8,128)(2,1)}) %all-gather.2.cloned.1.call-update) | async-done | bytes 2359312 | tf_op jit(solution)/shard_map/all_gather | solution.py:99
  216.1 2.8 copy.50
  219.0 1.5 fusion.1
  220.4 1.5 fusion
  221.9 0.0 all-reduce.7.cloned.1.call-update
  221.9 0.0 all-reduce.5.cloned.1.call-start
  222.0 1.0 fusion.8
  223.0 0.0 all-reduce.5.cloned.1.call-update
  223.0 0.1 fusion.10
  223.1 0.0 copy-done.9
  223.2 0.8 fusion.3
  224.0 14.8 %all-reduce.7.cloned.1.call-done = (bf16[96,512]{1,0:T(8,128)(2,1)}, bf16[96,512]{1,0:T(8,128)(2,1)}) async-done(((bf16[96,512]{1,0:T(8,128)(2,1)}, bf16[96,512]{1,0:T(8,128)(2,1)}), (bf16[96,512]{1,0:T(8,128)(2,1)}, bf16[96,512]{1,0:T(8,128)(2,1)})) %all-reduce.7.cloned.1.call-update) | async-done | bytes 196624 | tf_op jit(solution)/shard_map/psum | solution.py:113
  238.8 1.6 convert_element_type.118
  240.4 1.6 convert_element_type.120
  242.0 93.1 %all-reduce.5.cloned.1.call-done = (f32[512,153]{0,1:T(8,128)}, f32[512,153]{0,1:T(8,128)}) async-done(((f32[512,153]{0,1:T(8,128)}, f32[512,153]{0,1:T(8,128)}), (f32[512,153]{0,1:T(8,128)}, f32[512,153]{0,1:T(8,128)})) %all-reduce.5.cloned.1.call-update) | async-done | bytes 626704 | tf_op jit(solution)/shard_map/psum | solution.py:89
  335.1 1.7 copy.88
  336.8 1.7 copy.89
  (47 shorter events, 0.2 us)
Async XLA Ops:
  7.2 50.7 %copy-start = (bf16[512,153]{0,1:T(8,128)(2,1)S(1)}, bf16[512,153]{0,1:T(8,128)(2,1)}, u32[]{:S(2)}) copy-start(bf16[512,153]{0,1:T(8,128)(2,1)} %param.21) | copy-start | bytes 470020
  7.2 148.7 %reduce-scatter.4.cloned.1.call-start = ((), (), s32[]{:S(2)}) async-start(), calls=%async_computation.2 | async-start | bytes 5308416 | tf_op jit(solution)/shard_map/reduce_scatter | solution.py:56
  33.9 6.5 %copy-start.2 = (bf16[1,96,8,256]{3,2,1,0:T(8,128)(2,1)S(1)}, bf16[1,96,8,256]{3,2,1,0:T(8,128)(2,1)}, u32[]{:S(2)}) copy-start(bf16[1,96,8,256]{3,2,1,0:T(8,128)(2,1)} %param.14) | copy-start | bytes 1179652
  33.9 6.5 %copy-start.19 = (s32[1,256]{1,0:T(1,128)S(1)}, s32[1,256]{1,0:T(1,128)}, u32[]{:S(2)}) copy-start(s32[1,256]{1,0:T(1,128)} %param.18) | copy-start | bytes 3076
  33.9 6.7 %copy-start.6 = (bf16[1,96,256]{2,1,0:T(8,128)(2,1)S(1)}, bf16[1,96,256]{2,1,0:T(8,128)(2,1)}, u32[]{:S(2)}) copy-start(bf16[1,96,256]{2,1,0:T(8,128)(2,1)} %param.13) | copy-start | bytes 147460
  40.1 0.9 copy-start.11
  41.0 1.0 copy-start.3
  41.0 1.0 copy-start.12
  41.0 1.0 copy-start.13
  41.0 1.0 copy-start.14
  41.0 1.0 copy-start.15
  41.0 1.0 copy-start.16
  41.0 1.0 copy-start.17
  41.0 1.0 copy-start.18
  41.0 1.6 copy-start.10
  57.8 0.7 copy-start.4
  57.8 0.9 copy-start.20
  57.8 2.2 copy-start.8
  57.8 158.3 %all-gather.2.cloned.1.call-start = ((), (), s32[]{:S(2)}) async-start(), calls=%async_computation.1 | async-start | bytes 2654208 | tf_op jit(solution)/shard_map/all_gather | solution.py:99
  161.5 1.6 copy-start.1
  162.6 1.6 copy-start.5
  162.6 1.6 copy-start.21
  164.1 74.7 %all-reduce.7.cloned.1.call-start = ((), (), s32[]{:S(2)}) async-start(), calls=%async_computation.4 | async-start | bytes 393216 | tf_op jit(solution)/shard_map/psum | solution.py:113
  218.9 1.5 copy-start.7
  220.4 2.7 copy-start.9
  221.9 113.1 %all-reduce.5.cloned.1.call-start = ((), (), s32[]{:S(2)}) async-start(), calls=%async_computation.3 | async-start | bytes 1310720 | tf_op jit(solution)/shard_map/psum | solution.py:89
Sparse Core Ops, SparseCore 0:
  57.9 97.9 reduce-scatter.3
  164.2 51.8 all-gather.1
  222.1 16.6 all-reduce.6
  242.7 92.3 all-reduce.4
where the time goes:
time: 346 us; the launch traced here: 345 us
  waiting for transfers between devices  255 us (74%)
  local copies, waits for them, and re-layouts  52.5 us (15%)
  between operations  14.2 us (4%)
  other arithmetic  13.6 us (4%)
  matrix products  9.92 us (3%)
    reduce_scatter x1, waiting for transfers between devices, on_device(): lax.psum_scatter(project_rows(own_part, agg_part, w_self, w_neigh).reshap...  95.8 us
    psum x1, waiting for transfers between devices, on_device(): lax.psum((grad_v_self, grad_v_neigh), ('feat', 'rep'))  93.1 us
    all_gather x1, waiting for transfers between devices, on_device(): lax.all_gather(dpre.reshape(owned_seeds, slots * hidden_width), 'feat', a...  50.9 us
    gather x8, local copies, waits for them, and re-layouts, neighbour_mean(): picked = jnp.take(table, nbr_index[slot_index], axis=1).astype(jnp.float32)  26.3 us
    psum x1, waiting for transfers between devices, on_device(): lax.psum(grad_w_self.astype(jnp.bfloat16), 'rep').astype(jnp.float32)  14.8 us
    unnamed x55, local copies, waits for them, and re-layouts  14.8 us
  transfers between devices with their start and end apart: 4, of which 4 were waited for; matrix products, arithmetic and copies ran while one was open for 2% of the time, Pallas kernels for 0%

commit v1 on v0

v1 whole, which is shorter than its diff:
```python
import jax
import jax.numpy as jnp
from jax import lax
from jax.sharding import PartitionSpec as P

F32 = jnp.float32
BF16 = jnp.bfloat16


def neighbour_mean(table, nbr_index, hop_degree):
    total = jnp.zeros((table.shape[0],) + nbr_index.shape[1:], F32)
    for slot_index in range(nbr_index.shape[0]):
        picked = jnp.take(table, nbr_index[slot_index], axis=1).astype(F32)
        live_slot = (hop_degree > slot_index).astype(F32)
        total = total + picked * live_slot[None]
    return (total / hop_degree.astype(F32)[None]).astype(BF16)


def by_owner(hop, owners):
    f, t, s = hop.shape
    return hop.reshape(f, t, owners, s // owners).transpose(2, 0, 1, 3).reshape(owners, f, -1)


def on_device(
    seed_feat,
    hop_feat,
    frontier,
    nbr_index,
    hop_degree,
    seed_degree,
    w_self,
    w_neigh,
    v_self,
    v_neigh,
    cotangent,
):
    owners = lax.axis_size("feat")
    position = lax.axis_index("feat")
    half = lax.axis_index("rep")
    seeds = cotangent.shape[1]
    width = w_self.shape[1]
    fan = hop_feat.shape[2]
    own_hop = lax.all_to_all(by_owner(hop_feat[0], owners), "feat", 0, 0, tiled=True)
    seed_out = seed_feat[0].reshape(-1, owners, seeds).transpose(1, 0, 2)
    own_seed = lax.all_to_all(seed_out, "feat", 0, 0, tiled=True).reshape(-1, seeds)
    w_half = jnp.where(half == 0, w_self, w_neigh)
    w_half = lax.all_gather(w_half, "feat", axis=0, tiled=True)
    w_full = lax.all_gather(w_half, "rep", axis=0, tiled=False)
    hop_mean = neighbour_mean(frontier[0], nbr_index[0], hop_degree[0])
    agg_hop = lax.all_to_all(by_owner(hop_mean, owners), "feat", 0, 0, tiled=True)
    own_hop = own_hop.reshape(-1, fan * seeds)
    agg_hop = agg_hop.reshape(-1, fan * seeds)
    degree = lax.dynamic_slice_in_dim(seed_degree[0], position * seeds, seeds)
    degree_f = degree.astype(F32)
    live = (jnp.arange(fan, dtype=jnp.int32)[:, None] < degree[None, :]).astype(F32)
    seed_mean = (
        jnp.sum(own_hop.reshape(-1, fan, seeds).astype(F32) * live[None], axis=1) / degree_f[None]
    ).astype(BF16)
    own = jnp.concatenate([own_hop, own_seed], axis=1)
    agg = jnp.concatenate([agg_hop, seed_mean], axis=1)
    over_first = (((0,), (0,)), ((), ()))
    pre = lax.dot_general(own, w_full[0], over_first, preferred_element_type=F32)
    pre = pre + lax.dot_general(agg, w_full[1], over_first, preferred_element_type=F32)
    sigma = jax.nn.sigmoid(pre)
    hidden = (pre * sigma).astype(BF16)
    hops = fan * seeds
    seed_hidden = hidden[hops:]
    hidden_mean = (
        jnp.sum(hidden[:hops].reshape(fan, seeds, width).astype(F32) * live[:, :, None], axis=0)
        / degree_f[:, None]
    ).astype(BF16)
    logits = (
        jnp.dot(seed_hidden, v_self, preferred_element_type=F32)
        + jnp.dot(hidden_mean, v_neigh, preferred_element_type=F32)
    ).astype(BF16)
    cot = cotangent[0]
    over_classes = (((1,), (1,)), ((), ()))
    back_seed = lax.dot_general(cot, v_self, over_classes, preferred_element_type=F32)
    back_mean = lax.dot_general(cot, v_neigh, over_classes, preferred_element_type=F32)
    back_hops = back_mean[None] * live[:, :, None] / degree_f[None, :, None]
    back = jnp.concatenate([back_hops.reshape(hops, width), back_seed], axis=0)
    dpre = (back * sigma * (1.0 + pre * (1.0 - sigma))).astype(BF16)

    def swap(x):
        return lax.ppermute(x, "rep", [(0, 1), (1, 0)])

    mine = jnp.where(half == 0, own, agg)
    other = swap(jnp.where(half == 0, agg, own))
    dpre_other = swap(dpre)
    my_hidden = jnp.where(half == 0, seed_hidden, hidden_mean)
    other_hidden = swap(jnp.where(half == 0, hidden_mean, seed_hidden))
    partial = jnp.dot(mine, dpre, preferred_element_type=F32)
    partial = partial + jnp.dot(other, dpre_other, preferred_element_type=F32)
    blocks = lax.all_to_all(
        partial.astype(BF16).reshape(owners, -1, width), "feat", 0, 0, tiled=True
    )
    grad_w = jnp.sum(blocks.astype(F32), axis=0)
    hid = jnp.concatenate([my_hidden, other_hidden], axis=0)
    hid_all = lax.all_gather(hid, "feat", axis=0, tiled=False)
    cot_all = lax.all_gather(cot, "feat", axis=0, tiled=False)
    cot_other = swap(cot_all)
    cots = jnp.concatenate([cot_all, cot_other], axis=1)
    grad_v = lax.dot_general(
        hid_all, cots, (((0, 1), (0, 1)), ((), ())), preferred_element_type=F32
    )
    grad_w = lax.all_gather(grad_w, "rep", axis=0, tiled=False)
    grad_v = lax.all_gather(grad_v, "rep", axis=0, tiled=False)
    return (logits[None], grad_w[0], grad_w[1], grad_v[0], grad_v[1])


def solution(mesh):
    placed = (
        P(("groups", "rep"), "feat", None),
        P(("groups", "rep"), "feat", None, None),
        P(("groups", "rep"), "feat", None),
        P(("groups", "rep"), None, None, None),
        P(("groups", "rep"), None, None),
        P(("groups", "rep"), None),
        P("feat", None),
        P("feat", None),
        P(),
        P(),
        P(("groups", "rep"), "feat", None),
    )
    return jax.shard_map(
        on_device,
        mesh=mesh,
        in_specs=placed,
        out_specs=(
            P(("groups", "rep"), "feat", None),
            P(("groups", "feat"), None),
            P(("groups", "feat"), None),
            P("groups", None),
            P("groups", None),
        ),
        check_vma=False,
    )
```

time: 346 us -> 219 us (0.63)
  waiting for transfers between devices: 255 us -> 14.9 us
  blocking collectives: 0 us -> 112 us
  starting transfers between devices: 0.16 us -> 19 us
  local copies, waits for them, and re-layouts: 52.5 us -> 37.4 us
    all_gather x0 -> x5, blocking collectives: none -> 112 us  [the longest x1 40.5 us: on_device(): hid_all = lax.all_gather(hid, 'feat', axis=0, tiled=False)]
    psum x2 -> x0, waiting for transfers between devices: 108 us -> none  [the longest x1 93.1 us: on_device(): lax.psum((grad_v_self, grad_v_neigh), ('feat', 'rep'))]
    reduce_scatter x1 -> x0, waiting for transfers between devices: 95.8 us -> none  [on_device(): lax.psum_scatter(project_rows(own_part, agg_part, w_self, w_neigh).reshap...]
    all_gather x1, waiting for transfers between devices: 50.9 us -> 0.01 us  [on_device(): w_full = lax.all_gather(w_half, 'rep', axis=0, tiled=False)]
    all_to_all x0 -> x4, starting transfers between devices: none -> 18.2 us  [the longest x1 5.54 us: on_device(): lax.all_to_all(seed_out, 'feat', 0, 0, tiled=True).reshape(-1, seeds)]
    all_to_all x0 -> x4, waiting for transfers between devices: none -> 14.4 us  [the longest x1 8.89 us: on_device(): lax.all_to_all(by_owner(hop_mean, owners), 'feat', 0, 0, tiled=True)]
    unnamed x55 -> x41, local copies, waits for them, and re-layouts: 14.8 us -> 3.23 us
    add x1 -> x0, local copies, waits for them, and re-layouts: 6.08 us -> none  [project_rows(): return first + second]
  transfers between devices with their start and end apart: 4 -> 9, of which waited for: 4 -> 3; matrix products, arithmetic and copies ran while one was open for 2% -> 25% of each run, Pallas kernels for 0% -> 0%
where the time goes in v1:
time: 219 us; the launch traced here: 217 us
  blocking collectives  112 us (51%)
  local copies, waits for them, and re-layouts  37.4 us (17%)
  starting transfers between devices  19 us (9%)
  waiting for transfers between devices  14.9 us (7%)
  between operations  14.5 us (7%)
  other arithmetic  11.2 us (5%)
  matrix products  8.21 us (4%)
    all_gather x1, blocking collectives, on_device(): hid_all = lax.all_gather(hid, 'feat', axis=0, tiled=False)  40.5 us
    all_gather x1, blocking collectives, on_device(): w_half = lax.all_gather(w_half, 'feat', axis=0, tiled=True)  36.2 us
    all_gather x1, blocking collectives, on_device(): cot_all = lax.all_gather(cot, 'feat', axis=0, tiled=False)  31.1 us
    gather x4, local copies, waits for them, and re-layouts, neighbour_mean(): picked = jnp.take(table, nbr_index[slot_index], axis=1).astype(F32)  28.3 us
    all_to_all x1, waiting for transfers between devices, on_device(): lax.all_to_all(by_owner(hop_mean, owners), 'feat', 0, 0, tiled=True)  8.89 us
    all_to_all x1, starting transfers between devices, on_device(): lax.all_to_all(seed_out, 'feat', 0, 0, tiled=True).reshape(-1, seeds)  5.54 us
    all_to_all x1, waiting for transfers between devices, on_device(): lax.all_to_all(by_owner(hop_feat[0], owners), 'feat', 0, 0, tiled=True)  5.52 us
    all_to_all x1, starting transfers between devices, on_device(): lax.all_to_all(by_owner(hop_feat[0], owners), 'feat', 0, 0, tiled=True)  5.41 us
  transfers between devices with their start and end apart: 9, of which 3 were waited for; matrix products, arithmetic and copies ran while one was open for 25% of the time, Pallas kernels for 0%

profile of v1, /device:TPU:0, one launch (start us, length us, event | category | flops | bytes accessed | tf_op | source)
XLA Modules:
  0.0 217.3 jit_solution(5462567481140286361)
XLA Ops:
  7.2 0.0 copy-start
  7.2 0.0 all-gather.6.cloned.1.call-start
  7.3 0.9 broadcast_select_fusion.1
  8.2 36.2 %all_gather.30 = bf16[768,512]{1,0:T(8,128)(2,1)} all-gather(bf16[96,512]{1,0:T(8,128)(2,1)S(1)} %broadcast_select_fusion.1), channel_id=1, replica_groups=mesh['groups'=2,'feat'=8,'rep'=2] {'feat'}, dimensions={0}, use_global_device_ids=true | all-gather | bytes 884736 | tf_op jit(solution)/shard_map/all_gather | solution.py:47
  44.4 0.0 all-gather.6.cloned.1.call-update
  44.4 0.7 copy.37
  45.2 5.5 %all-to-all-start.1 = ((bf16[8,96,32]{1,2,0:T(8,128)(2,1)}), bf16[8,96,32]{1,2,0:T(8,128)(2,1)S(1)}, u32[]{:S(2)}, u32[]{:S(2)}) async-start(bf16[8,96,32]{1,2,0:T(8,128)(2,1)} %bitcast.5), calls=%async_computation.1 | async-start | bytes 131072 | tf_op jit(solution)/shard_map/all_to_all | solution.py:45
  50.7 31.1 %all_gather.37 = bf16[8,32,153]{2,1,0:T(8,128)(2,1)S(1)} all-gather(bf16[1,32,153]{2,1,0:T(8,128)(2,1)S(1)} %copy-done.5), channel_id=1, replica_groups=mesh['groups'=2,'feat'=8,'rep'=2] {'feat'}, dimensions={0}, use_global_device_ids=true | all-gather | bytes 88128 | tf_op jit(solution)/shard_map/all_gather | solution.py:100
  81.8 0.0 collective-permute-start.3
  81.8 0.6 compare_and_fusion.3
  82.4 0.6 convert_bitcast_fusion.4
  83.1 0.6 broadcast_clamp_fusion
  83.7 0.6 broadcast_clamp_fusion.3
  84.3 0.9 copy.40
  85.2 6.2 %gather_fusion.1 = bf16[2048,96]{1,0:T(8,128)(2,1)S(1)} fusion(bf16[96,6144]{0,1:T(8,128)(2,1)S(1)} %bitcast.106, s32[2048]{0:T(1024)S(1)} %broadcast_clamp_fusion.2), kind=kCustom, calls=%fused_computation.1.clone | custom fusion | bytes 794624 | tf_op jit(solution)/shard_map/jit(_take)/gather | solution.py:13
  91.4 6.2 %gather_fusion.2 = bf16[2048,96]{1,0:T(8,128)(2,1)S(1)} fusion(bf16[96,6144]{0,1:T(8,128)(2,1)S(1)} %bitcast.107, s32[2048]{0:T(1024)S(1)} %broadcast_clamp_fusion.1), kind=kCustom, calls=%fused_computation.2.clone | custom fusion | bytes 794624 | tf_op jit(solution)/shard_map/jit(_take)/gather | solution.py:13
  97.6 7.2 %gather_fusion.3 = bf16[2048,96]{1,0:T(8,128)(2,1)S(1)} fusion(bf16[96,6144]{0,1:T(8,128)(2,1)S(1)} %bitcast.108, s32[2048]{0:T(1024)} %broadcast_clamp_fusion), kind=kCustom, calls=%fused_computation.3.clone | custom fusion | bytes 794624 | tf_op jit(solution)/shard_map/jit(_take)/gather | solution.py:13
  104.7 8.8 %gather_fusion = bf16[2048,96]{1,0:T(8,128)(2,1)} fusion(bf16[96,6144]{0,1:T(8,128)(2,1)S(1)} %bitcast.109, s32[2048]{0:T(1024)} %broadcast_clamp_fusion.3), kind=kCustom, calls=%fused_computation.clone | custom fusion | bytes 794624 | tf_op jit(solution)/shard_map/jit(_take)/gather | solution.py:13
  113.5 1.3 copy.34
  115.0 1.0 copy.36
  115.9 5.4 %all-to-all-start = ((bf16[8,96,256]{2,1,0:T(8,128)(2,1)}), bf16[8,96,256]{2,1,0:T(8,128)(2,1)S(1)}, u32[]{:S(2)}, u32[]{:S(2)}) async-start(bf16[8,96,256]{2,1,0:T(8,128)(2,1)} %copy.36), calls=%async_computation | async-start | bytes 786432 | tf_op jit(solution)/shard_map/all_to_all | solution.py:43
  121.4 5.3 %divide_convert_fusion = bf16[96,8,256]{0,2,1:T(8,128)(2,1)S(1)} fusion(bf16[8,256,96]{2,1,0:T(8,128)(2,1)S(1)} %bitcast.120, bf16[8,256,96]{2,1,0:T(8,128)(2,1)S(1)} %bitcast.119, bf16[8,256,96]{2,1,0:T(8,128)(2,1)S(1)} %bitcast.118, bf16[8,256,96]{2,1,0:T(8,128)(2,1)} %bitcast.121, f32[8,256]{1,0:T(8,128)S(1)} %copy-done.9, ...), kind=kLoop, calls=%fused_computation.11 | loop fusion | flops 3342336 | bytes 2015232 | tf_op jit(solution)/shard_map/convert_element_type | solution.py:16
  126.8 0.1 fusion.31
  126.9 1.0 copy.42
  127.9 0.1 lt.48
  128.0 0.1 lt.46
  128.1 0.1 fusion.19
  128.2 5.5 %all-to-all-done = bf16[8,96,256]{2,1,0:T(8,128)(2,1)S(1)} async-done(((bf16[8,96,256]{2,1,0:T(8,128)(2,1)}), bf16[8,96,256]{2,1,0:T(8,128)(2,1)S(1)}, u32[]{:S(2)}, u32[]{:S(2)}) %all-to-all-start) | async-done | bytes 393248 | tf_op jit(solution)/shard_map/all_to_all | solution.py:43
  133.7 3.6 %all-to-all-start.2 = ((bf16[8,96,256]{2,1,0:T(8,128)(2,1)}), bf16[8,96,256]{2,1,0:T(8,128)(2,1)S(1)}, u32[]{:S(2)}, u32[]{:S(2)}) async-start(bf16[8,96,256]{2,1,0:T(8,128)(2,1)} %copy.42), calls=%async_computation.2 | async-start | bytes 786432 | tf_op jit(solution)/shard_map/all_to_all | solution.py:50
  137.4 0.1 div.54
  137.4 0.9 fusion.11
  138.4 0.8 fusion.17
  139.2 0.1 copy.46
  139.3 0.3 copy.43
  139.6 0.3 reshape.126
  140.0 0.1 multiply_reduce_fusion
  140.1 0.1 divide_convert_fusion.1
  140.2 0.2 copy.44
  140.3 8.9 %all-to-all-done.2 = bf16[8,96,256]{2,1,0:T(8,128)(2,1)S(1)} async-done(((bf16[8,96,256]{2,1,0:T(8,128)(2,1)}), bf16[8,96,256]{2,1,0:T(8,128)(2,1)S(1)}, u32[]{:S(2)}, u32[]{:S(2)}) %all-to-all-start.2) | async-done | bytes 393248 | tf_op jit(solution)/shard_map/all_to_all | solution.py:50
  149.2 0.2 broadcast_select_fusion
  149.4 1.0 copy.45
  150.4 0.0 all-gather.6.cloned.1.call-done
  150.5 1.7 fusion.3
  152.2 0.1 copy-done.16
  152.3 0.6 fusion.6
  152.9 0.1 fusion.10
  153.1 0.5 collective-permute-start.1
  153.5 0.1 copy-done.4
  153.6 0.1 broadcast_select_fusion.3
  153.7 0.6 fusion.7
  154.3 0.4 collective-permute-done.1
  154.7 1.5 add_convert_fusion
  156.2 3.7 %all-to-all-start.3 = ((bf16[8,96,512]{2,1,0:T(8,128)(2,1)}), bf16[8,96,512]{2,1,0:T(8,128)(2,1)S(1)}, u32[]{:S(2)}, u32[]{:S(2)}) async-start(bf16[8,96,512]{2,1,0:T(8,128)(2,1)} %bitcast.35), calls=%async_computation.3 | async-start | bytes 1572864 | tf_op jit(solution)/shard_map/all_to_all | solution.py:94
  159.9 0.8 broadcast_select_fusion.2
  160.6 0.3 collective-permute-start.2
  160.9 0.9 fusion.15
  161.8 0.8 fusion.1
  162.6 40.5 %all-gather.2 = bf16[512,512]{1,0:T(8,128)(2,1)S(1)} all-gather(bf16[64,512]{1,0:T(8,128)(2,1)S(1)} %pad_maximum_fusion.6), channel_id=4, replica_groups=mesh['groups'=2,'feat'=8,'rep'=2] {'feat'}, dimensions={0}, use_global_device_ids=true | all-gather | bytes 589824 | tf_op jit(solution)/shard_map/all_gather | solution.py:99
  203.2 1.2 convolution_bitcast_fusion
  204.4 2.3 %all-gather.3 = f32[1024,153]{0,1:T(8,128)S(1)} all-gather(f32[512,153]{0,1:T(8,128)S(1)} %convolution_bitcast_fusion), channel_id=5, replica_groups=mesh['groups'=2,'feat'=8,'rep'=2] {'rep'}, dimensions={0}, use_global_device_ids=true | all-gather | bytes 940032 | tf_op jit(solution)/shard_map/all_gather | solution.py:107
  206.6 0.9 fusion.33
  207.5 0.1 convert_reduce_fusion
  207.6 2.1 all-gather.1
  209.7 0.8 fusion.34
  (54 shorter events, 0.3 us)
Async XLA Ops:
  7.2 131.2 %copy-start = (bf16[512,153]{0,1:T(8,128)(2,1)S(1)}, bf16[512,153]{0,1:T(8,128)(2,1)}, u32[]{:S(2)}) copy-start(bf16[512,153]{0,1:T(8,128)(2,1)} %param.21) | copy-start | bytes 470020
  7.2 37.2 %copy-start.8 = (bf16[1,96,256]{2,1,0:T(8,128)(2,1)S(1)}, bf16[1,96,256]{2,1,0:T(8,128)(2,1)}, u32[]{:S(2)}) copy-start(bf16[1,96,256]{2,1,0:T(8,128)(2,1)} %param.13) | copy-start | bytes 147460
  7.2 43.5 %copy-start.5 = (bf16[1,32,153]{2,1,0:T(8,128)(2,1)S(1)}, bf16[1,32,153]{2,1,0:T(8,128)(2,1)}, u32[]{:S(2)}) copy-start(bf16[1,32,153]{2,1,0:T(8,128)(2,1)} %param.23) | copy-start | bytes 29380
  7.2 143.2 %all-gather.6.cloned.1.call-start = ((), (), s32[]{:S(2)}) async-start(), calls=%async_computation.4 | async-start | bytes 2359296 | tf_op jit(solution)/shard_map/all_gather | solution.py:48
  7.3 74.5 %copy-start.6 = (s32[1,4,8,256]{3,2,1,0:T(8,128)S(1)}, s32[1,4,8,256]{3,2,1,0:T(8,128)}, u32[]{:S(2)}) copy-start(s32[1,4,8,256]{3,2,1,0:T(8,128)} %param.16) | copy-start | bytes 98308
  7.3 75.2 %copy-start.10 = (s32[1,8,256]{2,1,0:T(8,128)S(1)}, s32[1,8,256]{2,1,0:T(8,128)}, u32[]{:S(2)}) copy-start(s32[1,8,256]{2,1,0:T(8,128)} %param.17) | copy-start | bytes 24580
  8.2 76.1 %copy-start.1 = (bf16[1,96,6144]{2,1,0:T(8,128)(2,1)S(1)}, bf16[1,96,6144]{2,1,0:T(8,128)(2,1)}, u32[]{:S(2)}) copy-start(bf16[1,96,6144]{2,1,0:T(8,128)(2,1)} %param.15) | copy-start | bytes 3538948
  45.2 70.8 %all-to-all-start.1 = ((bf16[8,96,32]{1,2,0:T(8,128)(2,1)}), bf16[8,96,32]{1,2,0:T(8,128)(2,1)S(1)}, u32[]{:S(2)}, u32[]{:S(2)}) async-start(bf16[8,96,32]{1,2,0:T(8,128)(2,1)} %bitcast.5), calls=%async_computation.1 | async-start | bytes 131072 | tf_op jit(solution)/shard_map/all_to_all | solution.py:45
  81.8 121.4 %collective-permute-start.3 = (bf16[8,32,153]{2,1,0:T(8,128)(2,1)S(1)}, bf16[8,32,153]{2,1,0:T(8,128)(2,1)}, u32[]{:S(2)}, u32[]{:S(2)}) collective-permute-start(bf16[8,32,153]{2,1,0:T(8,128)(2,1)S(1)} %all_gather.37), channel_id=1, source_target_pairs={{0,1},{1,0},{2,3},{3,2},{4,5},{5,4},{6,7},{7,6},{8,9},{9,8},{10,11... | collective-permute-start | bytes 235016 | tf_op jit(solution)/shard_map/ppermute | solution.py:85
  114.9 6.5 %copy-start.9 = (f32[8,256]{1,0:T(8,128)S(1)}, f32[8,256]{1,0:T(8,128)}, u32[]{:S(2)}) copy-start(f32[8,256]{1,0:T(8,128)} %convert_bitcast_fusion.4) | copy-start | bytes 24580
  114.9 6.5 %copy-start.11 = (pred[8,256]{1,0:T(8,128)(4,1)S(1)}, pred[8,256]{1,0:T(8,128)(4,1)}, u32[]{:S(2)}) copy-start(pred[8,256]{1,0:T(8,128)(4,1)} %get-tuple-element.16) | copy-start | bytes 6148
  114.9 6.5 %copy-start.12 = (pred[8,256]{1,0:T(8,128)(4,1)S(1)}, pred[8,256]{1,0:T(8,128)(4,1)}, u32[]{:S(2)}) copy-start(pred[8,256]{1,0:T(8,128)(4,1)} %get-tuple-element.17) | copy-start | bytes 6148
  114.9 6.5 %copy-start.13 = (pred[8,256]{1,0:T(8,128)(4,1)S(1)}, pred[8,256]{1,0:T(8,128)(4,1)}, u32[]{:S(2)}) copy-start(pred[8,256]{1,0:T(8,128)(4,1)} %get-tuple-element.18) | copy-start | bytes 6148
  114.9 6.5 %copy-start.14 = (pred[8,256]{1,0:T(8,128)(4,1)S(1)}, pred[8,256]{1,0:T(8,128)(4,1)}, u32[]{:S(2)}) copy-start(pred[8,256]{1,0:T(8,128)(4,1)} %get-tuple-element.19) | copy-start | bytes 6148
  115.9 17.8 %all-to-all-start = ((bf16[8,96,256]{2,1,0:T(8,128)(2,1)}), bf16[8,96,256]{2,1,0:T(8,128)(2,1)S(1)}, u32[]{:S(2)}, u32[]{:S(2)}) async-start(bf16[8,96,256]{2,1,0:T(8,128)(2,1)} %copy.36), calls=%async_computation | async-start | bytes 786432 | tf_op jit(solution)/shard_map/all_to_all | solution.py:43
  121.4 5.4 %copy-start.15 = (s32[1,256]{1,0:T(1,128)S(1)}, s32[1,256]{1,0:T(1,128)}, u32[]{:S(2)}) copy-start(s32[1,256]{1,0:T(1,128)} %param.18) | copy-start | bytes 3076
  126.7 1.3 copy-start.2
  133.7 15.5 %all-to-all-start.2 = ((bf16[8,96,256]{2,1,0:T(8,128)(2,1)}), bf16[8,96,256]{2,1,0:T(8,128)(2,1)S(1)}, u32[]{:S(2)}, u32[]{:S(2)}) async-start(bf16[8,96,256]{2,1,0:T(8,128)(2,1)} %copy.42), calls=%async_computation.2 | async-start | bytes 786432 | tf_op jit(solution)/shard_map/all_to_all | solution.py:50
  150.4 1.7 copy-start.3
  150.4 1.8 copy-start.7
  150.4 3.9 %collective-permute-start = (bf16[768,288]{0,1:T(8,128)(2,1)}, bf16[768,288]{0,1:T(8,128)(2,1)S(1)}, u32[]{:S(2)}, u32[]{:S(2)}) collective-permute-start(bf16[768,288]{0,1:T(8,128)(2,1)} %copy.45), channel_id=1, source_target_pairs={{0,1},{1,0},{2,3},{3,2},{4,5},{5,4},{6,7},{7,6},{8,9},{9,8},{10,11... | collective-permute-start | bytes 1327112 | tf_op jit(solution)/shard_map/ppermute | solution.py:85
  150.4 1.8 copy-start.16
  152.9 0.7 copy-start.4
  153.1 1.7 collective-permute-start.1
  156.2 51.3 %all-to-all-start.3 = ((bf16[8,96,512]{2,1,0:T(8,128)(2,1)}), bf16[8,96,512]{2,1,0:T(8,128)(2,1)S(1)}, u32[]{:S(2)}, u32[]{:S(2)}) async-start(bf16[8,96,512]{2,1,0:T(8,128)(2,1)} %bitcast.35), calls=%async_computation.3 | async-start | bytes 1572864 | tf_op jit(solution)/shard_map/all_to_all | solution.py:94
  160.6 2.0 collective-permute-start.2
Sparse Core Ops, SparseCore 0:
  44.5 10.7 all-gather.5

commit v2 on v1

v2 whole, which is shorter than its diff:
```python
import functools

import jax
import jax.numpy as jnp
from jax import lax
from jax.experimental import pallas as pl
from jax.experimental.pallas import tpu as pltpu
from jax.sharding import PartitionSpec as P

F32 = jnp.float32
BF16 = jnp.bfloat16
LANES = 128
VMEM = pl.BlockSpec(memory_space=pltpu.VMEM)
SMEM = pl.BlockSpec(memory_space=pltpu.SMEM)
OVER_FIRST = (((0,), (0,)), ((), ()))
OVER_LAST = (((1,), (1,)), ((), ()))


def up(n, m):
    return -(-n // m) * m


def call(body, name, outs, in_specs, scratch=(), micros=1):
    return pl.pallas_call(
        body,
        name=name,
        out_shape=outs,
        in_specs=in_specs,
        out_specs=jax.tree.map(lambda _: VMEM, outs),
        scratch_shapes=list(scratch),
        compiler_params=pltpu.CompilerParams(vmem_limit_bytes=48 << 20),
        cost_estimate=pl.CostEstimate(
            flops=0, bytes_accessed=int(micros * 3_000_000), transcendentals=0
        ),
    )


def mix_groups(pieces, seeds, towards):
    groups = LANES // seeds
    shape = next(p for p in pieces if p is not None).shape
    lane_group = lax.broadcasted_iota(jnp.int32, shape, 1) // seeds
    total = jnp.zeros(shape, F32)
    for k, piece in enumerate(pieces):
        if piece is None:
            continue
        turn = (k - towards) % groups
        moved = pltpu.roll(piece, turn * seeds, axis=1) if turn else piece
        total = jnp.where(lane_group == k, moved, total)
    return total


def first_messages(sizes, half_ref, hop_ref, seed_ref, ws_ref, wn_ref, cot_ref, out_ref, hop32, seed32):
    owners, seeds, fan, f, fp, seed_rows, width, classes = sizes
    groups = LANES // seeds
    hops = fan * seeds
    parts = width // hops
    w_at = fp + seed_rows
    cot_at = w_at + parts * fp
    zeros = jnp.zeros((out_ref.shape[1], hops), BF16)

    if fp != f or classes != hops:
        for d in range(owners):
            out_ref[d] = zeros

    def put_weights(ref):
        for p in range(parts):
            block = ref[:, p * hops : (p + 1) * hops]
            for d in range(owners):
                out_ref[d, w_at + p * fp : w_at + p * fp + f, :] = block

    @pl.when(half_ref[0] == 0)
    def _():
        put_weights(ws_ref)

    @pl.when(half_ref[0] != 0)
    def _():
        put_weights(wn_ref)

    for d in range(owners):
        out_ref[d, cot_at : cot_at + seeds, :classes] = cot_ref[0]

    for tile in range(owners // groups):
        at = slice(tile * LANES, (tile + 1) * LANES)
        hop32[tile] = hop_ref[0, :, :, at].astype(F32).reshape(f * fan, LANES)
        for block in range(fan // groups):
            taken = [
                hop32[tile, pl.ds(block * groups + k, f, stride=fan), :] for k in range(groups)
            ]
            for e in range(groups):
                out_ref[tile * groups + e, :f, block * LANES : (block + 1) * LANES] = mix_groups(
                    taken, seeds, e
                ).astype(BF16)
    if fp != f:
        seed32[...] = jnp.zeros_like(seed32)
    seed32[:f, :] = seed_ref[0].astype(F32)
    bands = fp // 16
    for tile in range(owners // groups):
        at = slice(tile * LANES, (tile + 1) * LANES)
        for block in range(-(-bands // groups)):
            taken = [
                seed32[(block * groups + k) * 16 : (block * groups + k + 1) * 16, at]
                if block * groups + k < bands
                else None
                for k in range(groups)
            ]
            row, lane = divmod(block * LANES, hops)
            for e in range(groups):
                out_ref[
                    tile * groups + e, fp + row * 16 : fp + row * 16 + 16, lane : lane + LANES
                ] = mix_groups(taken, seeds, e).astype(BF16)


def gather_mean(sizes, idx_ref, deg_ref, table_ref, out_ref, rows, picked, live_idx, idx, sem):
    owners, seeds, fan, f, fp = sizes
    nodes = table_ref.shape[2]
    slots = idx_ref.shape[1]
    for u in range(slots):
        live_idx[u] = jnp.where(deg_ref[0] > u, idx_ref[0, u], nodes)
    load = pltpu.make_async_copy(live_idx, idx, sem)
    load.start()
    step = 512 if nodes % 512 == 0 else LANES
    lanes = rows.shape[1]
    tail = (lax.broadcasted_iota(jnp.int32, (lanes - f, step), 0) == 0).astype(F32)

    def flip(i, _):
        at = pl.multiple_of(i * step, step)
        block = jnp.concatenate([table_ref[0, :, pl.ds(at, step)].astype(F32), tail], axis=0)
        rows[pl.ds(at, step), :] = block.T
        return 0

    lax.fori_loop(0, nodes // step, flip, 0)
    rows[nodes:, :] = jnp.zeros((8, lanes), F32)
    load.wait()

    def owner_step(d, _):
        def slot_step(t, _):
            src = d * seeds
            for k in range(seeds):
                total = rows[pl.ds(idx[0, t, src + k], 1), :]
                for u in range(1, slots):
                    total = total + rows[pl.ds(idx[u, t, src + k], 1), :]
                picked[pl.ds(t * seeds + k, 1), :] = total
            return 0

        lax.fori_loop(0, fan, slot_step, 0)
        flat = picked[...].T
        mean = flat[:f] / flat[f : f + 1]
        if fp != f:
            mean = jnp.concatenate([mean, jnp.zeros((fp - f, mean.shape[1]), F32)], axis=0)
        out_ref[d] = mean.astype(BF16)
        return 0

    lax.fori_loop(0, owners, owner_step, 0)


def my_degrees(where_ref, seed_degree_ref, seeds):
    half = seed_degree_ref.shape[1]
    wide = jnp.broadcast_to(seed_degree_ref[...], (8, half))
    shift = lax.rem(half - where_ref[1] * seeds, half)
    mine = pltpu.roll(wide, shift, axis=1)[:, :LANES]
    lane = lax.broadcasted_iota(jnp.int32, (8, LANES), 1)
    return jnp.where(lane < seeds, mine, 1)


def stack_features(sizes, where_ref, seed_degree_ref, first_ref, agg_ref, own_ref, mean_ref, send_ref):
    owners, seeds, fan, fp, seed_rows = sizes
    groups = LANES // seeds
    hops = fan * seeds
    depth = owners * fp
    own = first_ref[:, :fp, :].reshape(depth, hops)
    own_ref[:, :hops] = own
    mean_ref[:, :hops] = agg_ref[...].reshape(depth, hops)
    lane = lax.broadcasted_iota(jnp.int32, (16, LANES), 1)
    for c in range(owners):
        for band in range(fp // 16):
            row, place = divmod(band * seeds, hops)
            tile = place // LANES
            block = first_ref[
                c, fp + row * 16 : fp + row * 16 + 16, tile * LANES : (tile + 1) * LANES
            ].astype(F32)
            turn = (-(band % groups)) % groups
            if turn:
                block = pltpu.roll(block, turn * seeds, axis=1)
            at = c * fp + band * 16
            own_ref[at : at + 16, hops:] = jnp.where(lane < seeds, block, 0.0).astype(BF16)
    degree = my_degrees(where_ref, seed_degree_ref, seeds)[:1]
    node = lax.broadcasted_iota(jnp.int32, (hops, LANES), 0)
    seed = lax.broadcasted_iota(jnp.int32, (hops, LANES), 1)
    live = (node % seeds == seed) & (node // seeds < degree)
    total = jnp.dot(own, live.astype(F32).astype(BF16), preferred_element_type=F32)
    mean_ref[:, hops:] = (total / degree.astype(F32)).astype(BF16)

    @pl.when(where_ref[0] == 0)
    def _():
        send_ref[...] = mean_ref[...]

    @pl.when(where_ref[0] != 0)
    def _():
        send_ref[...] = own_ref[...]


def forward(
    sizes,
    where_ref,
    seed_degree_ref,
    own_ref,
    mean_ref,
    w_mine_ref,
    w_other_ref,
    vs_ref,
    vn_ref,
    cot_ref,
    logits_ref,
    hidden_ref,
    dpre_ref,
    ws,
    wn,
):
    owners, seeds, fan, fp, w_at, width = sizes
    hops = fan * seeds
    depth = owners * fp
    parts = width // hops

    def lay(w_mine, w_other):
        for p in range(parts):
            at = slice(p * hops, (p + 1) * hops)
            rows = slice(w_at + p * fp, w_at + (p + 1) * fp)
            w_mine[:, at] = w_mine_ref[:, rows, :].reshape(depth, hops)
            w_other[:, at] = w_other_ref[:, p * fp : (p + 1) * fp, :].reshape(depth, hops)

    @pl.when(where_ref[0] == 0)
    def _():
        lay(ws, wn)

    @pl.when(where_ref[0] != 0)
    def _():
        lay(wn, ws)

    pre = lax.dot_general(own_ref[...], ws[...], OVER_FIRST, preferred_element_type=F32)
    pre = pre + lax.dot_general(mean_ref[...], wn[...], OVER_FIRST, preferred_element_type=F32)
    pre = pre[: hops + seeds]
    sigma = jax.nn.sigmoid(pre)
    hidden = (pre * sigma).astype(BF16)
    slope = sigma * (1.0 + pre * (1.0 - sigma))
    degree = my_degrees(where_ref, seed_degree_ref, seeds).astype(F32)
    degree = jnp.broadcast_to(degree[:1], (LANES, LANES)).T[:seeds]
    degree = jnp.concatenate([degree] * (width // LANES), axis=1)
    total = jnp.zeros((seeds, width), F32)
    for t in range(fan):
        row = hidden[t * seeds : (t + 1) * seeds].astype(F32)
        total = total + jnp.where(degree > t, row, 0.0)
    hidden_mean = (total / degree).astype(BF16)
    seed_hidden = hidden[hops:]
    hidden_ref[0] = seed_hidden
    hidden_ref[1] = hidden_mean
    logits = jnp.dot(seed_hidden, vs_ref[...], preferred_element_type=F32)
    logits = logits + jnp.dot(hidden_mean, vn_ref[...], preferred_element_type=F32)
    logits_ref[0] = logits.astype(BF16)
    cot = cot_ref[0]
    back_seed = lax.dot_general(cot, vs_ref[...], OVER_LAST, preferred_element_type=F32)
    back_mean = lax.dot_general(cot, vn_ref[...], OVER_LAST, preferred_element_type=F32)
    back_mean = back_mean / degree
    for t in range(fan):
        at = slice(t * seeds, (t + 1) * seeds)
        dpre_ref[at, :] = (jnp.where(degree > t, back_mean, 0.0) * slope[at]).astype(BF16)
    dpre_ref[hops : hops + seeds, :] = (back_seed * slope[hops:]).astype(BF16)
    dpre_ref[hops + seeds :, :] = jnp.zeros((LANES - seeds, width), BF16)


def second_messages(
    sizes, where_ref, own_ref, mean_ref, x_ref, dpre_ref, dpre_other_ref, hid_ref, hid_other_ref, out_ref
):
    owners, seeds, fp, width = sizes

    def products(mine_ref):
        total = jnp.dot(mine_ref[...], dpre_ref[...], preferred_element_type=F32)
        total = total + jnp.dot(x_ref[...], dpre_other_ref[...], preferred_element_type=F32)
        out_ref[:, :fp, :] = total.astype(BF16).reshape(owners, fp, width)

    @pl.when(where_ref[0] == 0)
    def _():
        products(own_ref)
        for d in range(owners):
            out_ref[d, fp : fp + seeds, :] = hid_ref[0]
            out_ref[d, fp + seeds :, :] = hid_other_ref[0]

    @pl.when(where_ref[0] != 0)
    def _():
        products(mean_ref)
        for d in range(owners):
            out_ref[d, fp : fp + seeds, :] = hid_ref[1]
            out_ref[d, fp + seeds :, :] = hid_other_ref[1]


def total_gradients(sizes, second_ref, cot_ref, cot_other_ref, grad_w_ref, grad_v_ref):
    owners, seeds, f, fp, width, cot_at = sizes
    total = second_ref[0, :fp, :].astype(F32)
    for c in range(1, owners):
        total = total + second_ref[c, :fp, :].astype(F32)
    grad_w_ref[...] = total[:f]
    hops = cot_ref.shape[2]
    flat = owners * seeds
    hid = second_ref[:, fp : fp + seeds, :].reshape(flat, width)
    hid_other = second_ref[:, fp + seeds : fp + 2 * seeds, :].reshape(flat, width)
    cot = cot_ref[:, cot_at : cot_at + seeds, :].reshape(flat, hops)
    cot_other = cot_other_ref[...].reshape(flat, hops)
    grad_v = lax.dot_general(hid, cot, OVER_FIRST, preferred_element_type=F32)
    grad_v = grad_v + lax.dot_general(hid_other, cot_other, OVER_FIRST, preferred_element_type=F32)
    grad_v_ref[...] = grad_v[:, : grad_v_ref.shape[1]]


def place_gradients(where_ref, w_mine, w_other, v_mine, v_other, ws_ref, wn_ref, vs_ref, vn_ref):
    @pl.when(where_ref[0] == 0)
    def _():
        ws_ref[...] = w_mine[...]
        wn_ref[...] = w_other[...]
        vs_ref[...] = v_mine[...]
        vn_ref[...] = v_other[...]

    @pl.when(where_ref[0] != 0)
    def _():
        ws_ref[...] = w_other[...]
        wn_ref[...] = w_mine[...]
        vs_ref[...] = v_other[...]
        vn_ref[...] = v_mine[...]


def swap(x):
    return lax.ppermute(x, "rep", [(0, 1), (1, 0)])


def spread(x):
    return lax.all_to_all(x, "feat", 0, 0, tiled=True)


def on_device(
    seed_feat,
    hop_feat,
    frontier,
    nbr_index,
    hop_degree,
    seed_degree,
    w_self,
    w_neigh,
    v_self,
    v_neigh,
    cotangent,
):
    owners = lax.axis_size("feat")
    where = jnp.stack([lax.axis_index("rep"), lax.axis_index("feat")]).astype(jnp.int32)
    seeds, classes = cotangent.shape[1:]
    f, width = w_self.shape
    fan = hop_feat.shape[2]
    nodes = frontier.shape[2]
    hops = fan * seeds
    fp = up(f, 16)
    seed_rows = 16 * -(-(fp // 16) * seeds // hops)
    w_rows = width // hops * fp
    w_at = fp + seed_rows
    cot_at = w_at + w_rows
    depth = owners * fp
    struct = jax.ShapeDtypeStruct

    first = call(
        functools.partial(
            first_messages, (owners, seeds, fan, f, fp, seed_rows, width, classes)
        ),
        "first_messages",
        struct((owners, cot_at + seeds, hops), BF16),
        [SMEM] + [VMEM] * 5,
        [
            pltpu.VMEM((owners * seeds // LANES, f * fan, LANES), F32),
            pltpu.VMEM((fp, owners * seeds), F32),
        ],
        micros=2,
    )(where, hop_feat, seed_feat, w_self, w_neigh, cotangent)
    first = spread(first)

    lanes = up(f + 1, LANES)
    agg = call(
        functools.partial(gather_mean, (owners, seeds, fan, f, fp)),
        "gather_mean",
        struct((owners, fp, hops), BF16),
        [VMEM] * 3,
        [
            pltpu.VMEM((nodes + 8, lanes), F32),
            pltpu.VMEM((hops, lanes), F32),
            pltpu.VMEM(nbr_index.shape[1:], jnp.int32),
            pltpu.SMEM(nbr_index.shape[1:], jnp.int32),
            pltpu.SemaphoreType.DMA,
        ],
        micros=14,
    )(nbr_index, hop_degree, frontier)
    agg = spread(agg)

    w_other = swap(first[:, w_at:cot_at])
    cot_other = swap(first[:, cot_at:])
    stacked = struct((depth, hops + LANES), BF16)
    own, mean, send = call(
        functools.partial(stack_features, (owners, seeds, fan, fp, seed_rows)),
        "stack_features",
        (stacked, stacked, stacked),
        [SMEM] + [VMEM] * 3,
    )(where, seed_degree, first, agg)
    x_other = swap(send)
    logits, hidden, dpre = call(
        functools.partial(forward, (owners, seeds, fan, fp, w_at, width)),
        "forward",
        (
            struct((1, seeds, classes), BF16),
            struct((2, seeds, width), BF16),
            struct((hops + LANES, width), BF16),
        ),
        [SMEM] + [VMEM] * 8,
        [pltpu.VMEM((depth, width), BF16), pltpu.VMEM((depth, width), BF16)],
        micros=5,
    )(where, seed_degree, own, mean, first, w_other, v_self, v_neigh, cotangent)
    second = call(
        functools.partial(second_messages, (owners, seeds, fp, width)),
        "second_messages",
        struct((owners, fp + 2 * seeds, width), BF16),
        [SMEM] + [VMEM] * 7,
        micros=3,
    )(where, own, mean, x_other, dpre, swap(dpre), hidden, swap(hidden))
    second = spread(second)
    grad_w, grad_v = call(
        functools.partial(total_gradients, (owners, seeds, f, fp, width, cot_at)),
        "total_gradients",
        (struct((f, width), F32), struct((width, classes), F32)),
        [VMEM] * 3,
    )(second, first, cot_other)
    grads = call(
        place_gradients,
        "place_gradients",
        (struct((f, width), F32),) * 2 + (struct((width, classes), F32),) * 2,
        [SMEM] + [VMEM] * 4,
    )(where, grad_w, swap(grad_w), grad_v, swap(grad_v))
    return (logits, *grads)


def solution(mesh):
    placed = (
        P(("groups", "rep"), "feat", None),
        P(("groups", "rep"), "feat", None, None),
        P(("groups", "rep"), "feat", None),
        P(("groups", "rep"), None, None, None),
        P(("groups", "rep"), None, None),
        P(("groups", "rep"), None),
        P("feat", None),
        P("feat", None),
        P(),
        P(),
        P(("groups", "rep"), "feat", None),
    )
    return jax.shard_map(
        on_device,
        mesh=mesh,
        in_specs=placed,
        out_specs=(
            P(("groups", "rep"), "feat", None),
            P(("groups", "feat"), None),
            P(("groups", "feat"), None),
            P("groups", None),
            P("groups", None),
        ),
        check_vma=False,
    )
```

time: 219 us -> 115 us (0.53)
  blocking collectives: 112 us -> 0 us
  waiting for transfers between devices: 14.9 us -> 63.8 us
  local copies, waits for them, and re-layouts: 37.4 us -> 8.41 us
  Pallas kernels: 0 us -> 25.5 us
  between operations: 14.5 us -> 0.77 us
  other arithmetic: 11.2 us -> 0.08 us
  matrix products: 8.21 us -> 0 us
  starting transfers between devices: 19 us -> 16.2 us
    all_gather x5 -> x0, blocking collectives: 112 us -> none  [the longest x1 40.5 us: on_device(): hid_all = lax.all_gather(hid, 'feat', axis=0, tiled=False)]
    all_to_all x4 -> x3, waiting for transfers between devices: 14.4 us -> 59.6 us  [spread(): return lax.all_to_all(x, 'feat', 0, 0, tiled=True)]
    gather x4 -> x0, local copies, waits for them, and re-layouts: 28.3 us -> none  [neighbour_mean(): picked = jnp.take(table, nbr_index[slot_index], axis=1).astype(F32)]
    pallas_call x0 -> x7, Pallas kernels: none -> 25.5 us  [the longest x1 14.7 us: on_device(): call(functools.partial(gather_mean, (owners, seeds, fan, f, fp)), 'gather...]
    dot_general x9 -> x0, matrix products: 8.21 us -> none  [the longest x1 1.7 us: on_device(): lax.dot_general(own, w_full[0], over_first, preferred_element_type=F32)]
    convert_element_type x5 -> x0, other arithmetic: 5.48 us -> none  [the longest x1 5.31 us: neighbour_mean(): return (total / hop_degree.astype(F32)[None]).astype(BF16)]
    unnamed x41 -> x30, local copies, waits for them, and re-layouts: 3.23 us -> 7.46 us
    ppermute x4 -> x7, waiting for transfers between devices: 0.43 us -> 4.17 us  [swap(): return lax.ppermute(x, 'rep', [(0, 1), (1, 0)])]
  transfers between devices with their start and end apart: 9 -> 10, of which waited for: 3 -> 6; matrix products, arithmetic and copies ran while one was open for 25% -> 1% of each run, Pallas kernels for 0% -> 17%
where the time goes in v2:
time: 115 us
  waiting for transfers between devices  63.8 us (55%)
  Pallas kernels  25.5 us (22%)
  starting transfers between devices  16.2 us (14%)
  local copies, waits for them, and re-layouts  8.41 us (7%)
    all_to_all x3, waiting for transfers between devices, spread(): return lax.all_to_all(x, 'feat', 0, 0, tiled=True)  59.6 us
    all_to_all x3, starting transfers between devices, spread(): return lax.all_to_all(x, 'feat', 0, 0, tiled=True)  14.7 us
    pallas_call x1, Pallas kernels, on_device(): call(functools.partial(gather_mean, (owners, seeds, fan, f, fp)), 'gather...  14.7 us
    unnamed x30, local copies, waits for them, and re-layouts  7.46 us
    ppermute x7, waiting for transfers between devices, swap(): return lax.ppermute(x, 'rep', [(0, 1), (1, 0)])  4.17 us
    pallas_call x1, Pallas kernels, on_device(): call(functools.partial(forward, (owners, seeds, fan, fp, w_at, width)), '...  3 us
  transfers between devices with their start and end apart: 10, of which 6 were waited for; matrix products, arithmetic and copies ran while one was open for 1% of the time, Pallas kernels for 17%

profile of v2, /device:TPU:0, one launch (start us, length us, event | category | flops | bytes accessed | tf_op | source)
XLA Modules:
  0.0 114.7 jit_solution(17787869546642822561)
XLA Ops:
  0.6 0.1 pad_add_fusion.half_ref.where_ref
  0.7 0.0 copy-start.2
  0.7 1.0 copy-done.2
  1.7 0.0 copy-start.3
  1.7 0.9 copy-done.3
  2.6 0.0 copy-start.4
  2.6 0.9 copy-done.4
  3.5 0.0 copy-start.5
  3.5 0.7 copy-done.5
  4.2 0.0 copy-start.7
  4.2 0.8 copy-done.7
  5.0 2.3 %first_messages.1 = bf16[8,336,256]{2,1,0:T(8,128)(2,1)} custom-call(s32[2]{0:T(128)S(1)} %pad_add_fusion.half_ref.where_ref, bf16[1,96,8,256]{3,2,1,0:T(8,128)(2,1)S(1)} %copy-done.2, bf16[1,96,256]{2,1,0:T(8,128)(2,1)S(1)} %copy-done.7, bf16[96,512]{1,0:T(8,128)(2,1)S(1)} %copy-done.3, bf16[96,512]{1,0:T(8,128)(2,1)S(1)} %copy-done.4, ...), custom_call_target="tpu_custom_call" | custom-call | bytes 6000000 | tf_op jit(solution)/shard_map/first_messages/pallas_call | solution.py:364
  7.3 0.0 copy-start.1
  7.3 0.0 copy-start.8
  7.3 0.0 copy-start.9
  7.3 7.4 %all-to-all-start = ((bf16[8,336,256]{2,1,0:T(8,128)(2,1)}), bf16[8,336,256]{2,1,0:T(8,128)(2,1)S(1)}, u32[]{:S(2)}, u32[]{:S(2)}) async-start(bf16[8,336,256]{2,1,0:T(8,128)(2,1)} %first_messages.1), calls=%async_computation | async-start | bytes 2752512 | tf_op jit(solution)/shard_map/all_to_all | solution.py:333
  14.7 0.0 copy-done.1
  14.7 0.0 copy-done.8
  14.7 0.0 copy-done.9
  14.7 14.7 %gather_mean.1 = bf16[8,96,256]{2,1,0:T(8,128)(2,1)} custom-call(s32[1,4,8,256]{3,2,1,0:T(8,128)S(1)} %copy-done.8, s32[1,8,256]{2,1,0:T(8,128)S(1)} %copy-done.9, bf16[1,96,6144]{2,1,0:T(8,128)(2,1)S(1)} %copy-done.1), custom_call_target="tpu_custom_call" | custom-call | bytes 42000000 | tf_op jit(solution)/shard_map/gather_mean/pallas_call | solution.py:380
  29.4 0.0 copy-start.10
  29.4 18.1 %all-to-all-done.first_ref.w_mine_ref.cot_ref = bf16[8,336,256]{2,1,0:T(8,128)(2,1)S(1)} async-done(((bf16[8,336,256]{2,1,0:T(8,128)(2,1)}), bf16[8,336,256]{2,1,0:T(8,128)(2,1)S(1)}, u32[]{:S(2)}, u32[]{:S(2)}) %all-to-all-start) | async-done | bytes 1376288 | tf_op jit(solution)/shard_map/all_to_all | solution.py:333
  47.5 3.6 %all-to-all-start.1 = ((bf16[8,96,256]{2,1,0:T(8,128)(2,1)}), bf16[8,96,256]{2,1,0:T(8,128)(2,1)S(1)}, u32[]{:S(2)}, u32[]{:S(2)}) async-start(bf16[8,96,256]{2,1,0:T(8,128)(2,1)} %gather_mean.1), calls=%async_computation.1 | async-start | bytes 786432 | tf_op jit(solution)/shard_map/all_to_all | solution.py:333
  51.1 0.0 copy-start.11
  51.1 0.9 slice.8
  52.1 0.0 copy-start.12
  52.1 0.0 copy-start.6
  52.1 0.0 collective-permute-start
  52.1 10.9 %all-to-all-done.1.agg_ref = bf16[8,96,256]{2,1,0:T(8,128)(2,1)S(1)} async-done(((bf16[8,96,256]{2,1,0:T(8,128)(2,1)}), bf16[8,96,256]{2,1,0:T(8,128)(2,1)S(1)}, u32[]{:S(2)}, u32[]{:S(2)}) %all-to-all-start.1) | async-done | bytes 393248 | tf_op jit(solution)/shard_map/all_to_all | solution.py:333
  63.0 0.0 copy-done.10
  63.0 1.8 %stack_features.1 = (bf16[768,384]{1,0:T(8,128)(2,1)S(1)}, bf16[768,384]{1,0:T(8,128)(2,1)S(1)}, bf16[768,384]{1,0:T(8,128)(2,1)}) custom-call(s32[2]{0:T(128)S(1)} %pad_add_fusion.half_ref.where_ref, s32[1,256]{1,0:T(1,128)S(1)} %copy-done.10, bf16[8,336,256]{2,1,0:T(8,128)(2,1)S(1)} %all-to-all-done.first_ref.w_mine_ref.cot_ref, ...), custom_call_target="tpu_custom_call" | custom-call | bytes 3000000 | tf_op jit(solution)/shard_map/stack_features/pallas_call | solution.py:399
  64.7 0.0 collective-permute-start.1
  64.7 0.0 copy-done.11
  64.8 0.1 copy.16.vs_ref
  64.9 0.0 copy-done.12
  64.9 0.1 copy.17.vn_ref
  65.0 0.0 collective-permute-done.w_other_ref
  65.1 0.0 copy-done.6
  65.1 3.0 %forward.1 = (bf16[1,32,153]{2,1,0:T(8,128)(2,1)}, bf16[2,32,512]{2,1,0:T(8,128)(2,1)S(1)}, bf16[384,512]{1,0:T(8,128)(2,1)S(1)}) custom-call(s32[2]{0:T(128)S(1)} %pad_add_fusion.half_ref.where_ref, s32[1,256]{1,0:T(1,128)S(1)} %copy-done.10, bf16[768,384]{1,0:T(8,128)(2,1)S(1)} %get-tuple-element.17.own_ref, ...), custom_call_target="tpu_custom_call" | custom-call | bytes 15000000 | tf_op jit(solution)/shard_map/forward/pallas_call | solution.py:406
  68.1 0.5 collective-permute-start.2
  68.6 0.0 collective-permute-start.3
  68.6 0.0 collective-permute-done.1.x_ref
  68.6 1.4 %collective-permute-done.3.hid_other_ref = bf16[2,32,512]{2,1,0:T(8,128)(2,1)S(1)} collective-permute-done((bf16[2,32,512]{2,1,0:T(8,128)(2,1)S(1)}, bf16[2,32,512]{2,1,0:T(8,128)(2,1)S(1)}, u32[]{:S(2)}, u32[]{:S(2)}) %collective-permute-start.3) | collective-permute-done | bytes 65568 | tf_op jit(solution)/shard_map/ppermute | solution.py:329
  70.0 0.0 collective-permute-done.2.dpre_other_ref
  70.0 2.0 %second_messages.1 = bf16[8,160,512]{2,1,0:T(8,128)(2,1)S(1)} custom-call(s32[2]{0:T(128)S(1)} %pad_add_fusion.half_ref.where_ref, bf16[768,384]{1,0:T(8,128)(2,1)S(1)} %get-tuple-element.17.own_ref, bf16[768,384]{1,0:T(8,128)(2,1)S(1)} %get-tuple-element.18.mean_ref, bf16[768,384]{1,0:T(8,128)(2,1)} %collective-permute-done.1.x_ref, ...), custom_call_target="tpu_custom_call" | custom-call | bytes 9000000 | tf_op jit(solution)/shard_map/second_messages/pallas_call | solution.py:418
  72.1 0.0 copy-start
  72.1 1.1 copy-done
  73.2 3.7 %all-to-all-start.2 = ((bf16[8,160,512]{2,1,0:T(8,128)(2,1)}), bf16[8,160,512]{2,1,0:T(8,128)(2,1)S(1)}, u32[]{:S(2)}, u32[]{:S(2)}) async-start(bf16[8,160,512]{2,1,0:T(8,128)(2,1)} %copy-done), calls=%async_computation.2 | async-start | bytes 2621440 | tf_op jit(solution)/shard_map/all_to_all | solution.py:333
  76.8 0.4 collective-permute-start.4
  77.2 1.0 collective-permute-done.4.cot_other_ref
  78.2 30.6 %all-to-all-done.2.second_ref = bf16[8,160,512]{2,1,0:T(8,128)(2,1)S(1)} async-done(((bf16[8,160,512]{2,1,0:T(8,128)(2,1)}), bf16[8,160,512]{2,1,0:T(8,128)(2,1)S(1)}, u32[]{:S(2)}, u32[]{:S(2)}) %all-to-all-start.2) | async-done | bytes 1310752 | tf_op jit(solution)/shard_map/all_to_all | solution.py:333
  108.9 0.4 total_gradients.1
  109.3 0.1 collective-permute-start.6
  109.3 0.5 collective-permute-start.5
  109.8 1.7 %collective-permute-done.5.w_other = f32[96,512]{1,0:T(8,128)S(1)} collective-permute-done((f32[96,512]{1,0:T(8,128)S(1)}, f32[96,512]{1,0:T(8,128)S(1)}, u32[]{:S(2)}, u32[]{:S(2)}) %collective-permute-start.5) | collective-permute-done | bytes 196640 | tf_op jit(solution)/shard_map/ppermute | solution.py:329
  111.5 0.0 collective-permute-done.6.v_other
  111.5 1.4 %place_gradients.1 = (f32[96,512]{1,0:T(8,128)}, f32[96,512]{1,0:T(8,128)}, f32[512,153]{1,0:T(8,128)S(1)}, f32[512,153]{1,0:T(8,128)S(1)}) custom-call(s32[2]{0:T(128)S(1)} %pad_add_fusion.half_ref.where_ref, f32[96,512]{1,0:T(8,128)S(1)} %get-tuple-element.23.w_mine, f32[96,512]{1,0:T(8,128)S(1)} %collective-permute-done.5.w_other, ...), custom_call_target="tpu_custom_call" | custom-call | bytes 3000000 | tf_op jit(solution)/shard_map/place_gradients/pallas_call | solution.py:432
  112.9 0.9 copy.18
  113.8 0.9 copy.19
  (1 shorter events, 0.0 us)
Async XLA Ops:
  0.7 1.0 copy-start.2
  1.7 0.9 copy-start.3
  2.6 0.9 copy-start.4
  3.5 0.7 copy-start.5
  4.2 0.8 copy-start.7
  7.3 7.4 %copy-start.1 = (bf16[1,96,6144]{2,1,0:T(8,128)(2,1)S(1)}, bf16[1,96,6144]{2,1,0:T(8,128)(2,1)}, u32[]{:S(2)}) copy-start(bf16[1,96,6144]{2,1,0:T(8,128)(2,1)} %table_ref.1) | copy-start | bytes 3538948
  7.3 7.4 %copy-start.8 = (s32[1,4,8,256]{3,2,1,0:T(8,128)S(1)}, s32[1,4,8,256]{3,2,1,0:T(8,128)}, u32[]{:S(2)}) copy-start(s32[1,4,8,256]{3,2,1,0:T(8,128)} %idx_ref.1) | copy-start | bytes 98308
  7.3 7.4 %copy-start.9 = (s32[1,8,256]{2,1,0:T(8,128)S(1)}, s32[1,8,256]{2,1,0:T(8,128)}, u32[]{:S(2)}) copy-start(s32[1,8,256]{2,1,0:T(8,128)} %deg_ref.1) | copy-start | bytes 24580
  7.3 40.2 %all-to-all-start = ((bf16[8,336,256]{2,1,0:T(8,128)(2,1)}), bf16[8,336,256]{2,1,0:T(8,128)(2,1)S(1)}, u32[]{:S(2)}, u32[]{:S(2)}) async-start(bf16[8,336,256]{2,1,0:T(8,128)(2,1)} %first_messages.1), calls=%async_computation | async-start | bytes 2752512 | tf_op jit(solution)/shard_map/all_to_all | solution.py:333
  29.4 33.6 %copy-start.10 = (s32[1,256]{1,0:T(1,128)S(1)}, s32[1,256]{1,0:T(1,128)}, u32[]{:S(2)}) copy-start(s32[1,256]{1,0:T(1,128)} %seed_degree_ref.3) | copy-start | bytes 3076
  47.5 15.5 %all-to-all-start.1 = ((bf16[8,96,256]{2,1,0:T(8,128)(2,1)}), bf16[8,96,256]{2,1,0:T(8,128)(2,1)S(1)}, u32[]{:S(2)}, u32[]{:S(2)}) async-start(bf16[8,96,256]{2,1,0:T(8,128)(2,1)} %gather_mean.1), calls=%async_computation.1 | async-start | bytes 786432 | tf_op jit(solution)/shard_map/all_to_all | solution.py:333
  51.1 13.6 %copy-start.11 = (bf16[512,153]{0,1:T(8,128)(2,1)S(1)}, bf16[512,153]{0,1:T(8,128)(2,1)}, u32[]{:S(2)}) copy-start(bf16[512,153]{0,1:T(8,128)(2,1)} %param.19) | copy-start | bytes 470020
  52.1 12.8 %copy-start.12 = (bf16[512,153]{0,1:T(8,128)(2,1)S(1)}, bf16[512,153]{0,1:T(8,128)(2,1)}, u32[]{:S(2)}) copy-start(bf16[512,153]{0,1:T(8,128)(2,1)} %param.20) | copy-start | bytes 470020
  52.1 13.0 %copy-start.6 = (bf16[1,32,153]{2,1,0:T(8,128)(2,1)S(1)}, bf16[1,32,153]{2,1,0:T(8,128)(2,1)}, u32[]{:S(2)}) copy-start(bf16[1,32,153]{2,1,0:T(8,128)(2,1)} %cot_ref.3) | copy-start | bytes 29380
  52.1 13.0 %collective-permute-start = (bf16[8,192,256]{2,1,0:T(8,128)(2,1)}, bf16[8,192,256]{2,1,0:T(8,128)(2,1)}, u32[]{:S(2)}, u32[]{:S(2)}) collective-permute-start(bf16[8,192,256]{2,1,0:T(8,128)(2,1)} %slice.8), channel_id=1, source_target_pairs={{0,1},{1,0},{2,3},{3,2},{4,5},{5,4},{6,7},{7,6},{8,9},{9,8},{10,11... | collective-permute-start | bytes 2359304 | tf_op jit(solution)/shard_map/ppermute | solution.py:329
  64.7 3.8 %collective-permute-start.1 = (bf16[768,384]{1,0:T(8,128)(2,1)}, bf16[768,384]{1,0:T(8,128)(2,1)}, u32[]{:S(2)}, u32[]{:S(2)}) collective-permute-start(bf16[768,384]{1,0:T(8,128)(2,1)} %get-tuple-element.20), channel_id=1, source_target_pairs={{0,1},{1,0},{2,3},{3,2},{4,5},{5,4},{6,7},{7,6},{8,9},{9,8},{10,11... | collective-permute-start | bytes 1769480 | tf_op jit(solution)/shard_map/ppermute | solution.py:329
  68.1 2.0 %collective-permute-start.2 = (bf16[384,512]{1,0:T(8,128)(2,1)S(1)}, bf16[384,512]{1,0:T(8,128)(2,1)S(1)}, u32[]{:S(2)}, u32[]{:S(2)}) collective-permute-start(bf16[384,512]{1,0:T(8,128)(2,1)S(1)} %get-tuple-element.21.dpre_ref), channel_id=1, source_target_pairs={{0,1},{1,0},{2,3},{3,2},{4,5},{5,4},{6,7},{7,6},{8,9},{9,8},{10,11... | collective-permute-start | bytes 1179656 | tf_op jit(solution)/shard_map/ppermute | solution.py:329
  68.6 1.4 %collective-permute-start.3 = (bf16[2,32,512]{2,1,0:T(8,128)(2,1)S(1)}, bf16[2,32,512]{2,1,0:T(8,128)(2,1)S(1)}, u32[]{:S(2)}, u32[]{:S(2)}) collective-permute-start(bf16[2,32,512]{2,1,0:T(8,128)(2,1)S(1)} %get-tuple-element.22.hid_ref), channel_id=1, source_target_pairs={{0,1},{1,0},{2,3},{3,2},{4,5},{5,4},{6,7},{7,6},{8,9},{9,8},{10,11... | collective-permute-start | bytes 196616 | tf_op jit(solution)/shard_map/ppermute | solution.py:329
  72.1 1.1 copy-start
  73.2 35.7 %all-to-all-start.2 = ((bf16[8,160,512]{2,1,0:T(8,128)(2,1)}), bf16[8,160,512]{2,1,0:T(8,128)(2,1)S(1)}, u32[]{:S(2)}, u32[]{:S(2)}) async-start(bf16[8,160,512]{2,1,0:T(8,128)(2,1)} %copy-done), calls=%async_computation.2 | async-start | bytes 2621440 | tf_op jit(solution)/shard_map/all_to_all | solution.py:333
  76.8 1.4 %collective-permute-start.4 = (bf16[8,32,256]{2,1,0:T(8,128)(2,1)S(1)}, bf16[8,32,256]{2,1,0:T(8,128)(2,1)S(1)}, u32[]{:S(2)}, u32[]{:S(2)}) collective-permute-start(bf16[8,32,256]{2,1,0:T(8,128)(2,1)S(1)} %slice.9), channel_id=1, source_target_pairs={{0,1},{1,0},{2,3},{3,2},{4,5},{5,4},{6,7},{7,6},{8,9},{9,8},{10,11... | collective-permute-start | bytes 393224 | tf_op jit(solution)/shard_map/ppermute | solution.py:329
  109.3 2.3 %collective-permute-start.6 = (f32[512,153]{1,0:T(8,128)S(1)}, f32[512,153]{1,0:T(8,128)S(1)}, u32[]{:S(2)}, u32[]{:S(2)}) collective-permute-start(f32[512,153]{1,0:T(8,128)S(1)} %get-tuple-element.24.v_mine), channel_id=1, source_target_pairs={{0,1},{1,0},{2,3},{3,2},{4,5},{5,4},{6,7},{7,6},{8,9},{9,8},{10,11... | collective-permute-start | bytes 940040 | tf_op jit(solution)/shard_map/ppermute | solution.py:329
  109.3 2.2 %collective-permute-start.5 = (f32[96,512]{1,0:T(8,128)S(1)}, f32[96,512]{1,0:T(8,128)S(1)}, u32[]{:S(2)}, u32[]{:S(2)}) collective-permute-start(f32[96,512]{1,0:T(8,128)S(1)} %get-tuple-element.23.w_mine), channel_id=1, source_target_pairs={{0,1},{1,0},{2,3},{3,2},{4,5},{5,4},{6,7},{7,6},{8,9},{9,8},{10,11... | collective-permute-start | bytes 589832 | tf_op jit(solution)/shard_map/ppermute | solution.py:329

commit v3 on v2

v3 whole, which is shorter than its diff:
```python
import functools

import jax
import jax.numpy as jnp
from jax import lax
from jax.experimental import pallas as pl
from jax.experimental.pallas import tpu as pltpu
from jax.sharding import PartitionSpec as P

F32 = jnp.float32
BF16 = jnp.bfloat16
LANES = 128
MICROS = 1
VMEM = pl.BlockSpec(memory_space=pltpu.VMEM)
SMEM = pl.BlockSpec(memory_space=pltpu.SMEM)
HBM = pl.BlockSpec(memory_space=pltpu.HBM)
OVER_FIRST = (((0,), (0,)), ((), ()))
OVER_LAST = (((1,), (1,)), ((), ()))


def up(n, m):
    return -(-n // m) * m


def call(body, name, outs, in_specs, scratch=(), micros=1, vmem=40):
    return pl.pallas_call(
        body,
        name=name,
        out_shape=outs,
        in_specs=in_specs,
        out_specs=jax.tree.map(lambda _: VMEM, outs),
        scratch_shapes=list(scratch),
        compiler_params=pltpu.CompilerParams(vmem_limit_bytes=vmem << 20),
        cost_estimate=pl.CostEstimate(
            flops=0, bytes_accessed=int(micros * 3_000_000), transcendentals=0
        ),
    )


def mix_groups(pieces, seeds, towards):
    groups = LANES // seeds
    shape = next(p for p in pieces if p is not None).shape
    lane_group = lax.broadcasted_iota(jnp.int32, shape, 1) // seeds
    total = jnp.zeros(shape, F32)
    for k, piece in enumerate(pieces):
        if piece is None:
            continue
        turn = (k - towards) % groups
        moved = pltpu.roll(piece, turn * seeds, axis=1) if turn else piece
        total = jnp.where(lane_group == k, moved, total)
    return total


def weight_message(sizes, ws_ref, wn_ref, cot_ref, out_ref, cot, sems):
    seeds, f, fp, classes = sizes
    width = out_ref.shape[1]
    split = seeds // 16

    def fetch(ref):
        loads = (
            pltpu.make_async_copy(ref, out_ref.at[pl.ds(0, f), :], sems.at[0]),
            pltpu.make_async_copy(cot_ref, cot, sems.at[1]),
        )
        for load in loads:
            load.start()
        for load in loads:
            load.wait()

    @pl.when(lax.axis_index("rep") == 0)
    def _():
        fetch(ws_ref)

    @pl.when(lax.axis_index("rep") != 0)
    def _():
        fetch(wn_ref)

    if fp != f:
        out_ref[f:fp, :] = jnp.zeros((fp - f, width), BF16)
    out_ref[fp:, :] = jnp.zeros((16, width), BF16)
    for p in range(split):
        at = p * (width // split)
        out_ref[fp:, at : at + classes] = cot[0, p * 16 : (p + 1) * 16, :]


def pack_features(
    sizes,
    idx_ref,
    deg_ref,
    table_ref,
    hop_ref,
    seed_ref,
    keep_ref,
    pass_ref,
    rows,
    live_ref,
    table,
    hop,
    packed,
    hop32,
    seed,
    seed32,
    deg,
    idx,
    sems,
):
    owners, seeds, fan, f, fp = sizes
    groups = LANES // seeds
    hops = fan * seeds
    nodes = table.shape[2]
    loads = [
        pltpu.make_async_copy(source, target, sems.at[i])
        for i, (source, target) in enumerate(
            ((idx_ref, idx), (deg_ref, deg), (hop_ref, hop), (seed_ref, seed), (table_ref, table))
        )
    ]
    for load in loads:
        load.start()
    for load in loads[:4]:
        load.wait()
    for u in range(idx.shape[1]):
        live_ref[u] = jnp.where(deg[0] > u, idx[0, u], nodes)
    if fp != f:
        packed[...] = jnp.zeros_like(packed)
        seed32[...] = jnp.zeros_like(seed32)
    for tile in range(owners // groups):
        at = slice(tile * LANES, (tile + 1) * LANES)
        hop32[tile] = hop[0, :, :, at].astype(F32).reshape(f * fan, LANES)
        for block in range(fan // groups):
            taken = [
                hop32[tile, pl.ds(block * groups + k, f, stride=fan), :] for k in range(groups)
            ]
            for e in range(groups):
                packed[tile * groups + e, :f, block * LANES : (block + 1) * LANES] = mix_groups(
                    taken, seeds, e
                ).astype(BF16)
    seed32[:f, :] = seed[0].astype(F32)
    bands = fp // 16
    for tile in range(owners // groups):
        at = slice(tile * LANES, (tile + 1) * LANES)
        for block in range(-(-bands // groups)):
            taken = [
                seed32[(block * groups + k) * 16 : (block * groups + k + 1) * 16, at]
                if block * groups + k < bands
                else None
                for k in range(groups)
            ]
            row, lane = divmod(block * LANES, hops)
            for e in range(groups):
                packed[
                    tile * groups + e, fp + row * 16 : fp + row * 16 + 16, lane : lane + LANES
                ] = mix_groups(taken, seeds, e).astype(BF16)

    side = lax.rem(lax.axis_index("feat"), 2)
    for j in range(owners // 2):
        keep_ref[j] = packed[2 * j + side]
        pass_ref[j] = packed[2 * j + 1 - side]

    loads[4].wait()
    step = 512 if nodes % 512 == 0 else LANES
    lanes = rows.shape[1]
    tail = (lax.broadcasted_iota(jnp.int32, (lanes - f, step), 0) == 0).astype(F32)

    def flip(i, _):
        at = pl.multiple_of(i * step, step)
        block = jnp.concatenate([table[0, :, pl.ds(at, step)].astype(F32), tail], axis=0)
        rows[pl.ds(at, step), :] = block.T
        return 0

    lax.fori_loop(0, nodes // step, flip, 0)
    rows[nodes:, :] = jnp.zeros((8, lanes), F32)


def gather_means(sizes, across_pair, begin, idx, rows, *rest):
    owners, seeds, fan, f, fp = sizes
    if len(rest) > 2:
        first, second, out_ref, joined, picked = rest
        joined[: first.shape[0], :] = first[...]
        joined[first.shape[0] :, :] = second[...]
    else:
        out_ref, picked = rest
    slots = idx.shape[0]
    hops = out_ref.shape[2]
    side = lax.rem(lax.axis_index("feat"), 2)
    if across_pair:
        side = 1 - side
    for j in range(out_ref.shape[0]):
        src = (2 * (begin + j) + side) * seeds

        def slot_step(t, _):
            for k in range(seeds):
                total = rows[pl.ds(idx[0, t, src + k], 1), :]
                for u in range(1, slots):
                    total = total + rows[pl.ds(idx[u, t, src + k], 1), :]
                picked[pl.ds(t * seeds + k, 1), :] = total
            return 0

        lax.fori_loop(0, fan, slot_step, 0)
        flat = picked[...].T
        mean = flat[:f] / flat[f : f + 1]
        if fp != f:
            mean = jnp.concatenate([mean, jnp.zeros((fp - f, hops), F32)], axis=0)
        out_ref[j] = mean.astype(BF16)


def merge_by_part(keeps, passes, outs):
    count, rows = len(outs), keeps[0].shape[1]
    each = count // len(keeps)
    me = lax.axis_index("feat") // 2
    for step, out_ref in enumerate(outs):
        owner = lax.rem(me + step, count)
        for part, (keep_ref, passed_ref) in enumerate(zip(keeps, passes)):

            @pl.when(owner // each == part)
            def _():
                out_ref[:rows, :] = keep_ref[owner - part * each]
                out_ref[rows:, :] = passed_ref[owner - part * each]


def merge_pairs(parts, *rest):
    keeps, passes, outs = rest[:parts], rest[parts : 2 * parts], rest[2 * parts :]
    count, rows = len(outs), keeps[0].shape[1]
    if parts > 1:
        merge_by_part(keeps, passes, outs)
        return
    keep_ref, passed_ref = keeps[0], passes[0]
    me = lax.axis_index("feat") // 2
    for step, out_ref in enumerate(outs):
        owner = lax.rem(me + step, count)
        out_ref[:rows, :] = keep_ref[owner]
        out_ref[rows:, :] = passed_ref[owner]


def my_degrees(seed_degree_ref, seeds):
    half = seed_degree_ref.shape[1]
    wide = jnp.broadcast_to(seed_degree_ref[...], (8, half))
    shift = lax.rem(half - lax.axis_index("feat") * seeds, half)
    mine = pltpu.roll(wide, shift, axis=1)[:, :LANES]
    lane = lax.broadcasted_iota(jnp.int32, (8, LANES), 1)
    return jnp.where(lane < seeds, mine, 1)


def stack_features(sizes, seed_degree_ref, *rest):
    owners, seeds, fan, fp, seed_rows = sizes
    half = owners // 2
    own_blocks, agg_blocks = rest[:half], rest[half:owners]
    own_ref, mean_ref, send_ref = rest[owners:]
    groups = LANES // seeds
    hops = fan * seeds
    own_rows = fp + seed_rows
    lane = lax.broadcasted_iota(jnp.int32, (16, LANES), 1)
    for c in range(owners):
        ref, low = own_blocks[c // 2], c % 2 * own_rows
        own_ref[c * fp : (c + 1) * fp, :hops] = ref[low : low + fp, :]
        mean_ref[c * fp : (c + 1) * fp, :hops] = agg_blocks[c // 2][c % 2 * fp : (c % 2 + 1) * fp, :]
        for band in range(fp // 16):
            row, place = divmod(band * seeds, hops)
            tile = place // LANES
            row = low + fp + row * 16
            block = ref[row : row + 16, tile * LANES : (tile + 1) * LANES].astype(F32)
            turn = (-(band % groups)) % groups
            if turn:
                block = pltpu.roll(block, turn * seeds, axis=1)
            at = c * fp + band * 16
            own_ref[at : at + 16, hops:] = jnp.where(lane < seeds, block, 0.0).astype(BF16)
    degree = my_degrees(seed_degree_ref, seeds)[:1]
    node = lax.broadcasted_iota(jnp.int32, (hops, LANES), 0)
    seed = lax.broadcasted_iota(jnp.int32, (hops, LANES), 1)
    live = (node % seeds == seed) & (node // seeds < degree)
    total = jnp.dot(own_ref[:, :hops], live.astype(F32).astype(BF16), preferred_element_type=F32)
    mean_ref[:, hops:] = (total / degree.astype(F32)).astype(BF16)

    @pl.when(lax.axis_index("rep") == 0)
    def _():
        send_ref[...] = mean_ref[...]

    @pl.when(lax.axis_index("rep") != 0)
    def _():
        send_ref[...] = own_ref[...]


def forward(
    sizes,
    seed_degree_ref,
    own_ref,
    mean_ref,
    near_ref,
    far_ref,
    near_other_ref,
    far_other_ref,
    vs_ref,
    vn_ref,
    cot_ref,
    logits_ref,
    hidden_ref,
    dpre_ref,
    ws,
    wn,
):
    owners, seeds, fan, fp, width, offsets = sizes
    hops = fan * seeds
    half = owners // 2
    me = lax.axis_index("feat")
    block = near_ref.shape[0] // half

    def lay(near, far, w):
        for p, offset in enumerate(offsets):
            source = jnp.bitwise_xor(me, offset)
            c = 2 * lax.rem(me // 2 + half - source // 2, half) + offset % 2
            ref, q = (near, p) if p < half else (far, p - half)
            to = pl.ds(pl.multiple_of(c * fp, fp), fp)
            w[to, :] = ref[q * block : q * block + fp, :]

    @pl.when(lax.axis_index("rep") == 0)
    def _():
        lay(near_ref, far_ref, ws)
        lay(near_other_ref, far_other_ref, wn)

    @pl.when(lax.axis_index("rep") != 0)
    def _():
        lay(near_ref, far_ref, wn)
        lay(near_other_ref, far_other_ref, ws)

    pre = lax.dot_general(own_ref[...], ws[...], OVER_FIRST, preferred_element_type=F32)
    pre = pre + lax.dot_general(mean_ref[...], wn[...], OVER_FIRST, preferred_element_type=F32)
    pre = pre[: hops + seeds]
    sigma = jax.nn.sigmoid(pre)
    hidden = (pre * sigma).astype(BF16)
    slope = sigma * (1.0 + pre * (1.0 - sigma))
    degree = my_degrees(seed_degree_ref, seeds).astype(F32)
    degree = jnp.broadcast_to(degree[:1], (LANES, LANES)).T[:seeds]
    degree = jnp.concatenate([degree] * (width // LANES), axis=1)
    total = jnp.zeros((seeds, width), F32)
    for t in range(fan):
        row = hidden[t * seeds : (t + 1) * seeds].astype(F32)
        total = total + jnp.where(degree > t, row, 0.0)
    hidden_mean = (total / degree).astype(BF16)
    seed_hidden = hidden[hops:]
    hidden_ref[0] = seed_hidden
    hidden_ref[1] = hidden_mean
    logits = lax.dot_general(seed_hidden, vs_ref[...], OVER_LAST, preferred_element_type=F32)
    logits = logits + lax.dot_general(
        hidden_mean, vn_ref[...], OVER_LAST, preferred_element_type=F32
    )
    logits_ref[0] = logits.astype(BF16)
    cot = cot_ref[0]
    back_seed = jnp.dot(cot, vs_ref[...], preferred_element_type=F32)
    back_mean = jnp.dot(cot, vn_ref[...], preferred_element_type=F32)
    back_mean = back_mean / degree
    for t in range(fan):
        at = slice(t * seeds, (t + 1) * seeds)
        dpre_ref[at, :] = (jnp.where(degree > t, back_mean, 0.0) * slope[at]).astype(BF16)
    dpre_ref[hops : hops + seeds, :] = (back_seed * slope[hops:]).astype(BF16)
    dpre_ref[hops + seeds :, :] = jnp.zeros((LANES - seeds, width), BF16)


def products(
    sizes,
    own_ref,
    mean_ref,
    x_ref,
    dpre_ref,
    dpre_other_ref,
    hid_ref,
    hid_other_ref,
    keep_ref,
    pass_ref,
    both_ref,
):
    owners, seeds, fp = sizes

    def run(mine_ref, part):
        total = jnp.dot(mine_ref[...], dpre_ref[...], preferred_element_type=F32)
        total = total + jnp.dot(x_ref[...], dpre_other_ref[...], preferred_element_type=F32)
        for c in range(owners):
            block = total[c * fp : (c + 1) * fp]
            if c % 2:
                pass_ref[c // 2] = block.astype(BF16)
            else:
                keep_ref[c // 2] = block
        both_ref[:seeds, :] = hid_ref[part]
        both_ref[seeds:, :] = hid_other_ref[part]

    @pl.when(lax.axis_index("rep") == 0)
    def _():
        run(own_ref, 0)

    @pl.when(lax.axis_index("rep") != 0)
    def _():
        run(mean_ref, 1)


def join_pairs(keep_ref, passed_ref, first_ref, *outs):
    for i, out_ref in enumerate((first_ref, *outs)):
        total = keep_ref[i] + passed_ref[i].astype(F32)
        out_ref[...] = total.astype(out_ref.dtype)


def total_gradients(sizes, first_ref, hid_near, hid_far, near, far, near_other, far_other, *rest):
    owners, seeds, f, fp, classes = sizes
    half = owners // 2
    blocks = rest[: half - 1]
    grad_w_ref, grad_v_ref, cot = rest[half - 1 :]
    width = first_ref.shape[1]
    split = seeds // 16
    piece = width // split
    block = near.shape[0] // half
    total = first_ref[...]
    for ref in blocks:
        total = total + ref[...].astype(F32)
    grad_w_ref[...] = total[:f]
    grad_v = None
    for hid, mine, other in ((hid_near, near, near_other), (hid_far, far, far_other)):
        for q in range(half):
            for p in range(split):
                at = slice(p * piece, p * piece + cot.shape[1])
                source = slice(q * block + fp, q * block + fp + 16)
                row = q * 2 * seeds + p * 16
                cot[row : row + 16, :] = mine[source, at]
                cot[row + seeds : row + seeds + 16, :] = other[source, at]
        part = lax.dot_general(cot[...], hid[...], OVER_FIRST, preferred_element_type=F32)
        grad_v = part if grad_v is None else grad_v + part
    grad_v_ref[...] = grad_v[:classes]


def place_gradients(w_mine, w_other, v_mine, v_other, ws_ref, wn_ref, vs_ref, vn_ref):
    @pl.when(lax.axis_index("rep") == 0)
    def _():
        ws_ref[...] = w_mine[...]
        wn_ref[...] = w_other[...]
        vs_ref[...] = v_mine[...]
        vn_ref[...] = v_other[...]

    @pl.when(lax.axis_index("rep") != 0)
    def _():
        ws_ref[...] = w_other[...]
        wn_ref[...] = w_mine[...]
        vs_ref[...] = v_other[...]
        vn_ref[...] = v_mine[...]


def swap(x):
    return lax.ppermute(x, "rep", [(0, 1), (1, 0)])


def shift_by(x, step, owners):
    return lax.ppermute(x, "feat", [(k, (k + step) % owners) for k in range(owners)])


def across(x, mask, owners):
    return lax.ppermute(x, "feat", [(k, k ^ mask) for k in range(owners)])


def gather_blocks(x, owners):
    mask = owners // 2
    while mask > 1:
        x = jnp.concatenate([x, across(x, mask, owners)], axis=0)
        mask //= 2
    return x, across(x, 1, owners)


def offsets_of(owners):
    offsets = [0]
    mask = owners // 2
    while mask:
        offsets = offsets + [o ^ mask for o in offsets]
        mask //= 2
    return tuple(offsets)


def on_device(
    seed_feat,
    hop_feat,
    frontier,
    nbr_index,
    hop_degree,
    seed_degree,
    w_self,
    w_neigh,
    v_self,
    v_neigh,
    cotangent,
):
    owners = lax.axis_size("feat")
    seeds, classes = cotangent.shape[1:]
    f, width = w_self.shape
    fan = hop_feat.shape[2]
    nodes = frontier.shape[2]
    hops = fan * seeds
    fp = up(f, 16)
    seed_rows = 16 * -(-(fp // 16) * seeds // hops)
    depth = owners * fp
    struct = jax.ShapeDtypeStruct

    message = call(
        functools.partial(weight_message, (seeds, f, fp, classes)),
        "weight_message",
        struct((fp + 16, width), BF16),
        [HBM] * 3,
        [pltpu.VMEM(cotangent.shape, BF16), pltpu.SemaphoreType.DMA((2,))],
        vmem=62,
    )(w_self, w_neigh, cotangent)
    far_mask = owners // 2
    fetched = across(message, far_mask, owners)
    lanes = up(f + 1, LANES)
    half = owners * seeds
    own_rows = fp + seed_rows
    keep, passed, rows, live = call(
        functools.partial(pack_features, (owners, seeds, fan, f, fp)),
        "pack_features",
        (
            struct((owners // 2, own_rows, hops), BF16),
            struct((owners // 2, own_rows, hops), BF16),
            struct((nodes + 8, lanes), F32),
            struct(nbr_index.shape[1:], jnp.int32),
        ),
        [HBM] * 5,
        [
            pltpu.VMEM(frontier.shape, BF16),
            pltpu.VMEM(hop_feat.shape, BF16),
            pltpu.VMEM((owners, own_rows, hops), BF16),
            pltpu.VMEM((half // LANES, f * fan, LANES), F32),
            pltpu.VMEM(seed_feat.shape, BF16),
            pltpu.VMEM((fp, half), F32),
            pltpu.VMEM(hop_degree.shape, jnp.int32),
            pltpu.VMEM(nbr_index.shape, jnp.int32),
            pltpu.SemaphoreType.DMA((5,)),
        ],
        micros=4,
    )(nbr_index, hop_degree, frontier, hop_feat, seed_feat)
    pairs = owners // 2
    passed = across(passed, 1, owners)
    fetched, live = lax.optimization_barrier((fetched, live))
    pieces = [message, fetched]
    mask = far_mask // 2
    while mask > 1:
        joined = jnp.concatenate(pieces, axis=0)
        joined, live = lax.optimization_barrier((joined, live))
        pieces = [joined, across(joined, mask, owners)]
        mask //= 2

    def gather(across_pair, begin, live, joined=()):
        outs = (struct((pairs // 2, fp, hops), BF16),)
        if joined:
            outs += (struct((2 * joined[0].shape[0], width), BF16),)
        return call(
            functools.partial(gather_means, (owners, seeds, fan, f, fp), across_pair, begin),
            "gather_means",
            outs,
            [SMEM] + [VMEM] * (1 + len(joined)),
            [pltpu.VMEM((hops, lanes), F32)],
            micros=MICROS,
        )(live, rows, *joined)

    def merge(keeps, passes):
        rows = keeps[0].shape[1]
        return list(
            call(
                functools.partial(merge_pairs, len(keeps)),
                "merge_pairs",
                (struct((2 * rows, hops), BF16),) * pairs,
                [VMEM] * (len(keeps) + len(passes)),
            )(*keeps, *passes)
        )

    def along(blocks, sign):
        return [blocks[0]] + [
            shift_by(blocks[k], sign * 2 * k, owners) for k in range(1, pairs)
        ]

    (low_passed,) = gather(True, 0, live)
    passed, low_passed = lax.optimization_barrier((passed, low_passed))
    merged = merge([keep], [passed])
    merged[0], live = lax.optimization_barrier((merged[0], live))
    own_blocks = along(merged, 1)
    (high_passed,) = gather(True, pairs // 2, live)
    high_passed, live = lax.optimization_barrier((high_passed, live))
    low_passed = across(low_passed, 1, owners)
    high_passed = across(high_passed, 1, owners)
    live, low_passed = lax.optimization_barrier((live, low_passed))
    (low,) = gather(False, 0, live)
    low, live, high_passed, *own_blocks = lax.optimization_barrier(
        [low, live, high_passed] + own_blocks
    )
    high, near = gather(False, pairs // 2, live, pieces)
    far = across(near, 1, owners)
    agg_blocks = along(merge([low, high], [low_passed, high_passed]), 1)
    far, agg_blocks[1] = lax.optimization_barrier((far, agg_blocks[1]))
    near_other, far_other = swap(near), swap(far)

    stacked = struct((depth, hops + LANES), BF16)
    own, mean, send = call(
        functools.partial(stack_features, (owners, seeds, fan, fp, seed_rows)),
        "stack_features",
        (stacked, stacked, stacked),
        [VMEM] * (owners + 1),
    )(seed_degree, *own_blocks, *agg_blocks)
    x_other = swap(send)
    logits, hidden, dpre = call(
        functools.partial(forward, (owners, seeds, fan, fp, width, offsets_of(owners))),
        "forward",
        (
            struct((1, seeds, classes), BF16),
            struct((2, seeds, width), BF16),
            struct((hops + LANES, width), BF16),
        ),
        [VMEM] * 10,
        [pltpu.VMEM((depth, width), BF16), pltpu.VMEM((depth, width), BF16)],
        micros=3,
    )(
        seed_degree,
        own,
        mean,
        near,
        far,
        near_other,
        far_other,
        v_self.T,
        v_neigh.T,
        cotangent,
    )
    keep, passed, both = call(
        functools.partial(products, (owners, seeds, fp)),
        "products",
        (
            struct((pairs, fp, width), F32),
            struct((pairs, fp, width), BF16),
            struct((2 * seeds, width), BF16),
        ),
        [VMEM] * 7,
        micros=2,
    )(own, mean, x_other, dpre, swap(dpre), hidden, swap(hidden))
    passed = across(passed, 1, owners)
    hid_near, hid_far = gather_blocks(both, owners)
    blocks = call(
        join_pairs,
        "join_pairs",
        (struct((fp, width), F32),) + (struct((fp, width), BF16),) * (pairs - 1),
        [VMEM] * 2,
    )(keep, passed)
    first, *blocks = along(blocks, -1)
    grad_w, grad_v = call(
        functools.partial(total_gradients, (owners, seeds, f, fp, classes)),
        "total_gradients",
        (struct((f, width), F32), struct((classes, width), F32)),
        [VMEM] * (6 + pairs),
        [pltpu.VMEM((owners * seeds, up(classes, LANES)), BF16)],
    )(first, hid_near, hid_far, near, far, near_other, far_other, *blocks)
    grads = call(
        place_gradients,
        "place_gradients",
        (struct((f, width), F32),) * 2 + (struct((classes, width), F32),) * 2,
        [VMEM] * 4,
    )(grad_w, swap(grad_w), grad_v, swap(grad_v))
    return (logits, grads[0], grads[1], grads[2].T, grads[3].T)


def solution(mesh):
    placed = (
        P(("groups", "rep"), "feat", None),
        P(("groups", "rep"), "feat", None, None),
        P(("groups", "rep"), "feat", None),
        P(("groups", "rep"), None, None, None),
        P(("groups", "rep"), None, None),
        P(("groups", "rep"), None),
        P("feat", None),
        P("feat", None),
        P(),
        P(),
        P(("groups", "rep"), "feat", None),
    )
    return jax.shard_map(
        on_device,
        mesh=mesh,
        in_specs=placed,
        out_specs=(
            P(("groups", "rep"), "feat", None),
            P(("groups", "feat"), None),
            P(("groups", "feat"), None),
            P("groups", None),
            P("groups", None),
        ),
        check_vma=False,
    )
```

time: 115 us -> 93.1 us (0.81)
  waiting for transfers between devices: 63.8 us -> 31.8 us
  starting transfers between devices: 16.2 us -> 29 us
  local copies, waits for them, and re-layouts: 8.41 us -> 4.56 us
    all_to_all x3 -> x0, waiting for transfers between devices: 59.6 us -> none  [spread(): return lax.all_to_all(x, 'feat', 0, 0, tiled=True)]
    ppermute x0 -> x19, waiting for transfers between devices: none -> 28.9 us  [the longest x9 17.4 us: shift_by(): lax.ppermute(x, 'feat', [(k, (k + step) % owners) for k in range(owners)])]
    ppermute x0 -> x19, starting transfers between devices: none -> 27.8 us  [the longest x10 15.8 us: across(): return lax.ppermute(x, 'feat', [(k, k ^ mask) for k in range(owners)])]
    all_to_all x3 -> x0, starting transfers between devices: 14.7 us -> none  [spread(): return lax.all_to_all(x, 'feat', 0, 0, tiled=True)]
    unnamed x30 -> x20, local copies, waits for them, and re-layouts: 7.46 us -> 4.55 us
    pallas_call x5 -> x12, Pallas kernels: 22.4 us -> 24.2 us  [the longest x4 16.9 us: gather(): call(functools.partial(gather_means, (owners, seeds, fan, f, fp), across_...]
    ppermute x7, waiting for transfers between devices: 4.17 us -> 2.82 us  [swap(): return lax.ppermute(x, 'rep', [(0, 1), (1, 0)])]
    pallas_call x1, Pallas kernels: 1.75 us -> 0.41 us  [on_device(): call(functools.partial(stack_features, (owners, seeds, fan, fp, seed_rows...]
  transfers between devices with their start and end apart: 10 -> 26, of which waited for: 6 -> 11; matrix products, arithmetic and copies ran while one was open for 1% -> 1% of each run, Pallas kernels for 17% -> 19%
where the time goes in v3:
time: 93.1 us; the launch traced here: 92.7 us
  waiting for transfers between devices  31.8 us (34%)
  starting transfers between devices  29 us (31%)
  Pallas kernels  25.6 us (27%)
  local copies, waits for them, and re-layouts  4.56 us (5%)
    ppermute x9, waiting for transfers between devices, shift_by(): lax.ppermute(x, 'feat', [(k, (k + step) % owners) for k in range(owners)])  17.4 us
    pallas_call x4, Pallas kernels, gather(): call(functools.partial(gather_means, (owners, seeds, fan, f, fp), across_...  16.9 us
    ppermute x10, starting transfers between devices, across(): return lax.ppermute(x, 'feat', [(k, k ^ mask) for k in range(owners)])  15.8 us
    ppermute x9, starting transfers between devices, shift_by(): lax.ppermute(x, 'feat', [(k, (k + step) % owners) for k in range(owners)])  12.1 us
    ppermute x10, waiting for transfers between devices, across(): return lax.ppermute(x, 'feat', [(k, k ^ mask) for k in range(owners)])  11.5 us
    unnamed x20, local copies, waits for them, and re-layouts  4.55 us
    ppermute x7, waiting for transfers between devices, swap(): return lax.ppermute(x, 'rep', [(0, 1), (1, 0)])  2.82 us
    pallas_call x1, Pallas kernels, on_device(): call(functools.partial(pack_features, (owners, seeds, fan, f, fp)), 'pack...  2.33 us
  transfers between devices with their start and end apart: 26, of which 11 were waited for; matrix products, arithmetic and copies ran while one was open for 1% of the time, Pallas kernels for 19%

profile of v3, /device:TPU:0, one launch (start us, length us, event | category | flops | bytes accessed | tf_op | source)
XLA Modules:
  0.0 92.7 jit_solution(18420395619765186918)
XLA Ops:
  0.6 1.6 %weight_message.1 = bf16[112,512]{1,0:T(8,128)(2,1)} custom-call(bf16[96,512]{1,0:T(8,128)(2,1)} %ws_ref.1, bf16[96,512]{1,0:T(8,128)(2,1)} %wn_ref.1, bf16[1,32,153]{2,1,0:T(8,128)(2,1)} %cot_ref.3), custom_call_target="tpu_custom_call" | custom-call | bytes 3000000 | tf_op jit(solution)/shard_map/weight_message/pallas_call | solution.py:494
  2.2 4.1 %collective-permute-start.1 = (bf16[112,512]{1,0:T(8,128)(2,1)}, bf16[112,512]{1,0:T(8,128)(2,1)S(1)}, u32[]{:S(2)}, u32[]{:S(2)}) collective-permute-start(bf16[112,512]{1,0:T(8,128)(2,1)} %weight_message.1), channel_id=1, source_target_pairs={{0,8},{2,10},{4,12},{6,14},{8,0},{10,2},{12,4},{14,6},{1,9},{3,11}... | collective-permute-start | bytes 344072 | tf_op jit(solution)/shard_map/ppermute | solution.py:450
  6.3 1.3 %copy-done = bf16[1,96,6144]{2,1,0:T(8,128)(2,1)S(1)} copy-done((bf16[1,96,6144]{2,1,0:T(8,128)(2,1)S(1)}, bf16[1,96,6144]{2,1,0:T(8,128)(2,1)}, u32[]{:S(2)}) %copy-start) | copy-done | bytes 1179672
  7.6 1.0 %copy-done.1 = bf16[1,96,8,256]{3,2,1,0:T(8,128)(2,1)S(1)} copy-done((bf16[1,96,8,256]{3,2,1,0:T(8,128)(2,1)S(1)}, bf16[1,96,8,256]{3,2,1,0:T(8,128)(2,1)}, u32[]{:S(2)}) %copy-start.1) | copy-done | bytes 393240
  8.6 0.8 copy-done.5
  9.4 0.8 copy-done.6
  10.1 0.7 copy-done.7
  10.8 2.3 %pack_features.1 = (bf16[4,112,256]{2,1,0:T(8,128)(2,1)S(1)}, bf16[4,112,256]{2,1,0:T(8,128)(2,1)S(1)}, f32[6152,128]{1,0:T(8,128)S(1)}, s32[4,8,256]{2,1,0:T(8,128)S(1)}) custom-call(s32[1,4,8,256]{3,2,1,0:T(8,128)S(1)} %copy-done.6, s32[1,8,256]{2,1,0:T(8,128)S(1)} %copy-done.7, bf16[1,96,6144]{2,1,0:T(8,128)(2,1)S(1)} %copy-done, ...), custom_call_target="tpu_custom_call" | custom-call | bytes 12000000 | tf_op jit(solution)/shard_map/pack_features/pallas_call | solution.py:507
  13.2 1.6 %collective-permute-start = (bf16[4,112,256]{2,1,0:T(8,128)(2,1)S(1)}, bf16[4,112,256]{2,1,0:T(8,128)(2,1)S(1)}, u32[]{:S(2)}, u32[]{:S(2)}) collective-permute-start(bf16[4,112,256]{2,1,0:T(8,128)(2,1)S(1)} %get-tuple-element.60), channel_id=1, source_target_pairs={{0,2},{2,0},{4,6},{6,4},{8,10},{10,8},{12,14},{14,12},{1,3},{3,1},... | collective-permute-start | bytes 688136 | tf_op jit(solution)/shard_map/ppermute | solution.py:450
  14.8 0.0 collective-permute-done.1
  14.8 0.9 pad_maximum_fusion.rest_0_
  15.7 1.6 %collective-permute-start.7 = (bf16[224,512]{1,0:T(8,128)(2,1)S(1)}, bf16[224,512]{1,0:T(8,128)(2,1)S(1)}, u32[]{:S(2)}, u32[]{:S(2)}) collective-permute-start(bf16[224,512]{1,0:T(8,128)(2,1)S(1)} %pad_maximum_fusion.rest_0_), channel_id=1, source_target_pairs={{0,4},{2,6},{4,0},{6,2},{8,12},{10,14},{12,8},{14,10},{1,5},{3,7},... | collective-permute-start | bytes 688136 | tf_op jit(solution)/shard_map/ppermute | solution.py:450
  17.3 4.2 %gather_means.4 = bf16[2,96,256]{2,1,0:T(8,128)(2,1)S(1)} custom-call(s32[4,8,256]{2,1,0:T(8,128)S(1)} %get-tuple-element.82.idx, f32[6152,128]{1,0:T(8,128)S(1)} %get-tuple-element.65.rows), custom_call_target="tpu_custom_call" | custom-call | bytes 3000000 | tf_op jit(solution)/shard_map/gather_means/pallas_call | solution.py:545
  21.5 0.0 collective-permute-done.rest_1_
  21.6 0.6 collective-permute-start.2
  22.2 1.3 %collective-permute-start.4 = (bf16[224,256]{1,0:T(8,128)(2,1)S(1)}, bf16[224,256]{1,0:T(8,128)(2,1)S(1)}, u32[]{:S(2)}, u32[]{:S(2)}) collective-permute-start(bf16[224,256]{1,0:T(8,128)(2,1)S(1)} %get-tuple-element.74), channel_id=1, source_target_pairs={{0,4},{2,6},{4,8},{6,10},{8,12},{10,14},{12,0},{14,2},{1,5},{3,7},... | collective-permute-start | bytes 344072 | tf_op jit(solution)/shard_map/ppermute | solution.py:446
  23.5 0.3 collective-permute-start.5
  23.8 2.2 %collective-permute-start.6 = (bf16[224,256]{1,0:T(8,128)(2,1)S(1)}, bf16[224,256]{1,0:T(8,128)(2,1)S(1)}, u32[]{:S(2)}, u32[]{:S(2)}) collective-permute-start(bf16[224,256]{1,0:T(8,128)(2,1)S(1)} %get-tuple-element.76), channel_id=1, source_target_pairs={{0,12},{2,14},{4,0},{6,2},{8,4},{10,6},{12,8},{14,10},{1,13},{3,15... | collective-permute-start | bytes 344072 | tf_op jit(solution)/shard_map/ppermute | solution.py:446
  26.0 4.2 %gather_means.5 = bf16[2,96,256]{2,1,0:T(8,128)(2,1)S(1)} custom-call(s32[4,8,256]{2,1,0:T(8,128)S(1)} %get-tuple-element.82.idx, f32[6152,128]{1,0:T(8,128)S(1)} %get-tuple-element.65.rows), custom_call_target="tpu_custom_call" | custom-call | bytes 3000000 | tf_op jit(solution)/shard_map/gather_means/pallas_call | solution.py:545
  30.3 0.0 copy-start.8
  30.3 0.0 collective-permute-done.2.rest_2_
  30.3 1.6 %collective-permute-start.3 = (bf16[2,96,256]{2,1,0:T(8,128)(2,1)S(1)}, bf16[2,96,256]{2,1,0:T(8,128)(2,1)S(1)}, u32[]{:S(2)}, u32[]{:S(2)}) collective-permute-start(bf16[2,96,256]{2,1,0:T(8,128)(2,1)S(1)} %gather_means.5), channel_id=1, source_target_pairs={{0,2},{2,0},{4,6},{6,4},{8,10},{10,8},{12,14},{14,12},{1,3},{3,1},... | collective-permute-start | bytes 294920 | tf_op jit(solution)/shard_map/ppermute | solution.py:450
  31.9 4.2 %gather_means.6.rest_0_ = bf16[2,96,256]{2,1,0:T(8,128)(2,1)S(1)} custom-call(s32[4,8,256]{2,1,0:T(8,128)S(1)} %get-tuple-element.82.idx, f32[6152,128]{1,0:T(8,128)S(1)} %get-tuple-element.65.rows), custom_call_target="tpu_custom_call" | custom-call | bytes 3000000 | tf_op jit(solution)/shard_map/gather_means/pallas_call | solution.py:545
  36.1 0.0 copy-start.2
  36.1 0.0 copy-start.3
  36.1 0.0 copy-start.4
  36.1 0.0 collective-permute-done.4.rest_1_
  36.2 0.0 collective-permute-done.5.rest_2_
  36.2 0.0 collective-permute-done.7.rest_1_
  36.2 4.2 %gather_means.7 = (bf16[2,96,256]{2,1,0:T(8,128)(2,1)S(1)}, bf16[448,512]{1,0:T(8,128)(2,1)S(1)}) custom-call(s32[4,8,256]{2,1,0:T(8,128)S(1)} %get-tuple-element.82.idx, f32[6152,128]{1,0:T(8,128)S(1)} %get-tuple-element.65.rows, bf16[224,512]{1,0:T(8,128)(2,1)S(1)} %pad_maximum_fusion.rest_0_, bf16[224,512]{1,0:T(8,128)(2,1)S(1)} %collective-permute-done.7.rest_1_), custom_call_target="tpu_custom_call" | custom-call | bytes 3000000 | tf_op jit(solution)/shard_map/gather_means/pallas_call | solution.py:545
  40.4 0.6 collective-permute-start.8
  41.0 0.1 merge_pairs.3
  41.1 0.6 collective-permute-start.9
  41.7 5.9 %collective-permute-done.9.rest_5_ = bf16[192,256]{1,0:T(8,128)(2,1)S(1)} collective-permute-done((bf16[192,256]{1,0:T(8,128)(2,1)S(1)}, bf16[192,256]{1,0:T(8,128)(2,1)S(1)}, u32[]{:S(2)}, u32[]{:S(2)}) %collective-permute-start.9) | collective-permute-done | bytes 98336 | tf_op jit(solution)/shard_map/ppermute | solution.py:446
  47.5 3.2 %collective-permute-done.8.far_ref.far = bf16[448,512]{1,0:T(8,128)(2,1)S(1)} collective-permute-done((bf16[448,512]{1,0:T(8,128)(2,1)S(1)}, bf16[448,512]{1,0:T(8,128)(2,1)S(1)}, u32[]{:S(2)}, u32[]{:S(2)}) %collective-permute-start.8) | collective-permute-done | bytes 458784 | tf_op jit(solution)/shard_map/ppermute | solution.py:450
  50.8 1.7 %collective-permute-start.10 = (bf16[192,256]{1,0:T(8,128)(2,1)S(1)}, bf16[192,256]{1,0:T(8,128)(2,1)S(1)}, u32[]{:S(2)}, u32[]{:S(2)}) collective-permute-start(bf16[192,256]{1,0:T(8,128)(2,1)S(1)} %get-tuple-element.91), channel_id=1, source_target_pairs={{0,8},{2,10},{4,12},{6,14},{8,0},{10,2},{12,4},{14,6},{1,9},{3,11}... | collective-permute-start | bytes 294920 | tf_op jit(solution)/shard_map/ppermute | solution.py:446
  52.5 1.7 %collective-permute-start.11 = (bf16[192,256]{1,0:T(8,128)(2,1)S(1)}, bf16[192,256]{1,0:T(8,128)(2,1)S(1)}, u32[]{:S(2)}, u32[]{:S(2)}) collective-permute-start(bf16[192,256]{1,0:T(8,128)(2,1)S(1)} %get-tuple-element.92), channel_id=1, source_target_pairs={{0,12},{2,14},{4,0},{6,2},{8,4},{10,6},{12,8},{14,10},{1,13},{3,15... | collective-permute-start | bytes 294920 | tf_op jit(solution)/shard_map/ppermute | solution.py:446
  54.3 5.1 %collective-permute-done.10.rest_6_ = bf16[192,256]{1,0:T(8,128)(2,1)S(1)} collective-permute-done((bf16[192,256]{1,0:T(8,128)(2,1)S(1)}, bf16[192,256]{1,0:T(8,128)(2,1)S(1)}, u32[]{:S(2)}, u32[]{:S(2)}) %collective-permute-start.10) | collective-permute-done | bytes 98336 | tf_op jit(solution)/shard_map/ppermute | solution.py:446
  59.4 0.4 stack_features.1
  59.8 0.1 collective-permute-start.14
  60.0 1.9 %forward.1 = (bf16[1,32,153]{2,1,0:T(8,128)(2,1)}, bf16[2,32,512]{2,1,0:T(8,128)(2,1)S(1)}, bf16[384,512]{1,0:T(8,128)(2,1)S(1)}) custom-call(s32[1,256]{1,0:T(1,128)S(1)} %copy-done.8, bf16[768,384]{1,0:T(8,128)(2,1)S(1)} %get-tuple-element.93.own_ref, bf16[768,384]{1,0:T(8,128)(2,1)S(1)} %get-tuple-element.94.mean_ref, ...), custom_call_target="tpu_custom_call" | custom-call | bytes 9000000 | tf_op jit(solution)/shard_map/forward/pallas_call | solution.py:598
  61.9 0.5 collective-permute-start.15
  62.3 0.0 collective-permute-start.16
  62.4 1.4 %collective-permute-done.16.hid_other_ref = bf16[2,32,512]{2,1,0:T(8,128)(2,1)S(1)} collective-permute-done((bf16[2,32,512]{2,1,0:T(8,128)(2,1)S(1)}, bf16[2,32,512]{2,1,0:T(8,128)(2,1)S(1)}, u32[]{:S(2)}, u32[]{:S(2)}) %collective-permute-start.16) | collective-permute-done | bytes 65568 | tf_op jit(solution)/shard_map/ppermute | solution.py:442
  63.8 1.0 %products.1 = (f32[4,96,512]{2,1,0:T(8,128)S(1)}, bf16[4,96,512]{2,1,0:T(8,128)(2,1)S(1)}, bf16[64,512]{1,0:T(8,128)(2,1)S(1)}) custom-call(bf16[768,384]{1,0:T(8,128)(2,1)S(1)} %get-tuple-element.93.own_ref, bf16[768,384]{1,0:T(8,128)(2,1)S(1)} %get-tuple-element.94.mean_ref, bf16[768,384]{1,0:T(8,128)(2,1)S(1)} %collective-permute-done.14.x_ref, ...), custom_call_target="tpu_custom_call" | custom-call | bytes 6000000 | tf_op jit(solution)/shard_map/products/pallas_call | solution.py:621
  64.8 1.3 %collective-permute-start.18 = (bf16[64,512]{1,0:T(8,128)(2,1)S(1)}, bf16[64,512]{1,0:T(8,128)(2,1)S(1)}, u32[]{:S(2)}, u32[]{:S(2)}) collective-permute-start(bf16[64,512]{1,0:T(8,128)(2,1)S(1)} %get-tuple-element.103), channel_id=1, source_target_pairs={{0,8},{2,10},{4,12},{6,14},{8,0},{10,2},{12,4},{14,6},{1,9},{3,11}... | collective-permute-start | bytes 196616 | tf_op jit(solution)/shard_map/ppermute | solution.py:450
  66.1 1.0 %collective-permute-start.17 = (bf16[4,96,512]{2,1,0:T(8,128)(2,1)S(1)}, bf16[4,96,512]{2,1,0:T(8,128)(2,1)S(1)}, u32[]{:S(2)}, u32[]{:S(2)}) collective-permute-start(bf16[4,96,512]{2,1,0:T(8,128)(2,1)S(1)} %get-tuple-element.101), channel_id=1, source_target_pairs={{0,2},{2,0},{4,6},{6,4},{8,10},{10,8},{12,14},{14,12},{1,3},{3,1},... | collective-permute-start | bytes 1179656 | tf_op jit(solution)/shard_map/ppermute | solution.py:450
  67.1 3.0 %collective-permute-done.18 = bf16[64,512]{1,0:T(8,128)(2,1)S(1)} collective-permute-done((bf16[64,512]{1,0:T(8,128)(2,1)S(1)}, bf16[64,512]{1,0:T(8,128)(2,1)S(1)}, u32[]{:S(2)}, u32[]{:S(2)}) %collective-permute-start.18) | collective-permute-done | bytes 65568 | tf_op jit(solution)/shard_map/ppermute | solution.py:450
  70.1 2.4 %collective-permute-start.19 = (bf16[128,512]{1,0:T(8,128)(2,1)S(1)}, bf16[128,512]{1,0:T(8,128)(2,1)S(1)}, u32[]{:S(2)}, u32[]{:S(2)}) collective-permute-start(bf16[128,512]{1,0:T(8,128)(2,1)S(1)} %pad_maximum_fusion.1), channel_id=1, source_target_pairs={{0,4},{2,6},{4,0},{6,2},{8,12},{10,14},{12,8},{14,10},{1,5},{3,7},... | collective-permute-start | bytes 393224 | tf_op jit(solution)/shard_map/ppermute | solution.py:450
  72.5 3.2 %collective-permute-done.19 = bf16[128,512]{1,0:T(8,128)(2,1)S(1)} collective-permute-done((bf16[128,512]{1,0:T(8,128)(2,1)S(1)}, bf16[128,512]{1,0:T(8,128)(2,1)S(1)}, u32[]{:S(2)}, u32[]{:S(2)}) %collective-permute-start.19) | collective-permute-done | bytes 131104 | tf_op jit(solution)/shard_map/ppermute | solution.py:450
  75.7 1.0 %collective-permute-start.20 = (bf16[256,512]{1,0:T(8,128)(2,1)S(1)}, bf16[256,512]{1,0:T(8,128)(2,1)S(1)}, u32[]{:S(2)}, u32[]{:S(2)}) collective-permute-start(bf16[256,512]{1,0:T(8,128)(2,1)S(1)} %constant_dynamic-update-slice_fusion.hid_near), channel_id=1, source_target_pairs={{0,2},{2,0},{4,6},{6,4},{8,10},{10,8},{12,14},{14,12},{1,3},{3,1},... | collective-permute-start | bytes 786440 | tf_op jit(solution)/shard_map/ppermute | solution.py:450
  76.7 0.5 collective-permute-done.17.passed_ref
  77.2 0.1 join_pairs.1
  77.3 3.4 %collective-permute-start.21 = (bf16[96,512]{1,0:T(8,128)(2,1)S(1)}, bf16[96,512]{1,0:T(8,128)(2,1)S(1)}, u32[]{:S(2)}, u32[]{:S(2)}) collective-permute-start(bf16[96,512]{1,0:T(8,128)(2,1)S(1)} %get-tuple-element.104), channel_id=1, source_target_pairs={{0,12},{2,14},{4,0},{6,2},{8,4},{10,6},{12,8},{14,10},{1,13},{3,15... | collective-permute-start | bytes 294920 | tf_op jit(solution)/shard_map/ppermute | solution.py:446
  80.7 0.3 collective-permute-start.22
  81.0 0.3 collective-permute-start.23
  81.4 1.6 %collective-permute-done.20.hid_far = bf16[256,512]{1,0:T(8,128)(2,1)S(1)} collective-permute-done((bf16[256,512]{1,0:T(8,128)(2,1)S(1)}, bf16[256,512]{1,0:T(8,128)(2,1)S(1)}, u32[]{:S(2)}, u32[]{:S(2)}) %collective-permute-start.20) | collective-permute-done | bytes 262176 | tf_op jit(solution)/shard_map/ppermute | solution.py:450
  82.9 1.0 %collective-permute-done.21.rest_0_ = bf16[96,512]{1,0:T(8,128)(2,1)S(1)} collective-permute-done((bf16[96,512]{1,0:T(8,128)(2,1)S(1)}, bf16[96,512]{1,0:T(8,128)(2,1)S(1)}, u32[]{:S(2)}, u32[]{:S(2)}) %collective-permute-start.21) | collective-permute-done | bytes 98336 | tf_op jit(solution)/shard_map/ppermute | solution.py:446
  84.0 5.4 %collective-permute-done.22.rest_1_ = bf16[96,512]{1,0:T(8,128)(2,1)S(1)} collective-permute-done((bf16[96,512]{1,0:T(8,128)(2,1)S(1)}, bf16[96,512]{1,0:T(8,128)(2,1)S(1)}, u32[]{:S(2)}, u32[]{:S(2)}) %collective-permute-start.22) | collective-permute-done | bytes 98336 | tf_op jit(solution)/shard_map/ppermute | solution.py:446
  89.4 0.3 total_gradients.1
  89.7 0.1 collective-permute-start.25
  89.8 0.5 collective-permute-start.24
  90.3 1.4 %collective-permute-done.24.w_other = f32[96,512]{1,0:T(8,128)S(1)} collective-permute-done((f32[96,512]{1,0:T(8,128)S(1)}, f32[96,512]{1,0:T(8,128)S(1)}, u32[]{:S(2)}, u32[]{:S(2)}) %collective-permute-start.24) | collective-permute-done | bytes 196640 | tf_op jit(solution)/shard_map/ppermute | solution.py:442
  91.7 1.0 %place_gradients.1 = (f32[96,512]{1,0:T(8,128)}, f32[96,512]{1,0:T(8,128)}, f32[153,512]{1,0:T(8,128)}, f32[153,512]{1,0:T(8,128)}) custom-call(f32[96,512]{1,0:T(8,128)S(1)} %get-tuple-element.107.w_mine, f32[96,512]{1,0:T(8,128)S(1)} %collective-permute-done.24.w_other, f32[153,512]{1,0:T(8,128)S(1)} %get-tuple-element.108.v_mine, ...), custom_call_target="tpu_custom_call" | custom-call | bytes 3000000 | tf_op jit(solution)/shard_map/place_gradients/pallas_call | solution.py:648
  (25 shorter events, 0.1 us)
Async XLA Ops:
  2.2 12.6 %collective-permute-start.1 = (bf16[112,512]{1,0:T(8,128)(2,1)}, bf16[112,512]{1,0:T(8,128)(2,1)S(1)}, u32[]{:S(2)}, u32[]{:S(2)}) collective-permute-start(bf16[112,512]{1,0:T(8,128)(2,1)} %weight_message.1), channel_id=1, source_target_pairs={{0,8},{2,10},{4,12},{6,14},{8,0},{10,2},{12,4},{14,6},{1,9},{3,11}... | collective-permute-start | bytes 344072 | tf_op jit(solution)/shard_map/ppermute | solution.py:450
  6.3 1.3 %copy-start = (bf16[1,96,6144]{2,1,0:T(8,128)(2,1)S(1)}, bf16[1,96,6144]{2,1,0:T(8,128)(2,1)}, u32[]{:S(2)}) copy-start(bf16[1,96,6144]{2,1,0:T(8,128)(2,1)} %table_ref.1) | copy-start | bytes 3538948
  7.6 1.0 %copy-start.1 = (bf16[1,96,8,256]{3,2,1,0:T(8,128)(2,1)S(1)}, bf16[1,96,8,256]{3,2,1,0:T(8,128)(2,1)}, u32[]{:S(2)}) copy-start(bf16[1,96,8,256]{3,2,1,0:T(8,128)(2,1)} %hop_ref.1) | copy-start | bytes 1179652
  8.6 0.8 copy-start.5
  9.4 0.8 copy-start.6
  10.1 0.7 copy-start.7
  13.2 8.4 %collective-permute-start = (bf16[4,112,256]{2,1,0:T(8,128)(2,1)S(1)}, bf16[4,112,256]{2,1,0:T(8,128)(2,1)S(1)}, u32[]{:S(2)}, u32[]{:S(2)}) collective-permute-start(bf16[4,112,256]{2,1,0:T(8,128)(2,1)S(1)} %get-tuple-element.60), channel_id=1, source_target_pairs={{0,2},{2,0},{4,6},{6,4},{8,10},{10,8},{12,14},{14,12},{1,3},{3,1},... | collective-permute-start | bytes 688136 | tf_op jit(solution)/shard_map/ppermute | solution.py:450
  15.7 20.5 %collective-permute-start.7 = (bf16[224,512]{1,0:T(8,128)(2,1)S(1)}, bf16[224,512]{1,0:T(8,128)(2,1)S(1)}, u32[]{:S(2)}, u32[]{:S(2)}) collective-permute-start(bf16[224,512]{1,0:T(8,128)(2,1)S(1)} %pad_maximum_fusion.rest_0_), channel_id=1, source_target_pairs={{0,4},{2,6},{4,0},{6,2},{8,12},{10,14},{12,8},{14,10},{1,5},{3,7},... | collective-permute-start | bytes 688136 | tf_op jit(solution)/shard_map/ppermute | solution.py:450
  21.6 8.7 %collective-permute-start.2 = (bf16[2,96,256]{2,1,0:T(8,128)(2,1)S(1)}, bf16[2,96,256]{2,1,0:T(8,128)(2,1)S(1)}, u32[]{:S(2)}, u32[]{:S(2)}) collective-permute-start(bf16[2,96,256]{2,1,0:T(8,128)(2,1)S(1)} %gather_means.4), channel_id=1, source_target_pairs={{0,2},{2,0},{4,6},{6,4},{8,10},{10,8},{12,14},{14,12},{1,3},{3,1},... | collective-permute-start | bytes 294920 | tf_op jit(solution)/shard_map/ppermute | solution.py:450
  22.2 14.0 %collective-permute-start.4 = (bf16[224,256]{1,0:T(8,128)(2,1)S(1)}, bf16[224,256]{1,0:T(8,128)(2,1)S(1)}, u32[]{:S(2)}, u32[]{:S(2)}) collective-permute-start(bf16[224,256]{1,0:T(8,128)(2,1)S(1)} %get-tuple-element.74), channel_id=1, source_target_pairs={{0,4},{2,6},{4,8},{6,10},{8,12},{10,14},{12,0},{14,2},{1,5},{3,7},... | collective-permute-start | bytes 344072 | tf_op jit(solution)/shard_map/ppermute | solution.py:446
  23.5 12.7 %collective-permute-start.5 = (bf16[224,256]{1,0:T(8,128)(2,1)S(1)}, bf16[224,256]{1,0:T(8,128)(2,1)S(1)}, u32[]{:S(2)}, u32[]{:S(2)}) collective-permute-start(bf16[224,256]{1,0:T(8,128)(2,1)S(1)} %get-tuple-element.75), channel_id=1, source_target_pairs={{0,8},{2,10},{4,12},{6,14},{8,0},{10,2},{12,4},{14,6},{1,9},{3,11}... | collective-permute-start | bytes 344072 | tf_op jit(solution)/shard_map/ppermute | solution.py:446
  23.8 12.3 %collective-permute-start.6 = (bf16[224,256]{1,0:T(8,128)(2,1)S(1)}, bf16[224,256]{1,0:T(8,128)(2,1)S(1)}, u32[]{:S(2)}, u32[]{:S(2)}) collective-permute-start(bf16[224,256]{1,0:T(8,128)(2,1)S(1)} %get-tuple-element.76), channel_id=1, source_target_pairs={{0,12},{2,14},{4,0},{6,2},{8,4},{10,6},{12,8},{14,10},{1,13},{3,15... | collective-permute-start | bytes 344072 | tf_op jit(solution)/shard_map/ppermute | solution.py:446
  30.3 29.1 %copy-start.8 = (s32[1,256]{1,0:T(1,128)S(1)}, s32[1,256]{1,0:T(1,128)}, u32[]{:S(2)}) copy-start(s32[1,256]{1,0:T(1,128)} %seed_degree_ref.3) | copy-start | bytes 3076
  30.3 5.8 %collective-permute-start.3 = (bf16[2,96,256]{2,1,0:T(8,128)(2,1)S(1)}, bf16[2,96,256]{2,1,0:T(8,128)(2,1)S(1)}, u32[]{:S(2)}, u32[]{:S(2)}) collective-permute-start(bf16[2,96,256]{2,1,0:T(8,128)(2,1)S(1)} %gather_means.5), channel_id=1, source_target_pairs={{0,2},{2,0},{4,6},{6,4},{8,10},{10,8},{12,14},{14,12},{1,3},{3,1},... | collective-permute-start | bytes 294920 | tf_op jit(solution)/shard_map/ppermute | solution.py:450
  36.1 23.8 %copy-start.2 = (bf16[512,153]{0,1:T(8,128)(2,1)S(1)}, bf16[512,153]{0,1:T(8,128)(2,1)}, u32[]{:S(2)}) copy-start(bf16[512,153]{0,1:T(8,128)(2,1)} %param.19) | copy-start | bytes 470020
  36.1 23.8 %copy-start.3 = (bf16[512,153]{0,1:T(8,128)(2,1)S(1)}, bf16[512,153]{0,1:T(8,128)(2,1)}, u32[]{:S(2)}) copy-start(bf16[512,153]{0,1:T(8,128)(2,1)} %param.20) | copy-start | bytes 470020
  36.1 23.8 %copy-start.4 = (bf16[1,32,153]{2,1,0:T(8,128)(2,1)S(1)}, bf16[1,32,153]{2,1,0:T(8,128)(2,1)}, u32[]{:S(2)}) copy-start(bf16[1,32,153]{2,1,0:T(8,128)(2,1)} %cot_ref.3) | copy-start | bytes 29380
  40.4 10.4 %collective-permute-start.8 = (bf16[448,512]{1,0:T(8,128)(2,1)S(1)}, bf16[448,512]{1,0:T(8,128)(2,1)S(1)}, u32[]{:S(2)}, u32[]{:S(2)}) collective-permute-start(bf16[448,512]{1,0:T(8,128)(2,1)S(1)} %get-tuple-element.88.near_ref.near), channel_id=1, source_target_pairs={{0,2},{2,0},{4,6},{6,4},{8,10},{10,8},{12,14},{14,12},{1,3},{3,1},... | collective-permute-start | bytes 1376264 | tf_op jit(solution)/shard_map/ppermute | solution.py:450
  41.1 6.5 %collective-permute-start.9 = (bf16[192,256]{1,0:T(8,128)(2,1)S(1)}, bf16[192,256]{1,0:T(8,128)(2,1)S(1)}, u32[]{:S(2)}, u32[]{:S(2)}) collective-permute-start(bf16[192,256]{1,0:T(8,128)(2,1)S(1)} %get-tuple-element.89), channel_id=1, source_target_pairs={{0,4},{2,6},{4,8},{6,10},{8,12},{10,14},{12,0},{14,2},{1,5},{3,7},... | collective-permute-start | bytes 294920 | tf_op jit(solution)/shard_map/ppermute | solution.py:446
  41.7 18.2 %collective-permute-start.12 = (bf16[448,512]{1,0:T(8,128)(2,1)S(1)}, bf16[448,512]{1,0:T(8,128)(2,1)S(1)}, u32[]{:S(2)}, u32[]{:S(2)}) collective-permute-start(bf16[448,512]{1,0:T(8,128)(2,1)S(1)} %get-tuple-element.88.near_ref.near), channel_id=1, source_target_pairs={{0,1},{1,0},{2,3},{3,2},{4,5},{5,4},{6,7},{7,6},{8,9},{9,8},{10,11... | collective-permute-start | bytes 1376264 | tf_op jit(solution)/shard_map/ppermute | solution.py:442
  50.8 9.1 %collective-permute-start.13 = (bf16[448,512]{1,0:T(8,128)(2,1)S(1)}, bf16[448,512]{1,0:T(8,128)(2,1)S(1)}, u32[]{:S(2)}, u32[]{:S(2)}) collective-permute-start(bf16[448,512]{1,0:T(8,128)(2,1)S(1)} %collective-permute-done.8.far_ref.far), channel_id=1, source_target_pairs={{0,1},{1,0},{2,3},{3,2},{4,5},{5,4},{6,7},{7,6},{8,9},{9,8},{10,11... | collective-permute-start | bytes 1376264 | tf_op jit(solution)/shard_map/ppermute | solution.py:442
  50.8 8.6 %collective-permute-start.10 = (bf16[192,256]{1,0:T(8,128)(2,1)S(1)}, bf16[192,256]{1,0:T(8,128)(2,1)S(1)}, u32[]{:S(2)}, u32[]{:S(2)}) collective-permute-start(bf16[192,256]{1,0:T(8,128)(2,1)S(1)} %get-tuple-element.91), channel_id=1, source_target_pairs={{0,8},{2,10},{4,12},{6,14},{8,0},{10,2},{12,4},{14,6},{1,9},{3,11}... | collective-permute-start | bytes 294920 | tf_op jit(solution)/shard_map/ppermute | solution.py:446
  52.5 6.9 %collective-permute-start.11 = (bf16[192,256]{1,0:T(8,128)(2,1)S(1)}, bf16[192,256]{1,0:T(8,128)(2,1)S(1)}, u32[]{:S(2)}, u32[]{:S(2)}) collective-permute-start(bf16[192,256]{1,0:T(8,128)(2,1)S(1)} %get-tuple-element.92), channel_id=1, source_target_pairs={{0,12},{2,14},{4,0},{6,2},{8,4},{10,6},{12,8},{14,10},{1,13},{3,15... | collective-permute-start | bytes 294920 | tf_op jit(solution)/shard_map/ppermute | solution.py:446
  59.8 4.0 %collective-permute-start.14 = (bf16[768,384]{1,0:T(8,128)(2,1)S(1)}, bf16[768,384]{1,0:T(8,128)(2,1)S(1)}, u32[]{:S(2)}, u32[]{:S(2)}) collective-permute-start(bf16[768,384]{1,0:T(8,128)(2,1)S(1)} %get-tuple-element.97), channel_id=1, source_target_pairs={{0,1},{1,0},{2,3},{3,2},{4,5},{5,4},{6,7},{7,6},{8,9},{9,8},{10,11... | collective-permute-start | bytes 1769480 | tf_op jit(solution)/shard_map/ppermute | solution.py:442
  61.9 1.9 %collective-permute-start.15 = (bf16[384,512]{1,0:T(8,128)(2,1)S(1)}, bf16[384,512]{1,0:T(8,128)(2,1)S(1)}, u32[]{:S(2)}, u32[]{:S(2)}) collective-permute-start(bf16[384,512]{1,0:T(8,128)(2,1)S(1)} %get-tuple-element.98.dpre_ref), channel_id=1, source_target_pairs={{0,1},{1,0},{2,3},{3,2},{4,5},{5,4},{6,7},{7,6},{8,9},{9,8},{10,11... | collective-permute-start | bytes 1179656 | tf_op jit(solution)/shard_map/ppermute | solution.py:442
  62.3 1.4 %collective-permute-start.16 = (bf16[2,32,512]{2,1,0:T(8,128)(2,1)S(1)}, bf16[2,32,512]{2,1,0:T(8,128)(2,1)S(1)}, u32[]{:S(2)}, u32[]{:S(2)}) collective-permute-start(bf16[2,32,512]{2,1,0:T(8,128)(2,1)S(1)} %get-tuple-element.99.hid_ref), channel_id=1, source_target_pairs={{0,1},{1,0},{2,3},{3,2},{4,5},{5,4},{6,7},{7,6},{8,9},{9,8},{10,11... | collective-permute-start | bytes 196616 | tf_op jit(solution)/shard_map/ppermute | solution.py:442
  64.8 5.3 %collective-permute-start.18 = (bf16[64,512]{1,0:T(8,128)(2,1)S(1)}, bf16[64,512]{1,0:T(8,128)(2,1)S(1)}, u32[]{:S(2)}, u32[]{:S(2)}) collective-permute-start(bf16[64,512]{1,0:T(8,128)(2,1)S(1)} %get-tuple-element.103), channel_id=1, source_target_pairs={{0,8},{2,10},{4,12},{6,14},{8,0},{10,2},{12,4},{14,6},{1,9},{3,11}... | collective-permute-start | bytes 196616 | tf_op jit(solution)/shard_map/ppermute | solution.py:450
  66.1 11.1 %collective-permute-start.17 = (bf16[4,96,512]{2,1,0:T(8,128)(2,1)S(1)}, bf16[4,96,512]{2,1,0:T(8,128)(2,1)S(1)}, u32[]{:S(2)}, u32[]{:S(2)}) collective-permute-start(bf16[4,96,512]{2,1,0:T(8,128)(2,1)S(1)} %get-tuple-element.101), channel_id=1, source_target_pairs={{0,2},{2,0},{4,6},{6,4},{8,10},{10,8},{12,14},{14,12},{1,3},{3,1},... | collective-permute-start | bytes 1179656 | tf_op jit(solution)/shard_map/ppermute | solution.py:450
  70.1 5.6 %collective-permute-start.19 = (bf16[128,512]{1,0:T(8,128)(2,1)S(1)}, bf16[128,512]{1,0:T(8,128)(2,1)S(1)}, u32[]{:S(2)}, u32[]{:S(2)}) collective-permute-start(bf16[128,512]{1,0:T(8,128)(2,1)S(1)} %pad_maximum_fusion.1), channel_id=1, source_target_pairs={{0,4},{2,6},{4,0},{6,2},{8,12},{10,14},{12,8},{14,10},{1,5},{3,7},... | collective-permute-start | bytes 393224 | tf_op jit(solution)/shard_map/ppermute | solution.py:450
  75.7 7.2 %collective-permute-start.20 = (bf16[256,512]{1,0:T(8,128)(2,1)S(1)}, bf16[256,512]{1,0:T(8,128)(2,1)S(1)}, u32[]{:S(2)}, u32[]{:S(2)}) collective-permute-start(bf16[256,512]{1,0:T(8,128)(2,1)S(1)} %constant_dynamic-update-slice_fusion.hid_near), channel_id=1, source_target_pairs={{0,2},{2,0},{4,6},{6,4},{8,10},{10,8},{12,14},{14,12},{1,3},{3,1},... | collective-permute-start | bytes 786440 | tf_op jit(solution)/shard_map/ppermute | solution.py:450
  77.3 6.7 %collective-permute-start.21 = (bf16[96,512]{1,0:T(8,128)(2,1)S(1)}, bf16[96,512]{1,0:T(8,128)(2,1)S(1)}, u32[]{:S(2)}, u32[]{:S(2)}) collective-permute-start(bf16[96,512]{1,0:T(8,128)(2,1)S(1)} %get-tuple-element.104), channel_id=1, source_target_pairs={{0,12},{2,14},{4,0},{6,2},{8,4},{10,6},{12,8},{14,10},{1,13},{3,15... | collective-permute-start | bytes 294920 | tf_op jit(solution)/shard_map/ppermute | solution.py:446
  80.7 8.6 %collective-permute-start.22 = (bf16[96,512]{1,0:T(8,128)(2,1)S(1)}, bf16[96,512]{1,0:T(8,128)(2,1)S(1)}, u32[]{:S(2)}, u32[]{:S(2)}) collective-permute-start(bf16[96,512]{1,0:T(8,128)(2,1)S(1)} %get-tuple-element.105), channel_id=1, source_target_pairs={{0,8},{2,10},{4,12},{6,14},{8,0},{10,2},{12,4},{14,6},{1,9},{3,11}... | collective-permute-start | bytes 294920 | tf_op jit(solution)/shard_map/ppermute | solution.py:446
  81.0 8.3 %collective-permute-start.23 = (bf16[96,512]{1,0:T(8,128)(2,1)S(1)}, bf16[96,512]{1,0:T(8,128)(2,1)S(1)}, u32[]{:S(2)}, u32[]{:S(2)}) collective-permute-start(bf16[96,512]{1,0:T(8,128)(2,1)S(1)} %get-tuple-element.106), channel_id=1, source_target_pairs={{0,4},{2,6},{4,8},{6,10},{8,12},{10,14},{12,0},{14,2},{1,5},{3,7},... | collective-permute-start | bytes 294920 | tf_op jit(solution)/shard_map/ppermute | solution.py:446
  89.7 2.0 %collective-permute-start.25 = (f32[153,512]{1,0:T(8,128)S(1)}, f32[153,512]{1,0:T(8,128)S(1)}, u32[]{:S(2)}, u32[]{:S(2)}) collective-permute-start(f32[153,512]{1,0:T(8,128)S(1)} %get-tuple-element.108.v_mine), channel_id=1, source_target_pairs={{0,1},{1,0},{2,3},{3,2},{4,5},{5,4},{6,7},{7,6},{8,9},{9,8},{10,11... | collective-permute-start | bytes 940040 | tf_op jit(solution)/shard_map/ppermute | solution.py:442
  89.8 1.9 %collective-permute-start.24 = (f32[96,512]{1,0:T(8,128)S(1)}, f32[96,512]{1,0:T(8,128)S(1)}, u32[]{:S(2)}, u32[]{:S(2)}) collective-permute-start(f32[96,512]{1,0:T(8,128)S(1)} %get-tuple-element.107.w_mine), channel_id=1, source_target_pairs={{0,1},{1,0},{2,3},{3,2},{4,5},{5,4},{6,7},{7,6},{8,9},{9,8},{10,11... | collective-permute-start | bytes 589832 | tf_op jit(solution)/shard_map/ppermute | solution.py:442

commit v4 on v3

--- a/solution.py
+++ b/solution.py
@@ -10,7 +10,8 @@
 F32 = jnp.float32
 BF16 = jnp.bfloat16
 LANES = 128
-MICROS = 1
+PACK = 56
+FIRST = 62
 VMEM = pl.BlockSpec(memory_space=pltpu.VMEM)
 SMEM = pl.BlockSpec(memory_space=pltpu.SMEM)
 HBM = pl.BlockSpec(memory_space=pltpu.HBM)
@@ -86,12 +87,11 @@
     sizes,
     idx_ref,
     deg_ref,
-    table_ref,
     hop_ref,
     seed_ref,
+    table_ref,
     keep_ref,
     pass_ref,
-    rows,
     live_ref,
     table,
     hop,
@@ -103,10 +103,9 @@
     idx,
     sems,
 ):
-    owners, seeds, fan, f, fp = sizes
+    owners, seeds, fan, f, fp, nodes = sizes
     groups = LANES // seeds
     hops = fan * seeds
-    nodes = table.shape[2]
     loads = [
         pltpu.make_async_copy(source, target, sems.at[i])
         for i, (source, target) in enumerate(
@@ -117,8 +116,12 @@
         load.start()
     for load in loads[:4]:
         load.wait()
+    tiles = owners * seeds // LANES
     for u in range(idx.shape[1]):
-        live_ref[u] = jnp.where(deg[0] > u, idx[0, u], nodes)
+        live = jnp.where(deg[0] > u, idx[0, u], nodes)
+        for tile in range(tiles):
+            at = (u * tiles + tile) * fan
+            live_ref[at : at + fan, :] = live[:, tile * LANES : (tile + 1) * LANES]
     if fp != f:
         packed[...] = jnp.zeros_like(packed)
         seed32[...] = jnp.zeros_like(seed32)
@@ -152,10 +155,14 @@
 
     side = lax.rem(lax.axis_index("feat"), 2)
     for j in range(owners // 2):
-        keep_ref[j] = packed[2 * j + side]
-        pass_ref[j] = packed[2 * j + 1 - side]
-
+        owner = lax.rem(lax.axis_index("feat") // 2 + j, owners // 2)
+        keep_ref[j] = packed[2 * owner + side]
+        pass_ref[j] = packed[2 * owner + 1 - side]
     loads[4].wait()
+
+
+def turn_table(f, table, rows):
+    nodes = table.shape[2]
     step = 512 if nodes % 512 == 0 else LANES
     lanes = rows.shape[1]
     tail = (lax.broadcasted_iota(jnp.int32, (lanes - f, step), 0) == 0).astype(F32)
@@ -170,27 +177,27 @@
     rows[nodes:, :] = jnp.zeros((8, lanes), F32)
 
 
-def gather_means(sizes, across_pair, begin, idx, rows, *rest):
+def gather_means(sizes, across_pair, steps, idx, rows, out_ref, picked):
     owners, seeds, fan, f, fp = sizes
-    if len(rest) > 2:
-        first, second, out_ref, joined, picked = rest
-        joined[: first.shape[0], :] = first[...]
-        joined[first.shape[0] :, :] = second[...]
-    else:
-        out_ref, picked = rest
-    slots = idx.shape[0]
     hops = out_ref.shape[2]
-    side = lax.rem(lax.axis_index("feat"), 2)
+    groups = LANES // seeds
+    tiles = owners * seeds // LANES
+    slots = idx.shape[0] // (tiles * fan * LANES)
+    me = lax.axis_index("feat")
+    side = lax.rem(me, 2)
     if across_pair:
         side = 1 - side
-    for j in range(out_ref.shape[0]):
-        src = (2 * (begin + j) + side) * seeds
+    for i, step in enumerate(steps):
+        owner = 2 * lax.rem(me // 2 + step, owners // 2) + side
+        first = owner // groups * (fan * LANES) + lax.rem(owner, groups) * seeds
 
         def slot_step(t, _):
+            src = first + t * LANES
             for k in range(seeds):
-                total = rows[pl.ds(idx[0, t, src + k], 1), :]
+                total = rows[pl.ds(idx[src + k], 1), :]
                 for u in range(1, slots):
-                    total = total + rows[pl.ds(idx[u, t, src + k], 1), :]
+                    at = src + (u * tiles * fan * LANES + k)
+                    total = total + rows[pl.ds(idx[at], 1), :]
                 picked[pl.ds(t * seeds + k, 1), :] = total
             return 0
 
@@ -199,35 +206,23 @@
         mean = flat[:f] / flat[f : f + 1]
         if fp != f:
             mean = jnp.concatenate([mean, jnp.zeros((fp - f, hops), F32)], axis=0)
-        out_ref[j] = mean.astype(BF16)
-
-
-def merge_by_part(keeps, passes, outs):
-    count, rows = len(outs), keeps[0].shape[1]
-    each = count // len(keeps)
-    me = lax.axis_index("feat") // 2
-    for step, out_ref in enumerate(outs):
-        owner = lax.rem(me + step, count)
-        for part, (keep_ref, passed_ref) in enumerate(zip(keeps, passes)):
-
-            @pl.when(owner // each == part)
-            def _():
-                out_ref[:rows, :] = keep_ref[owner - part * each]
-                out_ref[rows:, :] = passed_ref[owner - part * each]
-
-
-def merge_pairs(parts, *rest):
-    keeps, passes, outs = rest[:parts], rest[parts : 2 * parts], rest[2 * parts :]
-    count, rows = len(outs), keeps[0].shape[1]
-    if parts > 1:
-        merge_by_part(keeps, passes, outs)
-        return
-    keep_ref, passed_ref = keeps[0], passes[0]
-    me = lax.axis_index("feat") // 2
-    for step, out_ref in enumerate(outs):
-        owner = lax.rem(me + step, count)
-        out_ref[:rows, :] = keep_ref[owner]
-        out_ref[rows:, :] = passed_ref[owner]
+        out_ref[i] = mean.astype(BF16)
+
+
+def join(first, second, joined):
+    joined[: first.shape[0], :] = first[...]
+    joined[first.shape[0] :, :] = second[...]
+
+
+def merge_pairs(keep_ref, pass_ref, *rest):
+    count, rows = keep_ref.shape[:2]
+    outs = rest
+    if len(rest) > count:
+        join(rest[0], rest[1], rest[-1])
+        outs = rest[2:-1]
+    for i, out_ref in enumerate(outs):
+        out_ref[:rows, :] = keep_ref[i]
+        out_ref[rows:, :] = pass_ref[i]
 
 
 def my_degrees(seed_degree_ref, seeds):
@@ -450,10 +445,17 @@
     return lax.ppermute(x, "feat", [(k, k ^ mask) for k in range(owners)])
 
 
+def join_rows(first, second):
+    rows, columns = first.shape
+    return call(
+        join, "join_rows", jax.ShapeDtypeStruct((2 * rows, columns), first.dtype), [VMEM] * 2
+    )(first, second)
+
+
 def gather_blocks(x, owners):
     mask = owners // 2
     while mask > 1:
-        x = jnp.concatenate([x, across(x, mask, owners)], axis=0)
+        x = join_rows(x, across(x, mask, owners))
         mask //= 2
     return x, across(x, 1, owners)
 
@@ -497,25 +499,24 @@
         struct((fp + 16, width), BF16),
         [HBM] * 3,
         [pltpu.VMEM(cotangent.shape, BF16), pltpu.SemaphoreType.DMA((2,))],
-        vmem=62,
+        vmem=FIRST,
     )(w_self, w_neigh, cotangent)
     far_mask = owners // 2
     fetched = across(message, far_mask, owners)
     lanes = up(f + 1, LANES)
     half = owners * seeds
     own_rows = fp + seed_rows
-    keep, passed, rows, live = call(
-        functools.partial(pack_features, (owners, seeds, fan, f, fp)),
+    keep, passed, live, table = call(
+        functools.partial(pack_features, (owners, seeds, fan, f, fp, nodes)),
         "pack_features",
         (
             struct((owners // 2, own_rows, hops), BF16),
             struct((owners // 2, own_rows, hops), BF16),
-            struct((nodes + 8, lanes), F32),
-            struct(nbr_index.shape[1:], jnp.int32),
+            struct((nbr_index.size // LANES, LANES), jnp.int32),
+            struct(frontier.shape, BF16),
         ),
         [HBM] * 5,
         [
-            pltpu.VMEM(frontier.shape, BF16),
             pltpu.VMEM(hop_feat.shape, BF16),
             pltpu.VMEM((owners, own_rows, hops), BF16),
             pltpu.VMEM((half // LANES, f * fan, LANES), F32),
@@ -525,67 +526,75 @@
             pltpu.VMEM(nbr_index.shape, jnp.int32),
             pltpu.SemaphoreType.DMA((5,)),
         ],
-        micros=4,
-    )(nbr_index, hop_degree, frontier, hop_feat, seed_feat)
+        vmem=PACK,
+    )(nbr_index, hop_degree, hop_feat, seed_feat, frontier)
+    rows = call(
+        functools.partial(turn_table, f),
+        "turn_table",
+        struct((nodes + 8, lanes), F32),
+        [VMEM],
+    )(table)
+    live = live.reshape(-1)
     pairs = owners // 2
     passed = across(passed, 1, owners)
-    fetched, live = lax.optimization_barrier((fetched, live))
+    fetched, live, rows = lax.optimization_barrier((fetched, live, rows))
     pieces = [message, fetched]
     mask = far_mask // 2
     while mask > 1:
-        joined = jnp.concatenate(pieces, axis=0)
+        joined = join_rows(*pieces)
         joined, live = lax.optimization_barrier((joined, live))
         pieces = [joined, across(joined, mask, owners)]
         mask //= 2
 
-    def gather(across_pair, begin, live, joined=()):
-        outs = (struct((pairs // 2, fp, hops), BF16),)
-        if joined:
-            outs += (struct((2 * joined[0].shape[0], width), BF16),)
+    def gather(across_pair, steps, live):
         return call(
-            functools.partial(gather_means, (owners, seeds, fan, f, fp), across_pair, begin),
+            functools.partial(gather_means, (owners, seeds, fan, f, fp), across_pair, steps),
             "gather_means",
-            outs,
-            [SMEM] + [VMEM] * (1 + len(joined)),
+            struct((len(steps), fp, hops), BF16),
+            [SMEM, VMEM],
             [pltpu.VMEM((hops, lanes), F32)],
-            micros=MICROS,
-        )(live, rows, *joined)
-
-    def merge(keeps, passes):
-        rows = keeps[0].shape[1]
+        )(live, rows)
+
+    def merge(keep, passed, pieces=()):
+        count, rows = keep.shape[:2]
+        outs = (struct((2 * rows, hops), BF16),) * count
+        if pieces:
+            outs += (struct((2 * pieces[0].shape[0], width), BF16),)
         return list(
-            call(
-                functools.partial(merge_pairs, len(keeps)),
-                "merge_pairs",
-                (struct((2 * rows, hops), BF16),) * pairs,
-                [VMEM] * (len(keeps) + len(passes)),
-            )(*keeps, *passes)
+            call(merge_pairs, "merge_pairs", outs, [VMEM] * (2 + len(pieces)))(
+                keep, passed, *pieces
+            )
         )
 
-    def along(blocks, sign):
-        return [blocks[0]] + [
-            shift_by(blocks[k], sign * 2 * k, owners) for k in range(1, pairs)
+    def along(blocks, sign, steps):
+        return [
+            shift_by(x, sign * 2 * k, owners) if k else x for k, x in zip(steps, blocks)
         ]
 
-    (low_passed,) = gather(True, 0, live)
-    passed, low_passed = lax.optimization_barrier((passed, low_passed))
-    merged = merge([keep], [passed])
+    order = sorted(range(1, pairs), key=lambda k: (-min(k, pairs - k), k)) + [0]
+    early, late = order[: pairs // 2], order[pairs // 2 :]
+    early_passed = gather(True, early, live)
+    passed, early_passed = lax.optimization_barrier((passed, early_passed))
+    *merged, near = merge(keep, passed, pieces)
     merged[0], live = lax.optimization_barrier((merged[0], live))
-    own_blocks = along(merged, 1)
-    (high_passed,) = gather(True, pairs // 2, live)
-    high_passed, live = lax.optimization_barrier((high_passed, live))
-    low_passed = across(low_passed, 1, owners)
-    high_passed = across(high_passed, 1, owners)
-    live, low_passed = lax.optimization_barrier((live, low_passed))
-    (low,) = gather(False, 0, live)
-    low, live, high_passed, *own_blocks = lax.optimization_barrier(
-        [low, live, high_passed] + own_blocks
+    own_blocks = along(merged, 1, range(pairs))
+    far = across(near, 1, owners)
+    early_passed = across(early_passed, 1, owners)
+    late_passed = gather(True, late, live)
+    late_passed, live = lax.optimization_barrier((late_passed, live))
+    late_passed = across(late_passed, 1, owners)
+    live, early_passed = lax.optimization_barrier((live, early_passed))
+    means = gather(False, early, live)
+    merged = merge(means, early_passed)
+    merged[0], live, near, far, *own_blocks = lax.optimization_barrier(
+        [merged[0], live, near, far] + own_blocks
     )
-    high, near = gather(False, pairs // 2, live, pieces)
-    far = across(near, 1, owners)
-    agg_blocks = along(merge([low, high], [low_passed, high_passed]), 1)
-    far, agg_blocks[1] = lax.optimization_barrier((far, agg_blocks[1]))
+    agg_blocks = dict(zip(early, along(merged, 1, early)))
+    means = gather(False, late, live)
     near_other, far_other = swap(near), swap(far)
+    means, near_other, far_other = lax.optimization_barrier((means, near_other, far_other))
+    agg_blocks |= dict(zip(late, along(merge(means, late_passed), 1, late)))
+    agg_blocks = [agg_blocks[k] for k in range(pairs)]
 
     stacked = struct((depth, hops + LANES), BF16)
     own, mean, send = call(
@@ -637,7 +646,7 @@
         (struct((fp, width), F32),) + (struct((fp, width), BF16),) * (pairs - 1),
         [VMEM] * 2,
     )(keep, passed)
-    first, *blocks = along(blocks, -1)
+    first, *blocks = along(blocks, -1, range(pairs))
     grad_w, grad_v = call(
         functools.partial(total_gradients, (owners, seeds, f, fp, classes)),
         "total_gradients",

time: 93.1 us -> 84.5 us (0.908)
  local copies, waits for them, and re-layouts: 4.56 us -> 1.3 us
  Pallas kernels: 25.6 us -> 22.5 us
  waiting for transfers between devices: 31.8 us -> 29.7 us
    ppermute x9, waiting for transfers between devices: 17.4 us -> 9.33 us  [shift_by(): lax.ppermute(x, 'feat', [(k, (k + step) % owners) for k in range(owners)])]
    ppermute x10, waiting for transfers between devices: 11.5 us -> 17.5 us  [across(): return lax.ppermute(x, 'feat', [(k, k ^ mask) for k in range(owners)])]
    pallas_call x4, Pallas kernels: 16.9 us -> 12.1 us  [gather(): call(functools.partial(gather_means, (owners, seeds, fan, f, fp), across_...]
    ppermute x9, starting transfers between devices: 12.1 us -> 16 us  [shift_by(): lax.ppermute(x, 'feat', [(k, (k + step) % owners) for k in range(owners)])]
    ppermute x10, starting transfers between devices: 15.8 us -> 12.2 us  [across(): return lax.ppermute(x, 'feat', [(k, k ^ mask) for k in range(owners)])]
    unnamed x20 -> x16, local copies, waits for them, and re-layouts: 4.55 us -> 1.3 us
    pallas_call x3 -> x8, Pallas kernels: 2.43 us -> 4.18 us  [the longest x1 2.8 us: on_device(): call(functools.partial(pack_features, (owners, seeds, fan, f, fp, nodes))...]
  transfers between devices with their start and end apart: 26 -> 26, of which waited for: 11 -> 10; matrix products, arithmetic and copies ran while one was open for 1% -> 0% of each run, Pallas kernels for 19% -> 22%
where the time goes in v4:
time: 84.5 us; the launch traced here: 84.3 us
  starting transfers between devices  29.9 us (35%)
  waiting for transfers between devices  29.7 us (35%)
  Pallas kernels  22.5 us (27%)
  local copies, waits for them, and re-layouts  1.3 us (2%)
  between operations  0.89 us (1%)
    ppermute x10, waiting for transfers between devices, across(): return lax.ppermute(x, 'feat', [(k, k ^ mask) for k in range(owners)])  17.5 us
    ppermute x9, starting transfers between devices, shift_by(): lax.ppermute(x, 'feat', [(k, (k + step) % owners) for k in range(owners)])  16 us
    ppermute x10, starting transfers between devices, across(): return lax.ppermute(x, 'feat', [(k, k ^ mask) for k in range(owners)])  12.2 us
    pallas_call x4, Pallas kernels, gather(): call(functools.partial(gather_means, (owners, seeds, fan, f, fp), across_...  12.1 us
    ppermute x9, waiting for transfers between devices, shift_by(): lax.ppermute(x, 'feat', [(k, (k + step) % owners) for k in range(owners)])  9.33 us
    ppermute x7, waiting for transfers between devices, swap(): return lax.ppermute(x, 'rep', [(0, 1), (1, 0)])  2.81 us
    pallas_call x1, Pallas kernels, on_device(): call(functools.partial(pack_features, (owners, seeds, fan, f, fp, nodes))...  2.8 us
    pallas_call x1, Pallas kernels, on_device(): call(functools.partial(forward, (owners, seeds, fan, fp, width, offsets_o...  1.88 us
  transfers between devices with their start and end apart: 26, of which 10 were waited for; matrix products, arithmetic and copies ran while one was open for 0% of the time, Pallas kernels for 22%

profile of v4, /device:TPU:0, one launch (start us, length us, event | category | flops | bytes accessed | tf_op | source)
XLA Modules:
  0.0 84.3 jit_solution(3841960465427221781)
XLA Ops:
  0.6 1.6 %weight_message.1.first = bf16[112,512]{1,0:T(8,128)(2,1)} custom-call(bf16[96,512]{1,0:T(8,128)(2,1)} %ws_ref.1, bf16[96,512]{1,0:T(8,128)(2,1)} %wn_ref.1, bf16[1,32,153]{2,1,0:T(8,128)(2,1)} %cot_ref.3), custom_call_target="tpu_custom_call" | custom-call | bytes 3000000 | tf_op jit(solution)/shard_map/weight_message/pallas_call | solution.py:496
  2.2 4.1 %collective-permute-start.1 = (bf16[112,512]{1,0:T(8,128)(2,1)}, bf16[112,512]{1,0:T(8,128)(2,1)S(1)}, u32[]{:S(2)}, u32[]{:S(2)}) collective-permute-start(bf16[112,512]{1,0:T(8,128)(2,1)} %weight_message.1.first), channel_id=1, source_target_pairs={{0,8},{2,10},{4,12},{6,14},{8,0},{10,2},{12,4},{14,6},{1,9},{3,11}... | collective-permute-start | bytes 344072 | tf_op jit(solution)/shard_map/ppermute | solution.py:445
  6.3 2.8 %pack_features.1 = (bf16[4,112,256]{2,1,0:T(8,128)(2,1)}, bf16[4,112,256]{2,1,0:T(8,128)(2,1)}, s32[64,128]{1,0:T(8,128)}, bf16[1,96,6144]{2,1,0:T(8,128)(2,1)}) custom-call(s32[1,4,8,256]{3,2,1,0:T(8,128)} %idx_ref.1, s32[1,8,256]{2,1,0:T(8,128)} %deg_ref.1, bf16[1,96,8,256]{3,2,1,0:T(8,128)(2,1)} %hop_ref.1, bf16[1,96,256]{2,1,0:T(8,128)(2,1)} %seed_ref.1, ...), custom_call_target="tpu_custom_call" | custom-call | bytes 3000000 | tf_op jit(solution)/shard_map/pack_features/pallas_call | solution.py:509
  9.1 1.6 %collective-permute-start = (bf16[4,112,256]{2,1,0:T(8,128)(2,1)}, bf16[4,112,256]{2,1,0:T(8,128)(2,1)S(1)}, u32[]{:S(2)}, u32[]{:S(2)}) collective-permute-start(bf16[4,112,256]{2,1,0:T(8,128)(2,1)} %get-tuple-element.62), channel_id=1, source_target_pairs={{0,2},{2,0},{4,6},{6,4},{8,10},{10,8},{12,14},{14,12},{1,3},{3,1},... | collective-permute-start | bytes 688136 | tf_op jit(solution)/shard_map/ppermute | solution.py:445
  10.7 1.3 %copy-done = bf16[1,96,6144]{2,1,0:T(8,128)(2,1)S(1)} copy-done((bf16[1,96,6144]{2,1,0:T(8,128)(2,1)S(1)}, bf16[1,96,6144]{2,1,0:T(8,128)(2,1)}, u32[]{:S(2)}) %copy-start) | copy-done | bytes 1179672
  12.0 1.2 %turn_table.1.rows = f32[6152,128]{1,0:T(8,128)S(1)} custom-call(bf16[1,96,6144]{2,1,0:T(8,128)(2,1)S(1)} %copy-done), custom_call_target="tpu_custom_call" | custom-call | bytes 3000000 | tf_op jit(solution)/shard_map/turn_table/pallas_call | solution.py:531
  13.2 0.0 collective-permute-done.1.second
  13.3 0.0 copy-start.3
  13.3 1.6 %collective-permute-start.2 = (bf16[224,512]{1,0:T(8,128)(2,1)S(1)}, bf16[224,512]{1,0:T(8,128)(2,1)S(1)}, u32[]{:S(2)}, u32[]{:S(2)}) collective-permute-start(bf16[224,512]{1,0:T(8,128)(2,1)S(1)} %join_rows.3.rest_0_), channel_id=1, source_target_pairs={{0,4},{2,6},{4,0},{6,2},{8,12},{10,14},{12,8},{14,10},{1,5},{3,7},... | collective-permute-start | bytes 688136 | tf_op jit(solution)/shard_map/ppermute | solution.py:445
  14.9 3.0 %gather_means.4 = bf16[2,96,256]{2,1,0:T(8,128)(2,1)S(1)} custom-call(s32[8192]{0:T(1024)S(1)} %bitcast.5, f32[6152,128]{1,0:T(8,128)S(1)} %turn_table.1.rows), custom_call_target="tpu_custom_call" | custom-call | bytes 3000000 | tf_op jit(solution)/shard_map/gather_means/pallas_call | solution.py:550
  18.0 0.0 collective-permute-done.pass_ref
  18.0 2.2 %collective-permute-done.2.rest_1_ = bf16[224,512]{1,0:T(8,128)(2,1)S(1)} collective-permute-done((bf16[224,512]{1,0:T(8,128)(2,1)S(1)}, bf16[224,512]{1,0:T(8,128)(2,1)S(1)}, u32[]{:S(2)}, u32[]{:S(2)}) %collective-permute-start.2) | collective-permute-done | bytes 229408 | tf_op jit(solution)/shard_map/ppermute | solution.py:445
  20.1 0.1 merge_pairs.3
  20.2 0.6 collective-permute-start.4
  20.8 1.6 %collective-permute-start.5 = (bf16[224,256]{1,0:T(8,128)(2,1)S(1)}, bf16[224,256]{1,0:T(8,128)(2,1)S(1)}, u32[]{:S(2)}, u32[]{:S(2)}) collective-permute-start(bf16[224,256]{1,0:T(8,128)(2,1)S(1)} %get-tuple-element.80), channel_id=1, source_target_pairs={{0,4},{2,6},{4,8},{6,10},{8,12},{10,14},{12,0},{14,2},{1,5},{3,7},... | collective-permute-start | bytes 344072 | tf_op jit(solution)/shard_map/ppermute | solution.py:441
  22.4 3.2 %collective-permute-start.6 = (bf16[224,256]{1,0:T(8,128)(2,1)S(1)}, bf16[224,256]{1,0:T(8,128)(2,1)S(1)}, u32[]{:S(2)}, u32[]{:S(2)}) collective-permute-start(bf16[224,256]{1,0:T(8,128)(2,1)S(1)} %get-tuple-element.81), channel_id=1, source_target_pairs={{0,8},{2,10},{4,12},{6,14},{8,0},{10,2},{12,4},{14,6},{1,9},{3,11}... | collective-permute-start | bytes 344072 | tf_op jit(solution)/shard_map/ppermute | solution.py:441
  25.5 1.2 %collective-permute-start.7 = (bf16[224,256]{1,0:T(8,128)(2,1)S(1)}, bf16[224,256]{1,0:T(8,128)(2,1)S(1)}, u32[]{:S(2)}, u32[]{:S(2)}) collective-permute-start(bf16[224,256]{1,0:T(8,128)(2,1)S(1)} %get-tuple-element.82), channel_id=1, source_target_pairs={{0,12},{2,14},{4,0},{6,2},{8,4},{10,6},{12,8},{14,10},{1,13},{3,15... | collective-permute-start | bytes 344072 | tf_op jit(solution)/shard_map/ppermute | solution.py:441
  26.7 0.5 collective-permute-start.3
  27.2 3.0 %gather_means.5 = bf16[2,96,256]{2,1,0:T(8,128)(2,1)S(1)} custom-call(s32[8192]{0:T(1024)S(1)} %bitcast.6, f32[6152,128]{1,0:T(8,128)S(1)} %turn_table.1.rows), custom_call_target="tpu_custom_call" | custom-call | bytes 3000000 | tf_op jit(solution)/shard_map/gather_means/pallas_call | solution.py:550
  30.2 2.9 %collective-permute-done.3.pass_ref = bf16[2,96,256]{2,1,0:T(8,128)(2,1)S(1)} collective-permute-done((bf16[2,96,256]{2,1,0:T(8,128)(2,1)S(1)}, bf16[2,96,256]{2,1,0:T(8,128)(2,1)S(1)}, u32[]{:S(2)}, u32[]{:S(2)}) %collective-permute-start.3) | collective-permute-done | bytes 98336 | tf_op jit(solution)/shard_map/ppermute | solution.py:445
  33.2 3.0 %gather_means.6.keep_ref = bf16[2,96,256]{2,1,0:T(8,128)(2,1)S(1)} custom-call(s32[8192]{0:T(1024)S(1)} %bitcast.7, f32[6152,128]{1,0:T(8,128)S(1)} %turn_table.1.rows), custom_call_target="tpu_custom_call" | custom-call | bytes 3000000 | tf_op jit(solution)/shard_map/gather_means/pallas_call | solution.py:550
  36.2 0.0 collective-permute-done.5.rest_1_
  36.2 0.0 collective-permute-done.6.rest_2_
  36.2 0.0 collective-permute-done.7.rest_3_
  36.2 0.0 collective-permute-done.4.far_ref.far
  36.2 0.1 collective-permute-start.8
  36.3 0.5 collective-permute-start.9
  36.8 0.5 collective-permute-start.10
  37.3 1.6 %collective-permute-start.11 = (bf16[192,256]{1,0:T(8,128)(2,1)S(1)}, bf16[192,256]{1,0:T(8,128)(2,1)S(1)}, u32[]{:S(2)}, u32[]{:S(2)}) collective-permute-start(bf16[192,256]{1,0:T(8,128)(2,1)S(1)} %get-tuple-element.93), channel_id=1, source_target_pairs={{0,4},{2,6},{4,8},{6,10},{8,12},{10,14},{12,0},{14,2},{1,5},{3,7},... | collective-permute-start | bytes 294920 | tf_op jit(solution)/shard_map/ppermute | solution.py:441
  39.0 3.0 %gather_means.7.keep_ref = bf16[2,96,256]{2,1,0:T(8,128)(2,1)S(1)} custom-call(s32[8192]{0:T(1024)S(1)} %bitcast.8, f32[6152,128]{1,0:T(8,128)S(1)} %turn_table.1.rows), custom_call_target="tpu_custom_call" | custom-call | bytes 3000000 | tf_op jit(solution)/shard_map/gather_means/pallas_call | solution.py:550
  42.0 4.0 %collective-permute-start.12 = (bf16[192,256]{1,0:T(8,128)(2,1)S(1)}, bf16[192,256]{1,0:T(8,128)(2,1)S(1)}, u32[]{:S(2)}, u32[]{:S(2)}) collective-permute-start(bf16[192,256]{1,0:T(8,128)(2,1)S(1)} %get-tuple-element.94), channel_id=1, source_target_pairs={{0,8},{2,10},{4,12},{6,14},{8,0},{10,2},{12,4},{14,6},{1,9},{3,11}... | collective-permute-start | bytes 294920 | tf_op jit(solution)/shard_map/ppermute | solution.py:441
  46.0 0.0 collective-permute-done.8.near_other_ref.near_other
  46.0 0.0 collective-permute-done.9.far_other_ref.far_other
  46.0 0.0 collective-permute-done.10.pass_ref
  46.1 1.6 %collective-permute-start.13 = (bf16[192,256]{1,0:T(8,128)(2,1)S(1)}, bf16[192,256]{1,0:T(8,128)(2,1)S(1)}, u32[]{:S(2)}, u32[]{:S(2)}) collective-permute-start(bf16[192,256]{1,0:T(8,128)(2,1)S(1)} %get-tuple-element.95), channel_id=1, source_target_pairs={{0,12},{2,14},{4,0},{6,2},{8,4},{10,6},{12,8},{14,10},{1,13},{3,15... | collective-permute-start | bytes 294920 | tf_op jit(solution)/shard_map/ppermute | solution.py:441
  47.6 0.0 collective-permute-done.11.rest_5_
  47.6 4.1 %collective-permute-done.12.rest_6_ = bf16[192,256]{1,0:T(8,128)(2,1)S(1)} collective-permute-done((bf16[192,256]{1,0:T(8,128)(2,1)S(1)}, bf16[192,256]{1,0:T(8,128)(2,1)S(1)}, u32[]{:S(2)}, u32[]{:S(2)}) %collective-permute-start.12) | collective-permute-done | bytes 98336 | tf_op jit(solution)/shard_map/ppermute | solution.py:441
  51.7 0.0 collective-permute-done.13.rest_7_
  51.7 0.4 stack_features.1
  52.1 0.1 collective-permute-start.14
  52.2 1.9 %forward.1 = (bf16[1,32,153]{2,1,0:T(8,128)(2,1)}, bf16[2,32,512]{2,1,0:T(8,128)(2,1)S(1)}, bf16[384,512]{1,0:T(8,128)(2,1)S(1)}) custom-call(s32[1,256]{1,0:T(1,128)S(1)} %copy-done.7, bf16[768,384]{1,0:T(8,128)(2,1)S(1)} %get-tuple-element.96.own_ref, bf16[768,384]{1,0:T(8,128)(2,1)S(1)} %get-tuple-element.97.mean_ref, ...), custom_call_target="tpu_custom_call" | custom-call | bytes 9000000 | tf_op jit(solution)/shard_map/forward/pallas_call | solution.py:607
  54.1 0.5 collective-permute-start.15
  54.6 0.0 collective-permute-start.16
  54.6 1.4 %collective-permute-done.16.hid_other_ref = bf16[2,32,512]{2,1,0:T(8,128)(2,1)S(1)} collective-permute-done((bf16[2,32,512]{2,1,0:T(8,128)(2,1)S(1)}, bf16[2,32,512]{2,1,0:T(8,128)(2,1)S(1)}, u32[]{:S(2)}, u32[]{:S(2)}) %collective-permute-start.16) | collective-permute-done | bytes 65568 | tf_op jit(solution)/shard_map/ppermute | solution.py:437
  56.0 0.0 collective-permute-done.15.dpre_other_ref
  56.0 1.0 %products.1 = (f32[4,96,512]{2,1,0:T(8,128)S(1)}, bf16[4,96,512]{2,1,0:T(8,128)(2,1)S(1)}, bf16[64,512]{1,0:T(8,128)(2,1)S(1)}) custom-call(bf16[768,384]{1,0:T(8,128)(2,1)S(1)} %get-tuple-element.96.own_ref, bf16[768,384]{1,0:T(8,128)(2,1)S(1)} %get-tuple-element.97.mean_ref, bf16[768,384]{1,0:T(8,128)(2,1)S(1)} %collective-permute-done.14.x_ref, ...), custom_call_target="tpu_custom_call" | custom-call | bytes 6000000 | tf_op jit(solution)/shard_map/products/pallas_call | solution.py:630
  57.0 0.6 collective-permute-start.17
  57.6 0.8 collective-permute-start.18
  58.4 5.8 %collective-permute-done.18.second = bf16[64,512]{1,0:T(8,128)(2,1)S(1)} collective-permute-done((bf16[64,512]{1,0:T(8,128)(2,1)S(1)}, bf16[64,512]{1,0:T(8,128)(2,1)S(1)}, u32[]{:S(2)}, u32[]{:S(2)}) %collective-permute-start.18) | collective-permute-done | bytes 65568 | tf_op jit(solution)/shard_map/ppermute | solution.py:445
  64.2 0.4 collective-permute-start.19
  64.6 4.7 %collective-permute-done.19.second = bf16[128,512]{1,0:T(8,128)(2,1)S(1)} collective-permute-done((bf16[128,512]{1,0:T(8,128)(2,1)S(1)}, bf16[128,512]{1,0:T(8,128)(2,1)S(1)}, u32[]{:S(2)}, u32[]{:S(2)}) %collective-permute-start.19) | collective-permute-done | bytes 131104 | tf_op jit(solution)/shard_map/ppermute | solution.py:445
  69.2 1.6 %collective-permute-start.20 = (bf16[256,512]{1,0:T(8,128)(2,1)S(1)}, bf16[256,512]{1,0:T(8,128)(2,1)S(1)}, u32[]{:S(2)}, u32[]{:S(2)}) collective-permute-start(bf16[256,512]{1,0:T(8,128)(2,1)S(1)} %join_rows.5.hid_near), channel_id=1, source_target_pairs={{0,2},{2,0},{4,6},{6,4},{8,10},{10,8},{12,14},{14,12},{1,3},{3,1},... | collective-permute-start | bytes 786440 | tf_op jit(solution)/shard_map/ppermute | solution.py:445
  70.8 0.1 join_pairs.1
  70.9 2.2 %collective-permute-start.21 = (bf16[96,512]{1,0:T(8,128)(2,1)S(1)}, bf16[96,512]{1,0:T(8,128)(2,1)S(1)}, u32[]{:S(2)}, u32[]{:S(2)}) collective-permute-start(bf16[96,512]{1,0:T(8,128)(2,1)S(1)} %get-tuple-element.108), channel_id=1, source_target_pairs={{0,12},{2,14},{4,0},{6,2},{8,4},{10,6},{12,8},{14,10},{1,13},{3,15... | collective-permute-start | bytes 294920 | tf_op jit(solution)/shard_map/ppermute | solution.py:441
  73.1 0.0 collective-permute-start.22
  73.1 0.6 collective-permute-start.23
  73.7 2.0 %collective-permute-done.20.hid_far = bf16[256,512]{1,0:T(8,128)(2,1)S(1)} collective-permute-done((bf16[256,512]{1,0:T(8,128)(2,1)S(1)}, bf16[256,512]{1,0:T(8,128)(2,1)S(1)}, u32[]{:S(2)}, u32[]{:S(2)}) %collective-permute-start.20) | collective-permute-done | bytes 262176 | tf_op jit(solution)/shard_map/ppermute | solution.py:445
  75.7 1.4 %collective-permute-done.21.rest_0_ = bf16[96,512]{1,0:T(8,128)(2,1)S(1)} collective-permute-done((bf16[96,512]{1,0:T(8,128)(2,1)S(1)}, bf16[96,512]{1,0:T(8,128)(2,1)S(1)}, u32[]{:S(2)}, u32[]{:S(2)}) %collective-permute-start.21) | collective-permute-done | bytes 98336 | tf_op jit(solution)/shard_map/ppermute | solution.py:441
  77.1 3.8 %collective-permute-done.22.rest_1_ = bf16[96,512]{1,0:T(8,128)(2,1)S(1)} collective-permute-done((bf16[96,512]{1,0:T(8,128)(2,1)S(1)}, bf16[96,512]{1,0:T(8,128)(2,1)S(1)}, u32[]{:S(2)}, u32[]{:S(2)}) %collective-permute-start.22) | collective-permute-done | bytes 98336 | tf_op jit(solution)/shard_map/ppermute | solution.py:441
  80.9 0.3 total_gradients.1
  81.3 0.1 collective-permute-start.25
  81.4 0.5 collective-permute-start.24
  81.8 1.4 %collective-permute-done.24.w_other = f32[96,512]{1,0:T(8,128)S(1)} collective-permute-done((f32[96,512]{1,0:T(8,128)S(1)}, f32[96,512]{1,0:T(8,128)S(1)}, u32[]{:S(2)}, u32[]{:S(2)}) %collective-permute-start.24) | collective-permute-done | bytes 196640 | tf_op jit(solution)/shard_map/ppermute | solution.py:437
  83.3 1.0 %place_gradients.1 = (f32[96,512]{1,0:T(8,128)}, f32[96,512]{1,0:T(8,128)}, f32[153,512]{1,0:T(8,128)}, f32[153,512]{1,0:T(8,128)}) custom-call(f32[96,512]{1,0:T(8,128)S(1)} %get-tuple-element.111.w_mine, f32[96,512]{1,0:T(8,128)S(1)} %collective-permute-done.24.w_other, f32[153,512]{1,0:T(8,128)S(1)} %get-tuple-element.112.v_mine, ...), custom_call_target="tpu_custom_call" | custom-call | bytes 3000000 | tf_op jit(solution)/shard_map/place_gradients/pallas_call | solution.py:657
  (23 shorter events, 0.1 us)
Async XLA Ops:
  2.2 11.0 %collective-permute-start.1 = (bf16[112,512]{1,0:T(8,128)(2,1)}, bf16[112,512]{1,0:T(8,128)(2,1)S(1)}, u32[]{:S(2)}, u32[]{:S(2)}) collective-permute-start(bf16[112,512]{1,0:T(8,128)(2,1)} %weight_message.1.first), channel_id=1, source_target_pairs={{0,8},{2,10},{4,12},{6,14},{8,0},{10,2},{12,4},{14,6},{1,9},{3,11}... | collective-permute-start | bytes 344072 | tf_op jit(solution)/shard_map/ppermute | solution.py:445
  9.1 8.8 %collective-permute-start = (bf16[4,112,256]{2,1,0:T(8,128)(2,1)}, bf16[4,112,256]{2,1,0:T(8,128)(2,1)S(1)}, u32[]{:S(2)}, u32[]{:S(2)}) collective-permute-start(bf16[4,112,256]{2,1,0:T(8,128)(2,1)} %get-tuple-element.62), channel_id=1, source_target_pairs={{0,2},{2,0},{4,6},{6,4},{8,10},{10,8},{12,14},{14,12},{1,3},{3,1},... | collective-permute-start | bytes 688136 | tf_op jit(solution)/shard_map/ppermute | solution.py:445
  10.7 1.3 %copy-start = (bf16[1,96,6144]{2,1,0:T(8,128)(2,1)S(1)}, bf16[1,96,6144]{2,1,0:T(8,128)(2,1)}, u32[]{:S(2)}) copy-start(bf16[1,96,6144]{2,1,0:T(8,128)(2,1)} %get-tuple-element.64.table) | copy-start | bytes 3538948
  12.0 1.3 %copy-start.2 = (bf16[112,512]{1,0:T(8,128)(2,1)S(1)}, bf16[112,512]{1,0:T(8,128)(2,1)}, u32[]{:S(2)}) copy-start(bf16[112,512]{1,0:T(8,128)(2,1)} %weight_message.1.first) | copy-start | bytes 344068
  12.0 3.0 %copy-start.1 = (s32[64,128]{1,0:T(8,128)S(1)}, s32[64,128]{1,0:T(8,128)}, u32[]{:S(2)}) copy-start(s32[64,128]{1,0:T(8,128)} %get-tuple-element.63) | copy-start | bytes 98308
  13.3 6.9 %copy-start.3 = (bf16[4,112,256]{2,1,0:T(8,128)(2,1)S(1)}, bf16[4,112,256]{2,1,0:T(8,128)(2,1)}, u32[]{:S(2)}) copy-start(bf16[4,112,256]{2,1,0:T(8,128)(2,1)} %get-tuple-element.61.keep_ref) | copy-start | bytes 688132
  13.3 6.9 %collective-permute-start.2 = (bf16[224,512]{1,0:T(8,128)(2,1)S(1)}, bf16[224,512]{1,0:T(8,128)(2,1)S(1)}, u32[]{:S(2)}, u32[]{:S(2)}) collective-permute-start(bf16[224,512]{1,0:T(8,128)(2,1)S(1)} %join_rows.3.rest_0_), channel_id=1, source_target_pairs={{0,4},{2,6},{4,0},{6,2},{8,12},{10,14},{12,8},{14,10},{1,5},{3,7},... | collective-permute-start | bytes 688136 | tf_op jit(solution)/shard_map/ppermute | solution.py:445
  20.2 16.0 %collective-permute-start.4 = (bf16[448,512]{1,0:T(8,128)(2,1)S(1)}, bf16[448,512]{1,0:T(8,128)(2,1)S(1)}, u32[]{:S(2)}, u32[]{:S(2)}) collective-permute-start(bf16[448,512]{1,0:T(8,128)(2,1)S(1)} %get-tuple-element.88.near_ref.near), channel_id=1, source_target_pairs={{0,2},{2,0},{4,6},{6,4},{8,10},{10,8},{12,14},{14,12},{1,3},{3,1},... | collective-permute-start | bytes 1376264 | tf_op jit(solution)/shard_map/ppermute | solution.py:445
  20.8 15.4 %collective-permute-start.5 = (bf16[224,256]{1,0:T(8,128)(2,1)S(1)}, bf16[224,256]{1,0:T(8,128)(2,1)S(1)}, u32[]{:S(2)}, u32[]{:S(2)}) collective-permute-start(bf16[224,256]{1,0:T(8,128)(2,1)S(1)} %get-tuple-element.80), channel_id=1, source_target_pairs={{0,4},{2,6},{4,8},{6,10},{8,12},{10,14},{12,0},{14,2},{1,5},{3,7},... | collective-permute-start | bytes 344072 | tf_op jit(solution)/shard_map/ppermute | solution.py:441
  22.4 13.9 %collective-permute-start.6 = (bf16[224,256]{1,0:T(8,128)(2,1)S(1)}, bf16[224,256]{1,0:T(8,128)(2,1)S(1)}, u32[]{:S(2)}, u32[]{:S(2)}) collective-permute-start(bf16[224,256]{1,0:T(8,128)(2,1)S(1)} %get-tuple-element.81), channel_id=1, source_target_pairs={{0,8},{2,10},{4,12},{6,14},{8,0},{10,2},{12,4},{14,6},{1,9},{3,11}... | collective-permute-start | bytes 344072 | tf_op jit(solution)/shard_map/ppermute | solution.py:441
  25.5 10.7 %collective-permute-start.7 = (bf16[224,256]{1,0:T(8,128)(2,1)S(1)}, bf16[224,256]{1,0:T(8,128)(2,1)S(1)}, u32[]{:S(2)}, u32[]{:S(2)}) collective-permute-start(bf16[224,256]{1,0:T(8,128)(2,1)S(1)} %get-tuple-element.82), channel_id=1, source_target_pairs={{0,12},{2,14},{4,0},{6,2},{8,4},{10,6},{12,8},{14,10},{1,13},{3,15... | collective-permute-start | bytes 344072 | tf_op jit(solution)/shard_map/ppermute | solution.py:441
  26.7 6.5 %collective-permute-start.3 = (bf16[2,96,256]{2,1,0:T(8,128)(2,1)S(1)}, bf16[2,96,256]{2,1,0:T(8,128)(2,1)S(1)}, u32[]{:S(2)}, u32[]{:S(2)}) collective-permute-start(bf16[2,96,256]{2,1,0:T(8,128)(2,1)S(1)} %gather_means.4), channel_id=1, source_target_pairs={{0,2},{2,0},{4,6},{6,4},{8,10},{10,8},{12,14},{14,12},{1,3},{3,1},... | collective-permute-start | bytes 294920 | tf_op jit(solution)/shard_map/ppermute | solution.py:445
  36.2 9.8 %collective-permute-start.8 = (bf16[448,512]{1,0:T(8,128)(2,1)S(1)}, bf16[448,512]{1,0:T(8,128)(2,1)S(1)}, u32[]{:S(2)}, u32[]{:S(2)}) collective-permute-start(bf16[448,512]{1,0:T(8,128)(2,1)S(1)} %get-tuple-element.88.near_ref.near), channel_id=1, source_target_pairs={{0,1},{1,0},{2,3},{3,2},{4,5},{5,4},{6,7},{7,6},{8,9},{9,8},{10,11... | collective-permute-start | bytes 1376264 | tf_op jit(solution)/shard_map/ppermute | solution.py:437
  36.3 9.7 %collective-permute-start.9 = (bf16[448,512]{1,0:T(8,128)(2,1)S(1)}, bf16[448,512]{1,0:T(8,128)(2,1)S(1)}, u32[]{:S(2)}, u32[]{:S(2)}) collective-permute-start(bf16[448,512]{1,0:T(8,128)(2,1)S(1)} %collective-permute-done.4.far_ref.far), channel_id=1, source_target_pairs={{0,1},{1,0},{2,3},{3,2},{4,5},{5,4},{6,7},{7,6},{8,9},{9,8},{10,11... | collective-permute-start | bytes 1376264 | tf_op jit(solution)/shard_map/ppermute | solution.py:437
  36.8 9.2 %collective-permute-start.10 = (bf16[2,96,256]{2,1,0:T(8,128)(2,1)S(1)}, bf16[2,96,256]{2,1,0:T(8,128)(2,1)S(1)}, u32[]{:S(2)}, u32[]{:S(2)}) collective-permute-start(bf16[2,96,256]{2,1,0:T(8,128)(2,1)S(1)} %gather_means.5), channel_id=1, source_target_pairs={{0,2},{2,0},{4,6},{6,4},{8,10},{10,8},{12,14},{14,12},{1,3},{3,1},... | collective-permute-start | bytes 294920 | tf_op jit(solution)/shard_map/ppermute | solution.py:445
  37.3 14.4 %copy-start.7 = (s32[1,256]{1,0:T(1,128)S(1)}, s32[1,256]{1,0:T(1,128)}, u32[]{:S(2)}) copy-start(s32[1,256]{1,0:T(1,128)} %seed_degree_ref.3) | copy-start | bytes 3076
  37.3 14.9 %copy-start.4 = (bf16[512,153]{0,1:T(8,128)(2,1)S(1)}, bf16[512,153]{0,1:T(8,128)(2,1)}, u32[]{:S(2)}) copy-start(bf16[512,153]{0,1:T(8,128)(2,1)} %param.19) | copy-start | bytes 470020
  37.3 14.9 %copy-start.5 = (bf16[512,153]{0,1:T(8,128)(2,1)S(1)}, bf16[512,153]{0,1:T(8,128)(2,1)}, u32[]{:S(2)}) copy-start(bf16[512,153]{0,1:T(8,128)(2,1)} %param.20) | copy-start | bytes 470020
  37.3 14.9 %copy-start.6 = (bf16[1,32,153]{2,1,0:T(8,128)(2,1)S(1)}, bf16[1,32,153]{2,1,0:T(8,128)(2,1)}, u32[]{:S(2)}) copy-start(bf16[1,32,153]{2,1,0:T(8,128)(2,1)} %cot_ref.3) | copy-start | bytes 29380
  37.3 10.3 %collective-permute-start.11 = (bf16[192,256]{1,0:T(8,128)(2,1)S(1)}, bf16[192,256]{1,0:T(8,128)(2,1)S(1)}, u32[]{:S(2)}, u32[]{:S(2)}) collective-permute-start(bf16[192,256]{1,0:T(8,128)(2,1)S(1)} %get-tuple-element.93), channel_id=1, source_target_pairs={{0,4},{2,6},{4,8},{6,10},{8,12},{10,14},{12,0},{14,2},{1,5},{3,7},... | collective-permute-start | bytes 294920 | tf_op jit(solution)/shard_map/ppermute | solution.py:441
  42.0 9.7 %collective-permute-start.12 = (bf16[192,256]{1,0:T(8,128)(2,1)S(1)}, bf16[192,256]{1,0:T(8,128)(2,1)S(1)}, u32[]{:S(2)}, u32[]{:S(2)}) collective-permute-start(bf16[192,256]{1,0:T(8,128)(2,1)S(1)} %get-tuple-element.94), channel_id=1, source_target_pairs={{0,8},{2,10},{4,12},{6,14},{8,0},{10,2},{12,4},{14,6},{1,9},{3,11}... | collective-permute-start | bytes 294920 | tf_op jit(solution)/shard_map/ppermute | solution.py:441
  46.1 5.6 %collective-permute-start.13 = (bf16[192,256]{1,0:T(8,128)(2,1)S(1)}, bf16[192,256]{1,0:T(8,128)(2,1)S(1)}, u32[]{:S(2)}, u32[]{:S(2)}) collective-permute-start(bf16[192,256]{1,0:T(8,128)(2,1)S(1)} %get-tuple-element.95), channel_id=1, source_target_pairs={{0,12},{2,14},{4,0},{6,2},{8,4},{10,6},{12,8},{14,10},{1,13},{3,15... | collective-permute-start | bytes 294920 | tf_op jit(solution)/shard_map/ppermute | solution.py:441
  52.1 3.9 %collective-permute-start.14 = (bf16[768,384]{1,0:T(8,128)(2,1)S(1)}, bf16[768,384]{1,0:T(8,128)(2,1)S(1)}, u32[]{:S(2)}, u32[]{:S(2)}) collective-permute-start(bf16[768,384]{1,0:T(8,128)(2,1)S(1)} %get-tuple-element.101), channel_id=1, source_target_pairs={{0,1},{1,0},{2,3},{3,2},{4,5},{5,4},{6,7},{7,6},{8,9},{9,8},{10,11... | collective-permute-start | bytes 1769480 | tf_op jit(solution)/shard_map/ppermute | solution.py:437
  54.1 1.9 %collective-permute-start.15 = (bf16[384,512]{1,0:T(8,128)(2,1)S(1)}, bf16[384,512]{1,0:T(8,128)(2,1)S(1)}, u32[]{:S(2)}, u32[]{:S(2)}) collective-permute-start(bf16[384,512]{1,0:T(8,128)(2,1)S(1)} %get-tuple-element.102.dpre_ref), channel_id=1, source_target_pairs={{0,1},{1,0},{2,3},{3,2},{4,5},{5,4},{6,7},{7,6},{8,9},{9,8},{10,11... | collective-permute-start | bytes 1179656 | tf_op jit(solution)/shard_map/ppermute | solution.py:437
  54.6 1.4 %collective-permute-start.16 = (bf16[2,32,512]{2,1,0:T(8,128)(2,1)S(1)}, bf16[2,32,512]{2,1,0:T(8,128)(2,1)S(1)}, u32[]{:S(2)}, u32[]{:S(2)}) collective-permute-start(bf16[2,32,512]{2,1,0:T(8,128)(2,1)S(1)} %get-tuple-element.103.hid_ref), channel_id=1, source_target_pairs={{0,1},{1,0},{2,3},{3,2},{4,5},{5,4},{6,7},{7,6},{8,9},{9,8},{10,11... | collective-permute-start | bytes 196616 | tf_op jit(solution)/shard_map/ppermute | solution.py:437
  57.0 13.8 %collective-permute-start.17 = (bf16[4,96,512]{2,1,0:T(8,128)(2,1)S(1)}, bf16[4,96,512]{2,1,0:T(8,128)(2,1)S(1)}, u32[]{:S(2)}, u32[]{:S(2)}) collective-permute-start(bf16[4,96,512]{2,1,0:T(8,128)(2,1)S(1)} %get-tuple-element.105), channel_id=1, source_target_pairs={{0,2},{2,0},{4,6},{6,4},{8,10},{10,8},{12,14},{14,12},{1,3},{3,1},... | collective-permute-start | bytes 1179656 | tf_op jit(solution)/shard_map/ppermute | solution.py:445
  57.6 6.6 %collective-permute-start.18 = (bf16[64,512]{1,0:T(8,128)(2,1)S(1)}, bf16[64,512]{1,0:T(8,128)(2,1)S(1)}, u32[]{:S(2)}, u32[]{:S(2)}) collective-permute-start(bf16[64,512]{1,0:T(8,128)(2,1)S(1)} %get-tuple-element.107.first), channel_id=1, source_target_pairs={{0,8},{2,10},{4,12},{6,14},{8,0},{10,2},{12,4},{14,6},{1,9},{3,11}... | collective-permute-start | bytes 196616 | tf_op jit(solution)/shard_map/ppermute | solution.py:445
  64.2 5.0 %collective-permute-start.19 = (bf16[128,512]{1,0:T(8,128)(2,1)S(1)}, bf16[128,512]{1,0:T(8,128)(2,1)S(1)}, u32[]{:S(2)}, u32[]{:S(2)}) collective-permute-start(bf16[128,512]{1,0:T(8,128)(2,1)S(1)} %join_rows.4.first), channel_id=1, source_target_pairs={{0,4},{2,6},{4,0},{6,2},{8,12},{10,14},{12,8},{14,10},{1,5},{3,7},... | collective-permute-start | bytes 393224 | tf_op jit(solution)/shard_map/ppermute | solution.py:445
  69.2 6.4 %collective-permute-start.20 = (bf16[256,512]{1,0:T(8,128)(2,1)S(1)}, bf16[256,512]{1,0:T(8,128)(2,1)S(1)}, u32[]{:S(2)}, u32[]{:S(2)}) collective-permute-start(bf16[256,512]{1,0:T(8,128)(2,1)S(1)} %join_rows.5.hid_near), channel_id=1, source_target_pairs={{0,2},{2,0},{4,6},{6,4},{8,10},{10,8},{12,14},{14,12},{1,3},{3,1},... | collective-permute-start | bytes 786440 | tf_op jit(solution)/shard_map/ppermute | solution.py:445
  70.9 6.2 %collective-permute-start.21 = (bf16[96,512]{1,0:T(8,128)(2,1)S(1)}, bf16[96,512]{1,0:T(8,128)(2,1)S(1)}, u32[]{:S(2)}, u32[]{:S(2)}) collective-permute-start(bf16[96,512]{1,0:T(8,128)(2,1)S(1)} %get-tuple-element.108), channel_id=1, source_target_pairs={{0,12},{2,14},{4,0},{6,2},{8,4},{10,6},{12,8},{14,10},{1,13},{3,15... | collective-permute-start | bytes 294920 | tf_op jit(solution)/shard_map/ppermute | solution.py:441
  73.1 7.9 %collective-permute-start.22 = (bf16[96,512]{1,0:T(8,128)(2,1)S(1)}, bf16[96,512]{1,0:T(8,128)(2,1)S(1)}, u32[]{:S(2)}, u32[]{:S(2)}) collective-permute-start(bf16[96,512]{1,0:T(8,128)(2,1)S(1)} %get-tuple-element.109), channel_id=1, source_target_pairs={{0,8},{2,10},{4,12},{6,14},{8,0},{10,2},{12,4},{14,6},{1,9},{3,11}... | collective-permute-start | bytes 294920 | tf_op jit(solution)/shard_map/ppermute | solution.py:441
  73.1 7.9 %collective-permute-start.23 = (bf16[96,512]{1,0:T(8,128)(2,1)S(1)}, bf16[96,512]{1,0:T(8,128)(2,1)S(1)}, u32[]{:S(2)}, u32[]{:S(2)}) collective-permute-start(bf16[96,512]{1,0:T(8,128)(2,1)S(1)} %get-tuple-element.110), channel_id=1, source_target_pairs={{0,4},{2,6},{4,8},{6,10},{8,12},{10,14},{12,0},{14,2},{1,5},{3,7},... | collective-permute-start | bytes 294920 | tf_op jit(solution)/shard_map/ppermute | solution.py:441
  81.3 2.0 %collective-permute-start.25 = (f32[153,512]{1,0:T(8,128)S(1)}, f32[153,512]{1,0:T(8,128)S(1)}, u32[]{:S(2)}, u32[]{:S(2)}) collective-permute-start(f32[153,512]{1,0:T(8,128)S(1)} %get-tuple-element.112.v_mine), channel_id=1, source_target_pairs={{0,1},{1,0},{2,3},{3,2},{4,5},{5,4},{6,7},{7,6},{8,9},{9,8},{10,11... | collective-permute-start | bytes 940040 | tf_op jit(solution)/shard_map/ppermute | solution.py:437
  81.4 1.9 %collective-permute-start.24 = (f32[96,512]{1,0:T(8,128)S(1)}, f32[96,512]{1,0:T(8,128)S(1)}, u32[]{:S(2)}, u32[]{:S(2)}) collective-permute-start(f32[96,512]{1,0:T(8,128)S(1)} %get-tuple-element.111.w_mine), channel_id=1, source_target_pairs={{0,1},{1,0},{2,3},{3,2},{4,5},{5,4},{6,7},{7,6},{8,9},{9,8},{10,11... | collective-permute-start | bytes 589832 | tf_op jit(solution)/shard_map/ppermute | solution.py:437

commit v5 on v4

--- a/solution.py
+++ b/solution.py
@@ -575,26 +575,27 @@
     early, late = order[: pairs // 2], order[pairs // 2 :]
     early_passed = gather(True, early, live)
     passed, early_passed = lax.optimization_barrier((passed, early_passed))
-    *merged, near = merge(keep, passed, pieces)
+    merged = merge(keep, passed)
     merged[0], live = lax.optimization_barrier((merged[0], live))
     own_blocks = along(merged, 1, range(pairs))
-    far = across(near, 1, owners)
     early_passed = across(early_passed, 1, owners)
     late_passed = gather(True, late, live)
     late_passed, live = lax.optimization_barrier((late_passed, live))
     late_passed = across(late_passed, 1, owners)
-    live, early_passed = lax.optimization_barrier((live, early_passed))
+    live, early_passed, *pieces = lax.optimization_barrier([live, early_passed] + pieces)
+    near = join_rows(*pieces)
+    near, live = lax.optimization_barrier((near, live))
+    far = across(near, 1, owners)
     means = gather(False, early, live)
     merged = merge(means, early_passed)
-    merged[0], live, near, far, *own_blocks = lax.optimization_barrier(
-        [merged[0], live, near, far] + own_blocks
-    )
+    merged[0], live = lax.optimization_barrier((merged[0], live))
     agg_blocks = dict(zip(early, along(merged, 1, early)))
     means = gather(False, late, live)
-    near_other, far_other = swap(near), swap(far)
-    means, near_other, far_other = lax.optimization_barrier((means, near_other, far_other))
+    means, *own_blocks = lax.optimization_barrier([means] + own_blocks)
     agg_blocks |= dict(zip(late, along(merge(means, late_passed), 1, late)))
     agg_blocks = [agg_blocks[k] for k in range(pairs)]
+    far, near, *agg_blocks = lax.optimization_barrier([far, near] + agg_blocks)
+    near_other, far_other = swap(near), swap(far)
 
     stacked = struct((depth, hops + LANES), BF16)
     own, mean, send = call(

time: 84.5 us -> 80.4 us (0.951)
  starting transfers between devices: 29.9 us -> 27.4 us
  waiting for transfers between devices: 29.7 us -> 28 us
    ppermute x10, waiting for transfers between devices: 17.5 us -> 13.3 us  [across(): return lax.ppermute(x, 'feat', [(k, k ^ mask) for k in range(owners)])]
    ppermute x9, starting transfers between devices: 16 us -> 13.4 us  [shift_by(): lax.ppermute(x, 'feat', [(k, (k + step) % owners) for k in range(owners)])]
    ppermute x9, waiting for transfers between devices: 9.33 us -> 10.6 us  [shift_by(): lax.ppermute(x, 'feat', [(k, (k + step) % owners) for k in range(owners)])]
    ppermute x7, waiting for transfers between devices: 2.81 us -> 4.11 us  [swap(): return lax.ppermute(x, 'rep', [(0, 1), (1, 0)])]
  transfers between devices with their start and end apart: 26 -> 26, of which waited for: 10 -> 11; matrix products, arithmetic and copies ran while one was open for 0% -> 0% of each run, Pallas kernels for 22% -> 23%
where the time goes in v5:
time: 80.4 us; the launch traced here: 80.2 us
  waiting for transfers between devices  28 us (35%)
  starting transfers between devices  27.4 us (34%)
  Pallas kernels  22.5 us (28%)
  local copies, waits for them, and re-layouts  1.31 us (2%)
  between operations  0.91 us (1%)
    ppermute x9, starting transfers between devices, shift_by(): lax.ppermute(x, 'feat', [(k, (k + step) % owners) for k in range(owners)])  13.4 us
    ppermute x10, waiting for transfers between devices, across(): return lax.ppermute(x, 'feat', [(k, k ^ mask) for k in range(owners)])  13.3 us
    ppermute x10, starting transfers between devices, across(): return lax.ppermute(x, 'feat', [(k, k ^ mask) for k in range(owners)])  12.3 us
    pallas_call x4, Pallas kernels, gather(): call(functools.partial(gather_means, (owners, seeds, fan, f, fp), across_...  12.1 us
    ppermute x9, waiting for transfers between devices, shift_by(): lax.ppermute(x, 'feat', [(k, (k + step) % owners) for k in range(owners)])  10.6 us
    ppermute x7, waiting for transfers between devices, swap(): return lax.ppermute(x, 'rep', [(0, 1), (1, 0)])  4.11 us
    pallas_call x1, Pallas kernels, on_device(): call(functools.partial(pack_features, (owners, seeds, fan, f, fp, nodes))...  2.8 us
    pallas_call x1, Pallas kernels, on_device(): call(functools.partial(forward, (owners, seeds, fan, fp, width, offsets_o...  1.88 us
  transfers between devices with their start and end apart: 26, of which 11 were waited for; matrix products, arithmetic and copies ran while one was open for 0% of the time, Pallas kernels for 23%

profile of v5, /device:TPU:0, one launch (start us, length us, event | category | flops | bytes accessed | tf_op | source)
XLA Modules:
  0.0 80.2 jit_solution(14768679691306055057)
XLA Ops:
  0.6 1.6 %weight_message.1.first = bf16[112,512]{1,0:T(8,128)(2,1)} custom-call(bf16[96,512]{1,0:T(8,128)(2,1)} %ws_ref.1, bf16[96,512]{1,0:T(8,128)(2,1)} %wn_ref.1, bf16[1,32,153]{2,1,0:T(8,128)(2,1)} %cot_ref.3), custom_call_target="tpu_custom_call" | custom-call | bytes 3000000 | tf_op jit(solution)/shard_map/weight_message/pallas_call | solution.py:496
  2.2 4.1 %collective-permute-start.1 = (bf16[112,512]{1,0:T(8,128)(2,1)}, bf16[112,512]{1,0:T(8,128)(2,1)S(1)}, u32[]{:S(2)}, u32[]{:S(2)}) collective-permute-start(bf16[112,512]{1,0:T(8,128)(2,1)} %weight_message.1.first), channel_id=1, source_target_pairs={{0,8},{2,10},{4,12},{6,14},{8,0},{10,2},{12,4},{14,6},{1,9},{3,11}... | collective-permute-start | bytes 344072 | tf_op jit(solution)/shard_map/ppermute | solution.py:445
  6.3 2.8 %pack_features.1 = (bf16[4,112,256]{2,1,0:T(8,128)(2,1)}, bf16[4,112,256]{2,1,0:T(8,128)(2,1)}, s32[64,128]{1,0:T(8,128)}, bf16[1,96,6144]{2,1,0:T(8,128)(2,1)}) custom-call(s32[1,4,8,256]{3,2,1,0:T(8,128)} %idx_ref.1, s32[1,8,256]{2,1,0:T(8,128)} %deg_ref.1, bf16[1,96,8,256]{3,2,1,0:T(8,128)(2,1)} %hop_ref.1, bf16[1,96,256]{2,1,0:T(8,128)(2,1)} %seed_ref.1, ...), custom_call_target="tpu_custom_call" | custom-call | bytes 3000000 | tf_op jit(solution)/shard_map/pack_features/pallas_call | solution.py:509
  9.1 1.6 %collective-permute-start = (bf16[4,112,256]{2,1,0:T(8,128)(2,1)}, bf16[4,112,256]{2,1,0:T(8,128)(2,1)S(1)}, u32[]{:S(2)}, u32[]{:S(2)}) collective-permute-start(bf16[4,112,256]{2,1,0:T(8,128)(2,1)} %get-tuple-element.67), channel_id=1, source_target_pairs={{0,2},{2,0},{4,6},{6,4},{8,10},{10,8},{12,14},{14,12},{1,3},{3,1},... | collective-permute-start | bytes 688136 | tf_op jit(solution)/shard_map/ppermute | solution.py:445
  10.7 1.3 %copy-done = bf16[1,96,6144]{2,1,0:T(8,128)(2,1)S(1)} copy-done((bf16[1,96,6144]{2,1,0:T(8,128)(2,1)S(1)}, bf16[1,96,6144]{2,1,0:T(8,128)(2,1)}, u32[]{:S(2)}) %copy-start) | copy-done | bytes 1179672
  12.0 1.2 %turn_table.1.rows = f32[6152,128]{1,0:T(8,128)S(1)} custom-call(bf16[1,96,6144]{2,1,0:T(8,128)(2,1)S(1)} %copy-done), custom_call_target="tpu_custom_call" | custom-call | bytes 3000000 | tf_op jit(solution)/shard_map/turn_table/pallas_call | solution.py:531
  13.2 0.0 collective-permute-done.1.second
  13.3 0.0 copy-start.3
  13.3 1.6 %collective-permute-start.3 = (bf16[224,512]{1,0:T(8,128)(2,1)S(1)}, bf16[224,512]{1,0:T(8,128)(2,1)S(1)}, u32[]{:S(2)}, u32[]{:S(2)}) collective-permute-start(bf16[224,512]{1,0:T(8,128)(2,1)S(1)} %join_rows.4.first), channel_id=1, source_target_pairs={{0,4},{2,6},{4,0},{6,2},{8,12},{10,14},{12,8},{14,10},{1,5},{3,7},... | collective-permute-start | bytes 688136 | tf_op jit(solution)/shard_map/ppermute | solution.py:445
  14.9 3.0 %gather_means.4 = bf16[2,96,256]{2,1,0:T(8,128)(2,1)S(1)} custom-call(s32[8192]{0:T(1024)S(1)} %bitcast.5, f32[6152,128]{1,0:T(8,128)S(1)} %turn_table.1.rows), custom_call_target="tpu_custom_call" | custom-call | bytes 3000000 | tf_op jit(solution)/shard_map/gather_means/pallas_call | solution.py:550
  18.0 0.6 collective-permute-start.2
  18.6 3.0 %gather_means.5 = bf16[2,96,256]{2,1,0:T(8,128)(2,1)S(1)} custom-call(s32[8192]{0:T(1024)S(1)} %bitcast.6, f32[6152,128]{1,0:T(8,128)S(1)} %turn_table.1.rows), custom_call_target="tpu_custom_call" | custom-call | bytes 3000000 | tf_op jit(solution)/shard_map/gather_means/pallas_call | solution.py:550
  21.6 1.0 %collective-permute-done.2.pass_ref = bf16[2,96,256]{2,1,0:T(8,128)(2,1)S(1)} collective-permute-done((bf16[2,96,256]{2,1,0:T(8,128)(2,1)S(1)}, bf16[2,96,256]{2,1,0:T(8,128)(2,1)S(1)}, u32[]{:S(2)}, u32[]{:S(2)}) %collective-permute-start.2) | collective-permute-done | bytes 98336 | tf_op jit(solution)/shard_map/ppermute | solution.py:445
  22.7 0.6 collective-permute-start.7
  23.3 1.0 %collective-permute-start.4 = (bf16[224,256]{1,0:T(8,128)(2,1)S(1)}, bf16[224,256]{1,0:T(8,128)(2,1)S(1)}, u32[]{:S(2)}, u32[]{:S(2)}) collective-permute-start(bf16[224,256]{1,0:T(8,128)(2,1)S(1)} %get-tuple-element.88), channel_id=1, source_target_pairs={{0,4},{2,6},{4,8},{6,10},{8,12},{10,14},{12,0},{14,2},{1,5},{3,7},... | collective-permute-start | bytes 344072 | tf_op jit(solution)/shard_map/ppermute | solution.py:441
  24.3 1.5 %collective-permute-start.5 = (bf16[224,256]{1,0:T(8,128)(2,1)S(1)}, bf16[224,256]{1,0:T(8,128)(2,1)S(1)}, u32[]{:S(2)}, u32[]{:S(2)}) collective-permute-start(bf16[224,256]{1,0:T(8,128)(2,1)S(1)} %get-tuple-element.89), channel_id=1, source_target_pairs={{0,8},{2,10},{4,12},{6,14},{8,0},{10,2},{12,4},{14,6},{1,9},{3,11}... | collective-permute-start | bytes 344072 | tf_op jit(solution)/shard_map/ppermute | solution.py:441
  25.8 2.8 %collective-permute-start.6 = (bf16[224,256]{1,0:T(8,128)(2,1)S(1)}, bf16[224,256]{1,0:T(8,128)(2,1)S(1)}, u32[]{:S(2)}, u32[]{:S(2)}) collective-permute-start(bf16[224,256]{1,0:T(8,128)(2,1)S(1)} %get-tuple-element.90), channel_id=1, source_target_pairs={{0,12},{2,14},{4,0},{6,2},{8,4},{10,6},{12,8},{14,10},{1,13},{3,15... | collective-permute-start | bytes 344072 | tf_op jit(solution)/shard_map/ppermute | solution.py:441
  28.6 0.5 collective-permute-start.8
  29.1 3.0 %gather_means.6.keep_ref = bf16[2,96,256]{2,1,0:T(8,128)(2,1)S(1)} custom-call(s32[8192]{0:T(1024)S(1)} %bitcast.7, f32[6152,128]{1,0:T(8,128)S(1)} %turn_table.1.rows), custom_call_target="tpu_custom_call" | custom-call | bytes 3000000 | tf_op jit(solution)/shard_map/gather_means/pallas_call | solution.py:550
  32.2 0.0 copy-start.7
  32.2 0.0 copy-start.4
  32.2 0.0 copy-start.5
  32.2 0.0 copy-start.6
  32.2 3.0 %gather_means.7.keep_ref = bf16[2,96,256]{2,1,0:T(8,128)(2,1)S(1)} custom-call(s32[8192]{0:T(1024)S(1)} %bitcast.8, f32[6152,128]{1,0:T(8,128)S(1)} %turn_table.1.rows), custom_call_target="tpu_custom_call" | custom-call | bytes 3000000 | tf_op jit(solution)/shard_map/gather_means/pallas_call | solution.py:550
  35.2 0.0 collective-permute-done.4.rest_1_
  35.3 0.0 collective-permute-done.5.rest_2_
  35.3 0.0 collective-permute-done.8.pass_ref
  35.3 2.6 %collective-permute-start.11 = (bf16[192,256]{1,0:T(8,128)(2,1)S(1)}, bf16[192,256]{1,0:T(8,128)(2,1)S(1)}, u32[]{:S(2)}, u32[]{:S(2)}) collective-permute-start(bf16[192,256]{1,0:T(8,128)(2,1)S(1)} %get-tuple-element.101), channel_id=1, source_target_pairs={{0,12},{2,14},{4,0},{6,2},{8,4},{10,6},{12,8},{14,10},{1,13},{3,15... | collective-permute-start | bytes 294920 | tf_op jit(solution)/shard_map/ppermute | solution.py:441
  37.9 0.3 collective-permute-start.10
  38.3 1.9 %collective-permute-start.9 = (bf16[192,256]{1,0:T(8,128)(2,1)S(1)}, bf16[192,256]{1,0:T(8,128)(2,1)S(1)}, u32[]{:S(2)}, u32[]{:S(2)}) collective-permute-start(bf16[192,256]{1,0:T(8,128)(2,1)S(1)} %get-tuple-element.99), channel_id=1, source_target_pairs={{0,4},{2,6},{4,8},{6,10},{8,12},{10,14},{12,0},{14,2},{1,5},{3,7},... | collective-permute-start | bytes 294920 | tf_op jit(solution)/shard_map/ppermute | solution.py:441
  40.2 0.8 collective-permute-done.11.rest_7_
  41.0 6.1 %collective-permute-done.10.rest_6_ = bf16[192,256]{1,0:T(8,128)(2,1)S(1)} collective-permute-done((bf16[192,256]{1,0:T(8,128)(2,1)S(1)}, bf16[192,256]{1,0:T(8,128)(2,1)S(1)}, u32[]{:S(2)}, u32[]{:S(2)}) %collective-permute-start.10) | collective-permute-done | bytes 98336 | tf_op jit(solution)/shard_map/ppermute | solution.py:441
  47.1 0.0 collective-permute-done.9.rest_5_
  47.1 0.0 collective-permute-done.7.far_ref.far
  47.1 0.0 collective-permute-start.12
  47.1 0.5 collective-permute-start.13
  47.6 0.4 stack_features.1
  48.1 0.1 collective-permute-start.14
  48.2 0.7 collective-permute-done.12.near_other_ref.near_other
  49.0 0.7 collective-permute-done.13.far_other_ref.far_other
  49.6 1.9 %forward.1 = (bf16[1,32,153]{2,1,0:T(8,128)(2,1)}, bf16[2,32,512]{2,1,0:T(8,128)(2,1)S(1)}, bf16[384,512]{1,0:T(8,128)(2,1)S(1)}) custom-call(s32[1,256]{1,0:T(1,128)S(1)} %copy-done.7, bf16[768,384]{1,0:T(8,128)(2,1)S(1)} %get-tuple-element.106.own_ref, bf16[768,384]{1,0:T(8,128)(2,1)S(1)} %get-tuple-element.107.mean_ref, ...), custom_call_target="tpu_custom_call" | custom-call | bytes 9000000 | tf_op jit(solution)/shard_map/forward/pallas_call | solution.py:608
  51.5 0.1 collective-permute-start.15
  51.6 0.4 collective-permute-start.16
  52.0 1.3 %collective-permute-done.16.hid_other_ref = bf16[2,32,512]{2,1,0:T(8,128)(2,1)S(1)} collective-permute-done((bf16[2,32,512]{2,1,0:T(8,128)(2,1)S(1)}, bf16[2,32,512]{2,1,0:T(8,128)(2,1)S(1)}, u32[]{:S(2)}, u32[]{:S(2)}) %collective-permute-start.16) | collective-permute-done | bytes 65568 | tf_op jit(solution)/shard_map/ppermute | solution.py:437
  53.3 1.0 %products.1 = (f32[4,96,512]{2,1,0:T(8,128)S(1)}, bf16[4,96,512]{2,1,0:T(8,128)(2,1)S(1)}, bf16[64,512]{1,0:T(8,128)(2,1)S(1)}) custom-call(bf16[768,384]{1,0:T(8,128)(2,1)S(1)} %get-tuple-element.106.own_ref, bf16[768,384]{1,0:T(8,128)(2,1)S(1)} %get-tuple-element.107.mean_ref, bf16[768,384]{1,0:T(8,128)(2,1)S(1)} %collective-permute-done.14.x_ref, ...), custom_call_target="tpu_custom_call" | custom-call | bytes 6000000 | tf_op jit(solution)/shard_map/products/pallas_call | solution.py:631
  54.3 0.1 collective-permute-start.17
  54.4 1.7 %collective-permute-start.18 = (bf16[64,512]{1,0:T(8,128)(2,1)S(1)}, bf16[64,512]{1,0:T(8,128)(2,1)S(1)}, u32[]{:S(2)}, u32[]{:S(2)}) collective-permute-start(bf16[64,512]{1,0:T(8,128)(2,1)S(1)} %get-tuple-element.117.first), channel_id=1, source_target_pairs={{0,8},{2,10},{4,12},{6,14},{8,0},{10,2},{12,4},{14,6},{1,9},{3,11}... | collective-permute-start | bytes 196616 | tf_op jit(solution)/shard_map/ppermute | solution.py:445
  56.1 4.1 %collective-permute-done.18.second = bf16[64,512]{1,0:T(8,128)(2,1)S(1)} collective-permute-done((bf16[64,512]{1,0:T(8,128)(2,1)S(1)}, bf16[64,512]{1,0:T(8,128)(2,1)S(1)}, u32[]{:S(2)}, u32[]{:S(2)}) %collective-permute-start.18) | collective-permute-done | bytes 65568 | tf_op jit(solution)/shard_map/ppermute | solution.py:445
  60.2 0.1 collective-permute-start.19
  60.3 5.4 %collective-permute-done.19.second = bf16[128,512]{1,0:T(8,128)(2,1)S(1)} collective-permute-done((bf16[128,512]{1,0:T(8,128)(2,1)S(1)}, bf16[128,512]{1,0:T(8,128)(2,1)S(1)}, u32[]{:S(2)}, u32[]{:S(2)}) %collective-permute-start.19) | collective-permute-done | bytes 131104 | tf_op jit(solution)/shard_map/ppermute | solution.py:445
  65.7 1.4 %collective-permute-start.20 = (bf16[256,512]{1,0:T(8,128)(2,1)S(1)}, bf16[256,512]{1,0:T(8,128)(2,1)S(1)}, u32[]{:S(2)}, u32[]{:S(2)}) collective-permute-start(bf16[256,512]{1,0:T(8,128)(2,1)S(1)} %join_rows.7.hid_near), channel_id=1, source_target_pairs={{0,2},{2,0},{4,6},{6,4},{8,10},{10,8},{12,14},{14,12},{1,3},{3,1},... | collective-permute-start | bytes 786440 | tf_op jit(solution)/shard_map/ppermute | solution.py:445
  67.1 0.0 collective-permute-done.17.passed_ref
  67.1 0.1 join_pairs.1
  67.2 1.2 %collective-permute-start.21 = (bf16[96,512]{1,0:T(8,128)(2,1)S(1)}, bf16[96,512]{1,0:T(8,128)(2,1)S(1)}, u32[]{:S(2)}, u32[]{:S(2)}) collective-permute-start(bf16[96,512]{1,0:T(8,128)(2,1)S(1)} %get-tuple-element.118), channel_id=1, source_target_pairs={{0,12},{2,14},{4,0},{6,2},{8,4},{10,6},{12,8},{14,10},{1,13},{3,15... | collective-permute-start | bytes 294920 | tf_op jit(solution)/shard_map/ppermute | solution.py:441
  68.4 0.6 collective-permute-start.22
  69.0 1.3 %collective-permute-start.23 = (bf16[96,512]{1,0:T(8,128)(2,1)S(1)}, bf16[96,512]{1,0:T(8,128)(2,1)S(1)}, u32[]{:S(2)}, u32[]{:S(2)}) collective-permute-start(bf16[96,512]{1,0:T(8,128)(2,1)S(1)} %get-tuple-element.120), channel_id=1, source_target_pairs={{0,4},{2,6},{4,8},{6,10},{8,12},{10,14},{12,0},{14,2},{1,5},{3,7},... | collective-permute-start | bytes 294920 | tf_op jit(solution)/shard_map/ppermute | solution.py:441
  70.3 2.8 %collective-permute-done.20.hid_far = bf16[256,512]{1,0:T(8,128)(2,1)S(1)} collective-permute-done((bf16[256,512]{1,0:T(8,128)(2,1)S(1)}, bf16[256,512]{1,0:T(8,128)(2,1)S(1)}, u32[]{:S(2)}, u32[]{:S(2)}) %collective-permute-start.20) | collective-permute-done | bytes 262176 | tf_op jit(solution)/shard_map/ppermute | solution.py:445
  73.1 0.0 collective-permute-done.21.rest_0_
  73.1 3.7 %collective-permute-done.22.rest_1_ = bf16[96,512]{1,0:T(8,128)(2,1)S(1)} collective-permute-done((bf16[96,512]{1,0:T(8,128)(2,1)S(1)}, bf16[96,512]{1,0:T(8,128)(2,1)S(1)}, u32[]{:S(2)}, u32[]{:S(2)}) %collective-permute-start.22) | collective-permute-done | bytes 98336 | tf_op jit(solution)/shard_map/ppermute | solution.py:441
  76.8 0.3 total_gradients.1
  77.2 0.1 collective-permute-start.25
  77.2 0.5 collective-permute-start.24
  77.7 1.4 %collective-permute-done.24.w_other = f32[96,512]{1,0:T(8,128)S(1)} collective-permute-done((f32[96,512]{1,0:T(8,128)S(1)}, f32[96,512]{1,0:T(8,128)S(1)}, u32[]{:S(2)}, u32[]{:S(2)}) %collective-permute-start.24) | collective-permute-done | bytes 196640 | tf_op jit(solution)/shard_map/ppermute | solution.py:437
  79.1 1.0 %place_gradients.1 = (f32[96,512]{1,0:T(8,128)}, f32[96,512]{1,0:T(8,128)}, f32[153,512]{1,0:T(8,128)}, f32[153,512]{1,0:T(8,128)}) custom-call(f32[96,512]{1,0:T(8,128)S(1)} %get-tuple-element.121.w_mine, f32[96,512]{1,0:T(8,128)S(1)} %collective-permute-done.24.w_other, f32[153,512]{1,0:T(8,128)S(1)} %get-tuple-element.122.v_mine, ...), custom_call_target="tpu_custom_call" | custom-call | bytes 3000000 | tf_op jit(solution)/shard_map/place_gradients/pallas_call | solution.py:658
  (24 shorter events, 0.2 us)
Async XLA Ops:
  2.2 11.0 %collective-permute-start.1 = (bf16[112,512]{1,0:T(8,128)(2,1)}, bf16[112,512]{1,0:T(8,128)(2,1)S(1)}, u32[]{:S(2)}, u32[]{:S(2)}) collective-permute-start(bf16[112,512]{1,0:T(8,128)(2,1)} %weight_message.1.first), channel_id=1, source_target_pairs={{0,8},{2,10},{4,12},{6,14},{8,0},{10,2},{12,4},{14,6},{1,9},{3,11}... | collective-permute-start | bytes 344072 | tf_op jit(solution)/shard_map/ppermute | solution.py:445
  9.1 8.8 %collective-permute-start = (bf16[4,112,256]{2,1,0:T(8,128)(2,1)}, bf16[4,112,256]{2,1,0:T(8,128)(2,1)S(1)}, u32[]{:S(2)}, u32[]{:S(2)}) collective-permute-start(bf16[4,112,256]{2,1,0:T(8,128)(2,1)} %get-tuple-element.67), channel_id=1, source_target_pairs={{0,2},{2,0},{4,6},{6,4},{8,10},{10,8},{12,14},{14,12},{1,3},{3,1},... | collective-permute-start | bytes 688136 | tf_op jit(solution)/shard_map/ppermute | solution.py:445
  10.7 1.3 %copy-start = (bf16[1,96,6144]{2,1,0:T(8,128)(2,1)S(1)}, bf16[1,96,6144]{2,1,0:T(8,128)(2,1)}, u32[]{:S(2)}) copy-start(bf16[1,96,6144]{2,1,0:T(8,128)(2,1)} %get-tuple-element.69.table) | copy-start | bytes 3538948
  12.0 1.3 %copy-start.2 = (bf16[112,512]{1,0:T(8,128)(2,1)S(1)}, bf16[112,512]{1,0:T(8,128)(2,1)}, u32[]{:S(2)}) copy-start(bf16[112,512]{1,0:T(8,128)(2,1)} %weight_message.1.first) | copy-start | bytes 344068
  12.0 3.0 %copy-start.1 = (s32[64,128]{1,0:T(8,128)S(1)}, s32[64,128]{1,0:T(8,128)}, u32[]{:S(2)}) copy-start(s32[64,128]{1,0:T(8,128)} %get-tuple-element.68) | copy-start | bytes 98308
  13.3 5.3 %copy-start.3 = (bf16[4,112,256]{2,1,0:T(8,128)(2,1)S(1)}, bf16[4,112,256]{2,1,0:T(8,128)(2,1)}, u32[]{:S(2)}) copy-start(bf16[4,112,256]{2,1,0:T(8,128)(2,1)} %get-tuple-element.66.keep_ref) | copy-start | bytes 688132
  13.3 9.4 %collective-permute-start.3 = (bf16[224,512]{1,0:T(8,128)(2,1)S(1)}, bf16[224,512]{1,0:T(8,128)(2,1)S(1)}, u32[]{:S(2)}, u32[]{:S(2)}) collective-permute-start(bf16[224,512]{1,0:T(8,128)(2,1)S(1)} %join_rows.4.first), channel_id=1, source_target_pairs={{0,4},{2,6},{4,0},{6,2},{8,12},{10,14},{12,8},{14,10},{1,5},{3,7},... | collective-permute-start | bytes 688136 | tf_op jit(solution)/shard_map/ppermute | solution.py:445
  18.0 4.7 %collective-permute-start.2 = (bf16[2,96,256]{2,1,0:T(8,128)(2,1)S(1)}, bf16[2,96,256]{2,1,0:T(8,128)(2,1)S(1)}, u32[]{:S(2)}, u32[]{:S(2)}) collective-permute-start(bf16[2,96,256]{2,1,0:T(8,128)(2,1)S(1)} %gather_means.4), channel_id=1, source_target_pairs={{0,2},{2,0},{4,6},{6,4},{8,10},{10,8},{12,14},{14,12},{1,3},{3,1},... | collective-permute-start | bytes 294920 | tf_op jit(solution)/shard_map/ppermute | solution.py:445
  22.7 24.4 %collective-permute-start.7 = (bf16[448,512]{1,0:T(8,128)(2,1)S(1)}, bf16[448,512]{1,0:T(8,128)(2,1)S(1)}, u32[]{:S(2)}, u32[]{:S(2)}) collective-permute-start(bf16[448,512]{1,0:T(8,128)(2,1)S(1)} %join_rows.5.near_ref.near), channel_id=1, source_target_pairs={{0,2},{2,0},{4,6},{6,4},{8,10},{10,8},{12,14},{14,12},{1,3},{3,1},... | collective-permute-start | bytes 1376264 | tf_op jit(solution)/shard_map/ppermute | solution.py:445
  23.3 12.0 %collective-permute-start.4 = (bf16[224,256]{1,0:T(8,128)(2,1)S(1)}, bf16[224,256]{1,0:T(8,128)(2,1)S(1)}, u32[]{:S(2)}, u32[]{:S(2)}) collective-permute-start(bf16[224,256]{1,0:T(8,128)(2,1)S(1)} %get-tuple-element.88), channel_id=1, source_target_pairs={{0,4},{2,6},{4,8},{6,10},{8,12},{10,14},{12,0},{14,2},{1,5},{3,7},... | collective-permute-start | bytes 344072 | tf_op jit(solution)/shard_map/ppermute | solution.py:441
  24.3 11.0 %collective-permute-start.5 = (bf16[224,256]{1,0:T(8,128)(2,1)S(1)}, bf16[224,256]{1,0:T(8,128)(2,1)S(1)}, u32[]{:S(2)}, u32[]{:S(2)}) collective-permute-start(bf16[224,256]{1,0:T(8,128)(2,1)S(1)} %get-tuple-element.89), channel_id=1, source_target_pairs={{0,8},{2,10},{4,12},{6,14},{8,0},{10,2},{12,4},{14,6},{1,9},{3,11}... | collective-permute-start | bytes 344072 | tf_op jit(solution)/shard_map/ppermute | solution.py:441
  25.8 9.5 %collective-permute-start.6 = (bf16[224,256]{1,0:T(8,128)(2,1)S(1)}, bf16[224,256]{1,0:T(8,128)(2,1)S(1)}, u32[]{:S(2)}, u32[]{:S(2)}) collective-permute-start(bf16[224,256]{1,0:T(8,128)(2,1)S(1)} %get-tuple-element.90), channel_id=1, source_target_pairs={{0,12},{2,14},{4,0},{6,2},{8,4},{10,6},{12,8},{14,10},{1,13},{3,15... | collective-permute-start | bytes 344072 | tf_op jit(solution)/shard_map/ppermute | solution.py:441
  28.6 6.7 %collective-permute-start.8 = (bf16[2,96,256]{2,1,0:T(8,128)(2,1)S(1)}, bf16[2,96,256]{2,1,0:T(8,128)(2,1)S(1)}, u32[]{:S(2)}, u32[]{:S(2)}) collective-permute-start(bf16[2,96,256]{2,1,0:T(8,128)(2,1)S(1)} %gather_means.5), channel_id=1, source_target_pairs={{0,2},{2,0},{4,6},{6,4},{8,10},{10,8},{12,14},{14,12},{1,3},{3,1},... | collective-permute-start | bytes 294920 | tf_op jit(solution)/shard_map/ppermute | solution.py:445
  32.2 15.5 %copy-start.7 = (s32[1,256]{1,0:T(1,128)S(1)}, s32[1,256]{1,0:T(1,128)}, u32[]{:S(2)}) copy-start(s32[1,256]{1,0:T(1,128)} %seed_degree_ref.3) | copy-start | bytes 3076
  32.2 17.4 %copy-start.4 = (bf16[512,153]{0,1:T(8,128)(2,1)S(1)}, bf16[512,153]{0,1:T(8,128)(2,1)}, u32[]{:S(2)}) copy-start(bf16[512,153]{0,1:T(8,128)(2,1)} %param.19) | copy-start | bytes 470020
  32.2 17.4 %copy-start.5 = (bf16[512,153]{0,1:T(8,128)(2,1)S(1)}, bf16[512,153]{0,1:T(8,128)(2,1)}, u32[]{:S(2)}) copy-start(bf16[512,153]{0,1:T(8,128)(2,1)} %param.20) | copy-start | bytes 470020
  32.2 17.4 %copy-start.6 = (bf16[1,32,153]{2,1,0:T(8,128)(2,1)S(1)}, bf16[1,32,153]{2,1,0:T(8,128)(2,1)}, u32[]{:S(2)}) copy-start(bf16[1,32,153]{2,1,0:T(8,128)(2,1)} %cot_ref.3) | copy-start | bytes 29380
  35.3 5.7 %collective-permute-start.11 = (bf16[192,256]{1,0:T(8,128)(2,1)S(1)}, bf16[192,256]{1,0:T(8,128)(2,1)S(1)}, u32[]{:S(2)}, u32[]{:S(2)}) collective-permute-start(bf16[192,256]{1,0:T(8,128)(2,1)S(1)} %get-tuple-element.101), channel_id=1, source_target_pairs={{0,12},{2,14},{4,0},{6,2},{8,4},{10,6},{12,8},{14,10},{1,13},{3,15... | collective-permute-start | bytes 294920 | tf_op jit(solution)/shard_map/ppermute | solution.py:441
  37.9 9.2 %collective-permute-start.10 = (bf16[192,256]{1,0:T(8,128)(2,1)S(1)}, bf16[192,256]{1,0:T(8,128)(2,1)S(1)}, u32[]{:S(2)}, u32[]{:S(2)}) collective-permute-start(bf16[192,256]{1,0:T(8,128)(2,1)S(1)} %get-tuple-element.100), channel_id=1, source_target_pairs={{0,8},{2,10},{4,12},{6,14},{8,0},{10,2},{12,4},{14,6},{1,9},{3,11}... | collective-permute-start | bytes 294920 | tf_op jit(solution)/shard_map/ppermute | solution.py:441
  38.3 8.8 %collective-permute-start.9 = (bf16[192,256]{1,0:T(8,128)(2,1)S(1)}, bf16[192,256]{1,0:T(8,128)(2,1)S(1)}, u32[]{:S(2)}, u32[]{:S(2)}) collective-permute-start(bf16[192,256]{1,0:T(8,128)(2,1)S(1)} %get-tuple-element.99), channel_id=1, source_target_pairs={{0,4},{2,6},{4,8},{6,10},{8,12},{10,14},{12,0},{14,2},{1,5},{3,7},... | collective-permute-start | bytes 294920 | tf_op jit(solution)/shard_map/ppermute | solution.py:441
  47.1 1.8 %collective-permute-start.12 = (bf16[448,512]{1,0:T(8,128)(2,1)S(1)}, bf16[448,512]{1,0:T(8,128)(2,1)S(1)}, u32[]{:S(2)}, u32[]{:S(2)}) collective-permute-start(bf16[448,512]{1,0:T(8,128)(2,1)S(1)} %join_rows.5.near_ref.near), channel_id=1, source_target_pairs={{0,1},{1,0},{2,3},{3,2},{4,5},{5,4},{6,7},{7,6},{8,9},{9,8},{10,11... | collective-permute-start | bytes 1376264 | tf_op jit(solution)/shard_map/ppermute | solution.py:437
  47.1 2.5 %collective-permute-start.13 = (bf16[448,512]{1,0:T(8,128)(2,1)S(1)}, bf16[448,512]{1,0:T(8,128)(2,1)S(1)}, u32[]{:S(2)}, u32[]{:S(2)}) collective-permute-start(bf16[448,512]{1,0:T(8,128)(2,1)S(1)} %collective-permute-done.7.far_ref.far), channel_id=1, source_target_pairs={{0,1},{1,0},{2,3},{3,2},{4,5},{5,4},{6,7},{7,6},{8,9},{9,8},{10,11... | collective-permute-start | bytes 1376264 | tf_op jit(solution)/shard_map/ppermute | solution.py:437
  48.1 5.3 %collective-permute-start.14 = (bf16[768,384]{1,0:T(8,128)(2,1)S(1)}, bf16[768,384]{1,0:T(8,128)(2,1)S(1)}, u32[]{:S(2)}, u32[]{:S(2)}) collective-permute-start(bf16[768,384]{1,0:T(8,128)(2,1)S(1)} %get-tuple-element.111), channel_id=1, source_target_pairs={{0,1},{1,0},{2,3},{3,2},{4,5},{5,4},{6,7},{7,6},{8,9},{9,8},{10,11... | collective-permute-start | bytes 1769480 | tf_op jit(solution)/shard_map/ppermute | solution.py:437
  51.5 1.8 %collective-permute-start.15 = (bf16[384,512]{1,0:T(8,128)(2,1)S(1)}, bf16[384,512]{1,0:T(8,128)(2,1)S(1)}, u32[]{:S(2)}, u32[]{:S(2)}) collective-permute-start(bf16[384,512]{1,0:T(8,128)(2,1)S(1)} %get-tuple-element.112.dpre_ref), channel_id=1, source_target_pairs={{0,1},{1,0},{2,3},{3,2},{4,5},{5,4},{6,7},{7,6},{8,9},{9,8},{10,11... | collective-permute-start | bytes 1179656 | tf_op jit(solution)/shard_map/ppermute | solution.py:437
  51.6 1.7 %collective-permute-start.16 = (bf16[2,32,512]{2,1,0:T(8,128)(2,1)S(1)}, bf16[2,32,512]{2,1,0:T(8,128)(2,1)S(1)}, u32[]{:S(2)}, u32[]{:S(2)}) collective-permute-start(bf16[2,32,512]{2,1,0:T(8,128)(2,1)S(1)} %get-tuple-element.113.hid_ref), channel_id=1, source_target_pairs={{0,1},{1,0},{2,3},{3,2},{4,5},{5,4},{6,7},{7,6},{8,9},{9,8},{10,11... | collective-permute-start | bytes 196616 | tf_op jit(solution)/shard_map/ppermute | solution.py:437
  54.3 12.8 %collective-permute-start.17 = (bf16[4,96,512]{2,1,0:T(8,128)(2,1)S(1)}, bf16[4,96,512]{2,1,0:T(8,128)(2,1)S(1)}, u32[]{:S(2)}, u32[]{:S(2)}) collective-permute-start(bf16[4,96,512]{2,1,0:T(8,128)(2,1)S(1)} %get-tuple-element.115), channel_id=1, source_target_pairs={{0,2},{2,0},{4,6},{6,4},{8,10},{10,8},{12,14},{14,12},{1,3},{3,1},... | collective-permute-start | bytes 1179656 | tf_op jit(solution)/shard_map/ppermute | solution.py:445
  54.4 5.8 %collective-permute-start.18 = (bf16[64,512]{1,0:T(8,128)(2,1)S(1)}, bf16[64,512]{1,0:T(8,128)(2,1)S(1)}, u32[]{:S(2)}, u32[]{:S(2)}) collective-permute-start(bf16[64,512]{1,0:T(8,128)(2,1)S(1)} %get-tuple-element.117.first), channel_id=1, source_target_pairs={{0,8},{2,10},{4,12},{6,14},{8,0},{10,2},{12,4},{14,6},{1,9},{3,11}... | collective-permute-start | bytes 196616 | tf_op jit(solution)/shard_map/ppermute | solution.py:445
  60.2 5.5 %collective-permute-start.19 = (bf16[128,512]{1,0:T(8,128)(2,1)S(1)}, bf16[128,512]{1,0:T(8,128)(2,1)S(1)}, u32[]{:S(2)}, u32[]{:S(2)}) collective-permute-start(bf16[128,512]{1,0:T(8,128)(2,1)S(1)} %join_rows.6.first), channel_id=1, source_target_pairs={{0,4},{2,6},{4,0},{6,2},{8,12},{10,14},{12,8},{14,10},{1,5},{3,7},... | collective-permute-start | bytes 393224 | tf_op jit(solution)/shard_map/ppermute | solution.py:445
  65.7 7.4 %collective-permute-start.20 = (bf16[256,512]{1,0:T(8,128)(2,1)S(1)}, bf16[256,512]{1,0:T(8,128)(2,1)S(1)}, u32[]{:S(2)}, u32[]{:S(2)}) collective-permute-start(bf16[256,512]{1,0:T(8,128)(2,1)S(1)} %join_rows.7.hid_near), channel_id=1, source_target_pairs={{0,2},{2,0},{4,6},{6,4},{8,10},{10,8},{12,14},{14,12},{1,3},{3,1},... | collective-permute-start | bytes 786440 | tf_op jit(solution)/shard_map/ppermute | solution.py:445
  67.2 5.9 %collective-permute-start.21 = (bf16[96,512]{1,0:T(8,128)(2,1)S(1)}, bf16[96,512]{1,0:T(8,128)(2,1)S(1)}, u32[]{:S(2)}, u32[]{:S(2)}) collective-permute-start(bf16[96,512]{1,0:T(8,128)(2,1)S(1)} %get-tuple-element.118), channel_id=1, source_target_pairs={{0,12},{2,14},{4,0},{6,2},{8,4},{10,6},{12,8},{14,10},{1,13},{3,15... | collective-permute-start | bytes 294920 | tf_op jit(solution)/shard_map/ppermute | solution.py:441
  68.4 8.4 %collective-permute-start.22 = (bf16[96,512]{1,0:T(8,128)(2,1)S(1)}, bf16[96,512]{1,0:T(8,128)(2,1)S(1)}, u32[]{:S(2)}, u32[]{:S(2)}) collective-permute-start(bf16[96,512]{1,0:T(8,128)(2,1)S(1)} %get-tuple-element.119), channel_id=1, source_target_pairs={{0,8},{2,10},{4,12},{6,14},{8,0},{10,2},{12,4},{14,6},{1,9},{3,11}... | collective-permute-start | bytes 294920 | tf_op jit(solution)/shard_map/ppermute | solution.py:441
  69.0 7.8 %collective-permute-start.23 = (bf16[96,512]{1,0:T(8,128)(2,1)S(1)}, bf16[96,512]{1,0:T(8,128)(2,1)S(1)}, u32[]{:S(2)}, u32[]{:S(2)}) collective-permute-start(bf16[96,512]{1,0:T(8,128)(2,1)S(1)} %get-tuple-element.120), channel_id=1, source_target_pairs={{0,4},{2,6},{4,8},{6,10},{8,12},{10,14},{12,0},{14,2},{1,5},{3,7},... | collective-permute-start | bytes 294920 | tf_op jit(solution)/shard_map/ppermute | solution.py:441
  77.2 2.0 %collective-permute-start.25 = (f32[153,512]{1,0:T(8,128)S(1)}, f32[153,512]{1,0:T(8,128)S(1)}, u32[]{:S(2)}, u32[]{:S(2)}) collective-permute-start(f32[153,512]{1,0:T(8,128)S(1)} %get-tuple-element.122.v_mine), channel_id=1, source_target_pairs={{0,1},{1,0},{2,3},{3,2},{4,5},{5,4},{6,7},{7,6},{8,9},{9,8},{10,11... | collective-permute-start | bytes 940040 | tf_op jit(solution)/shard_map/ppermute | solution.py:437
  77.2 1.9 %collective-permute-start.24 = (f32[96,512]{1,0:T(8,128)S(1)}, f32[96,512]{1,0:T(8,128)S(1)}, u32[]{:S(2)}, u32[]{:S(2)}) collective-permute-start(f32[96,512]{1,0:T(8,128)S(1)} %get-tuple-element.121.w_mine), channel_id=1, source_target_pairs={{0,1},{1,0},{2,3},{3,2},{4,5},{5,4},{6,7},{7,6},{8,9},{9,8},{10,11... | collective-permute-start | bytes 589832 | tf_op jit(solution)/shard_map/ppermute | solution.py:437

commit v6 on v5

--- a/solution.py
+++ b/solution.py
@@ -11,7 +11,6 @@
 BF16 = jnp.bfloat16
 LANES = 128
 PACK = 56
-FIRST = 62
 VMEM = pl.BlockSpec(memory_space=pltpu.VMEM)
 SMEM = pl.BlockSpec(memory_space=pltpu.SMEM)
 HBM = pl.BlockSpec(memory_space=pltpu.HBM)
@@ -52,48 +51,15 @@
     return total
 
 
-def weight_message(sizes, ws_ref, wn_ref, cot_ref, out_ref, cot, sems):
-    seeds, f, fp, classes = sizes
-    width = out_ref.shape[1]
-    split = seeds // 16
-
-    def fetch(ref):
-        loads = (
-            pltpu.make_async_copy(ref, out_ref.at[pl.ds(0, f), :], sems.at[0]),
-            pltpu.make_async_copy(cot_ref, cot, sems.at[1]),
-        )
-        for load in loads:
-            load.start()
-        for load in loads:
-            load.wait()
-
-    @pl.when(lax.axis_index("rep") == 0)
-    def _():
-        fetch(ws_ref)
-
-    @pl.when(lax.axis_index("rep") != 0)
-    def _():
-        fetch(wn_ref)
-
-    if fp != f:
-        out_ref[f:fp, :] = jnp.zeros((fp - f, width), BF16)
-    out_ref[fp:, :] = jnp.zeros((16, width), BF16)
-    for p in range(split):
-        at = p * (width // split)
-        out_ref[fp:, at : at + classes] = cot[0, p * 16 : (p + 1) * 16, :]
-
-
 def pack_features(
     sizes,
     idx_ref,
     deg_ref,
     hop_ref,
     seed_ref,
-    table_ref,
     keep_ref,
     pass_ref,
     live_ref,
-    table,
     hop,
     packed,
     hop32,
@@ -109,18 +75,19 @@
     loads = [
         pltpu.make_async_copy(source, target, sems.at[i])
         for i, (source, target) in enumerate(
-            ((idx_ref, idx), (deg_ref, deg), (hop_ref, hop), (seed_ref, seed), (table_ref, table))
+            ((idx_ref, idx), (deg_ref, deg), (hop_ref, hop), (seed_ref, seed))
         )
     ]
     for load in loads:
         load.start()
-    for load in loads[:4]:
+    for load in loads:
         load.wait()
     tiles = owners * seeds // LANES
-    for u in range(idx.shape[1]):
+    for u in range(0, idx.shape[1], 2):
         live = jnp.where(deg[0] > u, idx[0, u], nodes)
+        live = live + (jnp.where(deg[0] > u + 1, idx[0, u + 1], nodes) << 16)
         for tile in range(tiles):
-            at = (u * tiles + tile) * fan
+            at = (u // 2 * tiles + tile) * fan
             live_ref[at : at + fan, :] = live[:, tile * LANES : (tile + 1) * LANES]
     if fp != f:
         packed[...] = jnp.zeros_like(packed)
@@ -158,7 +125,6 @@
         owner = lax.rem(lax.axis_index("feat") // 2 + j, owners // 2)
         keep_ref[j] = packed[2 * owner + side]
         pass_ref[j] = packed[2 * owner + 1 - side]
-    loads[4].wait()
 
 
 def turn_table(f, table, rows):
@@ -194,10 +160,12 @@
         def slot_step(t, _):
             src = first + t * LANES
             for k in range(seeds):
-                total = rows[pl.ds(idx[src + k], 1), :]
-                for u in range(1, slots):
-                    at = src + (u * tiles * fan * LANES + k)
-                    total = total + rows[pl.ds(idx[at], 1), :]
+                total = None
+                for u in range(slots):
+                    two = idx[src + (u * tiles * fan * LANES + k)]
+                    low = rows[pl.ds(two & 0xFFFF, 1), :]
+                    total = low if total is None else total + low
+                    total = total + rows[pl.ds(two >> 16, 1), :]
                 picked[pl.ds(t * seeds + k, 1), :] = total
             return 0
 
@@ -493,29 +461,27 @@
     depth = owners * fp
     struct = jax.ShapeDtypeStruct
 
-    message = call(
-        functools.partial(weight_message, (seeds, f, fp, classes)),
-        "weight_message",
-        struct((fp + 16, width), BF16),
-        [HBM] * 3,
-        [pltpu.VMEM(cotangent.shape, BF16), pltpu.SemaphoreType.DMA((2,))],
-        vmem=FIRST,
-    )(w_self, w_neigh, cotangent)
+    chosen = jnp.where(lax.axis_index("rep") == 0, w_self, w_neigh)
+    split = seeds // 16
+    pieces = cotangent[0].reshape(split, 16, classes)
+    pieces = jnp.pad(pieces, ((0, 0), (0, 0), (0, width // split - classes)))
+    message = jnp.concatenate(
+        [jnp.pad(chosen, ((0, fp - f), (0, 0)))] + [jnp.concatenate(list(pieces), axis=1)], axis=0
+    )
     far_mask = owners // 2
     fetched = across(message, far_mask, owners)
     lanes = up(f + 1, LANES)
     half = owners * seeds
     own_rows = fp + seed_rows
-    keep, passed, live, table = call(
+    keep, passed, live = call(
         functools.partial(pack_features, (owners, seeds, fan, f, fp, nodes)),
         "pack_features",
         (
             struct((owners // 2, own_rows, hops), BF16),
             struct((owners // 2, own_rows, hops), BF16),
-            struct((nbr_index.size // LANES, LANES), jnp.int32),
-            struct(frontier.shape, BF16),
+            struct((nbr_index.size // 2 // LANES, LANES), jnp.int32),
         ),
-        [HBM] * 5,
+        [HBM] * 4,
         [
             pltpu.VMEM(hop_feat.shape, BF16),
             pltpu.VMEM((owners, own_rows, hops), BF16),
@@ -524,16 +490,16 @@
             pltpu.VMEM((fp, half), F32),
             pltpu.VMEM(hop_degree.shape, jnp.int32),
             pltpu.VMEM(nbr_index.shape, jnp.int32),
-            pltpu.SemaphoreType.DMA((5,)),
+            pltpu.SemaphoreType.DMA((4,)),
         ],
         vmem=PACK,
-    )(nbr_index, hop_degree, hop_feat, seed_feat, frontier)
+    )(nbr_index, hop_degree, hop_feat, seed_feat)
     rows = call(
         functools.partial(turn_table, f),
         "turn_table",
         struct((nodes + 8, lanes), F32),
         [VMEM],
-    )(table)
+    )(frontier)
     live = live.reshape(-1)
     pairs = owners // 2
     passed = across(passed, 1, owners)

time: 80.4 us -> 79.5 us (0.989)
  Pallas kernels: 22.5 us -> 19.4 us
  starting transfers between devices: 27.4 us -> 28.5 us
  other arithmetic: 0 us -> 0.92 us
    pallas_call x1 -> x0, Pallas kernels: 1.57 us -> none  [on_device(): call(functools.partial(weight_message, (seeds, f, fp, classes)), 'weight_...]
    pallas_call x4, Pallas kernels: 12.1 us -> 11 us  [gather(): call(functools.partial(gather_means, (owners, seeds, fan, f, fp), across_...]
    ppermute x10, waiting for transfers between devices: 13.3 us -> 12.3 us  [across(): return lax.ppermute(x, 'feat', [(k, k ^ mask) for k in range(owners)])]
    select_n x0 -> x1, other arithmetic: none -> 0.91 us  [on_device(): chosen = jnp.where(lax.axis_index('rep') == 0, w_self, w_neigh)]
  transfers between devices with their start and end apart: 26 -> 26, of which waited for: 11 -> 12; matrix products, arithmetic and copies ran while one was open for 0% -> 0% of each run, Pallas kernels for 23% -> 21%
where the time goes in v6:
time: 79.5 us; the launch traced here: 79.2 us
  starting transfers between devices  28.5 us (36%)
  waiting for transfers between devices  27.6 us (35%)
  Pallas kernels  19.4 us (24%)
  local copies, waits for them, and re-layouts  2.02 us (3%)
  other arithmetic  0.92 us (1%)
  between operations  0.85 us (1%)
    ppermute x9, starting transfers between devices, shift_by(): lax.ppermute(x, 'feat', [(k, (k + step) % owners) for k in range(owners)])  13.7 us
    ppermute x10, starting transfers between devices, across(): return lax.ppermute(x, 'feat', [(k, k ^ mask) for k in range(owners)])  13 us
    ppermute x10, waiting for transfers between devices, across(): return lax.ppermute(x, 'feat', [(k, k ^ mask) for k in range(owners)])  12.3 us
    ppermute x9, waiting for transfers between devices, shift_by(): lax.ppermute(x, 'feat', [(k, (k + step) % owners) for k in range(owners)])  11.1 us
    pallas_call x4, Pallas kernels, gather(): call(functools.partial(gather_means, (owners, seeds, fan, f, fp), across_...  11 us
    ppermute x7, waiting for transfers between devices, swap(): return lax.ppermute(x, 'rep', [(0, 1), (1, 0)])  4.11 us
    pallas_call x1, Pallas kernels, on_device(): call(functools.partial(pack_features, (owners, seeds, fan, f, fp, nodes))...  2.34 us
    pallas_call x1, Pallas kernels, on_device(): call(functools.partial(forward, (owners, seeds, fan, fp, width, offsets_o...  1.88 us
  transfers between devices with their start and end apart: 26, of which 12 were waited for; matrix products, arithmetic and copies ran while one was open for 0% of the time, Pallas kernels for 21%

profile of v6, /device:TPU:0, one launch (start us, length us, event | category | flops | bytes accessed | tf_op | source)
XLA Modules:
  0.0 79.2 jit_solution(3563319156905662173)
XLA Ops:
  0.6 0.7 fusion
  1.4 0.9 %broadcast_select_fusion = bf16[96,512]{1,0:T(8,128)(2,1)S(1)} fusion(bf16[96,512]{1,0:T(8,128)(2,1)} %param.17, bf16[96,512]{1,0:T(8,128)(2,1)} %param.18, pred[]{:T(512)S(6)} %eq.3), kind=kLoop, calls=%fused_computation.1 | loop fusion | flops 49152 | bytes 294913 | tf_op jit(solution)/shard_map/jit(_where)/select_n | solution.py:464
  2.3 4.1 %collective-permute-start.1 = (bf16[112,512]{1,0:T(8,128)(2,1)S(1)}, bf16[112,512]{1,0:T(8,128)(2,1)S(1)}, u32[]{:S(2)}, u32[]{:S(2)}) collective-permute-start(bf16[112,512]{1,0:T(8,128)(2,1)S(1)} %maximum_maximum_fusion.first), channel_id=1, source_target_pairs={{0,8},{2,10},{4,12},{6,14},{8,0},{10,2},{12,4},{14,6},{1,9},{3,11}... | collective-permute-start | bytes 344072 | tf_op jit(solution)/shard_map/ppermute | solution.py:413
  6.4 2.3 %pack_features.1 = (bf16[4,112,256]{2,1,0:T(8,128)(2,1)}, bf16[4,112,256]{2,1,0:T(8,128)(2,1)}, s32[32,128]{1,0:T(8,128)}) custom-call(s32[1,4,8,256]{3,2,1,0:T(8,128)} %idx_ref.1, s32[1,8,256]{2,1,0:T(8,128)} %deg_ref.1, bf16[1,96,8,256]{3,2,1,0:T(8,128)(2,1)} %hop_ref.1, bf16[1,96,256]{2,1,0:T(8,128)(2,1)} %seed_ref.1), custom_call_target="tpu_custom_call" | custom-call | bytes 3000000 | tf_op jit(solution)/shard_map/pack_features/pallas_call | solution.py:476
  8.7 1.6 %collective-permute-start = (bf16[4,112,256]{2,1,0:T(8,128)(2,1)}, bf16[4,112,256]{2,1,0:T(8,128)(2,1)S(1)}, u32[]{:S(2)}, u32[]{:S(2)}) collective-permute-start(bf16[4,112,256]{2,1,0:T(8,128)(2,1)} %get-tuple-element.66), channel_id=1, source_target_pairs={{0,2},{2,0},{4,6},{6,4},{8,10},{10,8},{12,14},{14,12},{1,3},{3,1},... | collective-permute-start | bytes 688136 | tf_op jit(solution)/shard_map/ppermute | solution.py:413
  10.3 1.3 %copy-done = bf16[1,96,6144]{2,1,0:T(8,128)(2,1)S(1)} copy-done((bf16[1,96,6144]{2,1,0:T(8,128)(2,1)S(1)}, bf16[1,96,6144]{2,1,0:T(8,128)(2,1)}, u32[]{:S(2)}) %copy-start) | copy-done | bytes 1179672
  11.6 1.2 %turn_table.1.rows = f32[6152,128]{1,0:T(8,128)S(1)} custom-call(bf16[1,96,6144]{2,1,0:T(8,128)(2,1)S(1)} %copy-done), custom_call_target="tpu_custom_call" | custom-call | bytes 3000000 | tf_op jit(solution)/shard_map/turn_table/pallas_call | solution.py:497
  12.8 0.0 collective-permute-done.1.second
  12.9 1.6 %collective-permute-start.3 = (bf16[224,512]{1,0:T(8,128)(2,1)S(1)}, bf16[224,512]{1,0:T(8,128)(2,1)S(1)}, u32[]{:S(2)}, u32[]{:S(2)}) collective-permute-start(bf16[224,512]{1,0:T(8,128)(2,1)S(1)} %join_rows.4.first), channel_id=1, source_target_pairs={{0,4},{2,6},{4,0},{6,2},{8,12},{10,14},{12,8},{14,10},{1,5},{3,7},... | collective-permute-start | bytes 688136 | tf_op jit(solution)/shard_map/ppermute | solution.py:413
  14.5 2.7 %gather_means.4 = bf16[2,96,256]{2,1,0:T(8,128)(2,1)S(1)} custom-call(s32[4096]{0:T(1024)S(1)} %bitcast.10, f32[6152,128]{1,0:T(8,128)S(1)} %turn_table.1.rows), custom_call_target="tpu_custom_call" | custom-call | bytes 3000000 | tf_op jit(solution)/shard_map/gather_means/pallas_call | solution.py:516
  17.3 0.0 collective-permute-done.pass_ref
  17.3 0.6 collective-permute-start.2
  17.9 2.7 %gather_means.5 = bf16[2,96,256]{2,1,0:T(8,128)(2,1)S(1)} custom-call(s32[4096]{0:T(1024)S(1)} %bitcast.11, f32[6152,128]{1,0:T(8,128)S(1)} %turn_table.1.rows), custom_call_target="tpu_custom_call" | custom-call | bytes 3000000 | tf_op jit(solution)/shard_map/gather_means/pallas_call | solution.py:516
  20.6 1.3 %collective-permute-done.2.pass_ref = bf16[2,96,256]{2,1,0:T(8,128)(2,1)S(1)} collective-permute-done((bf16[2,96,256]{2,1,0:T(8,128)(2,1)S(1)}, bf16[2,96,256]{2,1,0:T(8,128)(2,1)S(1)}, u32[]{:S(2)}, u32[]{:S(2)}) %collective-permute-start.2) | collective-permute-done | bytes 98336 | tf_op jit(solution)/shard_map/ppermute | solution.py:413
  22.0 0.0 collective-permute-done.3.second
  22.0 0.6 collective-permute-start.7
  22.6 1.3 %collective-permute-start.4 = (bf16[224,256]{1,0:T(8,128)(2,1)S(1)}, bf16[224,256]{1,0:T(8,128)(2,1)S(1)}, u32[]{:S(2)}, u32[]{:S(2)}) collective-permute-start(bf16[224,256]{1,0:T(8,128)(2,1)S(1)} %get-tuple-element.86), channel_id=1, source_target_pairs={{0,4},{2,6},{4,8},{6,10},{8,12},{10,14},{12,0},{14,2},{1,5},{3,7},... | collective-permute-start | bytes 344072 | tf_op jit(solution)/shard_map/ppermute | solution.py:409
  23.9 1.5 %collective-permute-start.5 = (bf16[224,256]{1,0:T(8,128)(2,1)S(1)}, bf16[224,256]{1,0:T(8,128)(2,1)S(1)}, u32[]{:S(2)}, u32[]{:S(2)}) collective-permute-start(bf16[224,256]{1,0:T(8,128)(2,1)S(1)} %get-tuple-element.87), channel_id=1, source_target_pairs={{0,8},{2,10},{4,12},{6,14},{8,0},{10,2},{12,4},{14,6},{1,9},{3,11}... | collective-permute-start | bytes 344072 | tf_op jit(solution)/shard_map/ppermute | solution.py:409
  25.4 2.9 %collective-permute-start.6 = (bf16[224,256]{1,0:T(8,128)(2,1)S(1)}, bf16[224,256]{1,0:T(8,128)(2,1)S(1)}, u32[]{:S(2)}, u32[]{:S(2)}) collective-permute-start(bf16[224,256]{1,0:T(8,128)(2,1)S(1)} %get-tuple-element.88), channel_id=1, source_target_pairs={{0,12},{2,14},{4,0},{6,2},{8,4},{10,6},{12,8},{14,10},{1,13},{3,15... | collective-permute-start | bytes 344072 | tf_op jit(solution)/shard_map/ppermute | solution.py:409
  28.2 0.5 collective-permute-start.8
  28.7 2.7 %gather_means.6.keep_ref = bf16[2,96,256]{2,1,0:T(8,128)(2,1)S(1)} custom-call(s32[4096]{0:T(1024)S(1)} %bitcast.12, f32[6152,128]{1,0:T(8,128)S(1)} %turn_table.1.rows), custom_call_target="tpu_custom_call" | custom-call | bytes 3000000 | tf_op jit(solution)/shard_map/gather_means/pallas_call | solution.py:516
  31.5 2.7 %gather_means.7.keep_ref = bf16[2,96,256]{2,1,0:T(8,128)(2,1)S(1)} custom-call(s32[4096]{0:T(1024)S(1)} %bitcast.13, f32[6152,128]{1,0:T(8,128)S(1)} %turn_table.1.rows), custom_call_target="tpu_custom_call" | custom-call | bytes 3000000 | tf_op jit(solution)/shard_map/gather_means/pallas_call | solution.py:516
  34.3 0.0 collective-permute-done.4.rest_1_
  34.3 0.0 collective-permute-done.5.rest_2_
  34.3 0.0 collective-permute-done.6.rest_3_
  34.3 0.2 collective-permute-done.8.pass_ref
  34.5 2.7 %collective-permute-start.11 = (bf16[192,256]{1,0:T(8,128)(2,1)S(1)}, bf16[192,256]{1,0:T(8,128)(2,1)S(1)}, u32[]{:S(2)}, u32[]{:S(2)}) collective-permute-start(bf16[192,256]{1,0:T(8,128)(2,1)S(1)} %get-tuple-element.99), channel_id=1, source_target_pairs={{0,12},{2,14},{4,0},{6,2},{8,4},{10,6},{12,8},{14,10},{1,13},{3,15... | collective-permute-start | bytes 294920 | tf_op jit(solution)/shard_map/ppermute | solution.py:409
  37.2 0.3 collective-permute-start.10
  37.6 1.9 %collective-permute-start.9 = (bf16[192,256]{1,0:T(8,128)(2,1)S(1)}, bf16[192,256]{1,0:T(8,128)(2,1)S(1)}, u32[]{:S(2)}, u32[]{:S(2)}) collective-permute-start(bf16[192,256]{1,0:T(8,128)(2,1)S(1)} %get-tuple-element.97), channel_id=1, source_target_pairs={{0,4},{2,6},{4,8},{6,10},{8,12},{10,14},{12,0},{14,2},{1,5},{3,7},... | collective-permute-start | bytes 294920 | tf_op jit(solution)/shard_map/ppermute | solution.py:409
  39.5 0.5 collective-permute-done.11.rest_7_
  40.0 6.2 %collective-permute-done.10.rest_6_ = bf16[192,256]{1,0:T(8,128)(2,1)S(1)} collective-permute-done((bf16[192,256]{1,0:T(8,128)(2,1)S(1)}, bf16[192,256]{1,0:T(8,128)(2,1)S(1)}, u32[]{:S(2)}, u32[]{:S(2)}) %collective-permute-start.10) | collective-permute-done | bytes 98336 | tf_op jit(solution)/shard_map/ppermute | solution.py:409
  46.2 0.0 collective-permute-done.9.rest_5_
  46.2 0.0 collective-permute-done.7.far_ref.far
  46.2 0.0 collective-permute-start.12
  46.2 0.5 collective-permute-start.13
  46.7 0.4 stack_features.1
  47.1 0.1 collective-permute-start.14
  47.3 0.7 collective-permute-done.12.near_other_ref.near_other
  48.0 0.7 collective-permute-done.13.far_other_ref.far_other
  48.7 1.9 %forward.1 = (bf16[1,32,153]{2,1,0:T(8,128)(2,1)}, bf16[2,32,512]{2,1,0:T(8,128)(2,1)S(1)}, bf16[384,512]{1,0:T(8,128)(2,1)S(1)}) custom-call(s32[1,256]{1,0:T(1,128)S(1)} %copy-done.6, bf16[768,384]{1,0:T(8,128)(2,1)S(1)} %get-tuple-element.104.own_ref, bf16[768,384]{1,0:T(8,128)(2,1)S(1)} %get-tuple-element.105.mean_ref, ...), custom_call_target="tpu_custom_call" | custom-call | bytes 9000000 | tf_op jit(solution)/shard_map/forward/pallas_call | solution.py:574
  50.6 0.1 collective-permute-start.15
  50.7 0.4 collective-permute-start.16
  51.1 1.3 %collective-permute-done.16.hid_other_ref = bf16[2,32,512]{2,1,0:T(8,128)(2,1)S(1)} collective-permute-done((bf16[2,32,512]{2,1,0:T(8,128)(2,1)S(1)}, bf16[2,32,512]{2,1,0:T(8,128)(2,1)S(1)}, u32[]{:S(2)}, u32[]{:S(2)}) %collective-permute-start.16) | collective-permute-done | bytes 65568 | tf_op jit(solution)/shard_map/ppermute | solution.py:405
  52.4 0.0 collective-permute-done.14.x_ref
  52.4 1.0 %products.1 = (f32[4,96,512]{2,1,0:T(8,128)S(1)}, bf16[4,96,512]{2,1,0:T(8,128)(2,1)S(1)}, bf16[64,512]{1,0:T(8,128)(2,1)S(1)}) custom-call(bf16[768,384]{1,0:T(8,128)(2,1)S(1)} %get-tuple-element.104.own_ref, bf16[768,384]{1,0:T(8,128)(2,1)S(1)} %get-tuple-element.105.mean_ref, bf16[768,384]{1,0:T(8,128)(2,1)S(1)} %collective-permute-done.14.x_ref, ...), custom_call_target="tpu_custom_call" | custom-call | bytes 6000000 | tf_op jit(solution)/shard_map/products/pallas_call | solution.py:597
  53.4 0.4 collective-permute-start.17
  53.8 1.7 %collective-permute-start.18 = (bf16[64,512]{1,0:T(8,128)(2,1)S(1)}, bf16[64,512]{1,0:T(8,128)(2,1)S(1)}, u32[]{:S(2)}, u32[]{:S(2)}) collective-permute-start(bf16[64,512]{1,0:T(8,128)(2,1)S(1)} %get-tuple-element.115.first), channel_id=1, source_target_pairs={{0,8},{2,10},{4,12},{6,14},{8,0},{10,2},{12,4},{14,6},{1,9},{3,11}... | collective-permute-start | bytes 196616 | tf_op jit(solution)/shard_map/ppermute | solution.py:413
  55.5 3.7 %collective-permute-done.18.second = bf16[64,512]{1,0:T(8,128)(2,1)S(1)} collective-permute-done((bf16[64,512]{1,0:T(8,128)(2,1)S(1)}, bf16[64,512]{1,0:T(8,128)(2,1)S(1)}, u32[]{:S(2)}, u32[]{:S(2)}) %collective-permute-start.18) | collective-permute-done | bytes 65568 | tf_op jit(solution)/shard_map/ppermute | solution.py:413
  59.3 0.1 collective-permute-start.19
  59.4 5.0 %collective-permute-done.19.second = bf16[128,512]{1,0:T(8,128)(2,1)S(1)} collective-permute-done((bf16[128,512]{1,0:T(8,128)(2,1)S(1)}, bf16[128,512]{1,0:T(8,128)(2,1)S(1)}, u32[]{:S(2)}, u32[]{:S(2)}) %collective-permute-start.19) | collective-permute-done | bytes 131104 | tf_op jit(solution)/shard_map/ppermute | solution.py:413
  64.4 1.8 %collective-permute-start.20 = (bf16[256,512]{1,0:T(8,128)(2,1)S(1)}, bf16[256,512]{1,0:T(8,128)(2,1)S(1)}, u32[]{:S(2)}, u32[]{:S(2)}) collective-permute-start(bf16[256,512]{1,0:T(8,128)(2,1)S(1)} %join_rows.7.hid_near), channel_id=1, source_target_pairs={{0,2},{2,0},{4,6},{6,4},{8,10},{10,8},{12,14},{14,12},{1,3},{3,1},... | collective-permute-start | bytes 786440 | tf_op jit(solution)/shard_map/ppermute | solution.py:413
  66.2 0.0 collective-permute-done.17.passed_ref
  66.2 0.1 join_pairs.1
  66.3 2.2 %collective-permute-start.21 = (bf16[96,512]{1,0:T(8,128)(2,1)S(1)}, bf16[96,512]{1,0:T(8,128)(2,1)S(1)}, u32[]{:S(2)}, u32[]{:S(2)}) collective-permute-start(bf16[96,512]{1,0:T(8,128)(2,1)S(1)} %get-tuple-element.116), channel_id=1, source_target_pairs={{0,12},{2,14},{4,0},{6,2},{8,4},{10,6},{12,8},{14,10},{1,13},{3,15... | collective-permute-start | bytes 294920 | tf_op jit(solution)/shard_map/ppermute | solution.py:409
  68.4 0.0 collective-permute-start.22
  68.4 0.9 %collective-permute-start.23 = (bf16[96,512]{1,0:T(8,128)(2,1)S(1)}, bf16[96,512]{1,0:T(8,128)(2,1)S(1)}, u32[]{:S(2)}, u32[]{:S(2)}) collective-permute-start(bf16[96,512]{1,0:T(8,128)(2,1)S(1)} %get-tuple-element.118), channel_id=1, source_target_pairs={{0,4},{2,6},{4,8},{6,10},{8,12},{10,14},{12,0},{14,2},{1,5},{3,7},... | collective-permute-start | bytes 294920 | tf_op jit(solution)/shard_map/ppermute | solution.py:409
  69.3 2.1 %collective-permute-done.20.hid_far = bf16[256,512]{1,0:T(8,128)(2,1)S(1)} collective-permute-done((bf16[256,512]{1,0:T(8,128)(2,1)S(1)}, bf16[256,512]{1,0:T(8,128)(2,1)S(1)}, u32[]{:S(2)}, u32[]{:S(2)}) %collective-permute-start.20) | collective-permute-done | bytes 262176 | tf_op jit(solution)/shard_map/ppermute | solution.py:413
  71.4 0.0 collective-permute-done.21.rest_0_
  71.4 4.4 %collective-permute-done.22.rest_1_ = bf16[96,512]{1,0:T(8,128)(2,1)S(1)} collective-permute-done((bf16[96,512]{1,0:T(8,128)(2,1)S(1)}, bf16[96,512]{1,0:T(8,128)(2,1)S(1)}, u32[]{:S(2)}, u32[]{:S(2)}) %collective-permute-start.22) | collective-permute-done | bytes 98336 | tf_op jit(solution)/shard_map/ppermute | solution.py:409
  75.9 0.3 total_gradients.1
  76.2 0.1 collective-permute-start.25
  76.3 0.5 collective-permute-start.24
  76.8 1.4 %collective-permute-done.24.w_other = f32[96,512]{1,0:T(8,128)S(1)} collective-permute-done((f32[96,512]{1,0:T(8,128)S(1)}, f32[96,512]{1,0:T(8,128)S(1)}, u32[]{:S(2)}, u32[]{:S(2)}) %collective-permute-start.24) | collective-permute-done | bytes 196640 | tf_op jit(solution)/shard_map/ppermute | solution.py:405
  78.2 1.0 %place_gradients.1 = (f32[96,512]{1,0:T(8,128)}, f32[96,512]{1,0:T(8,128)}, f32[153,512]{1,0:T(8,128)}, f32[153,512]{1,0:T(8,128)}) custom-call(f32[96,512]{1,0:T(8,128)S(1)} %get-tuple-element.119.w_mine, f32[96,512]{1,0:T(8,128)S(1)} %collective-permute-done.24.w_other, f32[153,512]{1,0:T(8,128)S(1)} %get-tuple-element.120.v_mine, ...), custom_call_target="tpu_custom_call" | custom-call | bytes 3000000 | tf_op jit(solution)/shard_map/place_gradients/pallas_call | solution.py:624
  (24 shorter events, 0.2 us)
Async XLA Ops:
  2.3 10.6 %collective-permute-start.1 = (bf16[112,512]{1,0:T(8,128)(2,1)S(1)}, bf16[112,512]{1,0:T(8,128)(2,1)S(1)}, u32[]{:S(2)}, u32[]{:S(2)}) collective-permute-start(bf16[112,512]{1,0:T(8,128)(2,1)S(1)} %maximum_maximum_fusion.first), channel_id=1, source_target_pairs={{0,8},{2,10},{4,12},{6,14},{8,0},{10,2},{12,4},{14,6},{1,9},{3,11}... | collective-permute-start | bytes 344072 | tf_op jit(solution)/shard_map/ppermute | solution.py:413
  8.7 8.5 %collective-permute-start = (bf16[4,112,256]{2,1,0:T(8,128)(2,1)}, bf16[4,112,256]{2,1,0:T(8,128)(2,1)S(1)}, u32[]{:S(2)}, u32[]{:S(2)}) collective-permute-start(bf16[4,112,256]{2,1,0:T(8,128)(2,1)} %get-tuple-element.66), channel_id=1, source_target_pairs={{0,2},{2,0},{4,6},{6,4},{8,10},{10,8},{12,14},{14,12},{1,3},{3,1},... | collective-permute-start | bytes 688136 | tf_op jit(solution)/shard_map/ppermute | solution.py:413
  10.3 1.3 %copy-start = (bf16[1,96,6144]{2,1,0:T(8,128)(2,1)S(1)}, bf16[1,96,6144]{2,1,0:T(8,128)(2,1)}, u32[]{:S(2)}) copy-start(bf16[1,96,6144]{2,1,0:T(8,128)(2,1)} %table.1) | copy-start | bytes 3538948
  11.6 2.9 %copy-start.1 = (s32[32,128]{1,0:T(8,128)S(1)}, s32[32,128]{1,0:T(8,128)}, u32[]{:S(2)}) copy-start(s32[32,128]{1,0:T(8,128)} %get-tuple-element.67) | copy-start | bytes 49156
  11.6 6.3 %copy-start.2 = (bf16[4,112,256]{2,1,0:T(8,128)(2,1)S(1)}, bf16[4,112,256]{2,1,0:T(8,128)(2,1)}, u32[]{:S(2)}) copy-start(bf16[4,112,256]{2,1,0:T(8,128)(2,1)} %get-tuple-element.65.keep_ref) | copy-start | bytes 688132
  12.9 9.1 %collective-permute-start.3 = (bf16[224,512]{1,0:T(8,128)(2,1)S(1)}, bf16[224,512]{1,0:T(8,128)(2,1)S(1)}, u32[]{:S(2)}, u32[]{:S(2)}) collective-permute-start(bf16[224,512]{1,0:T(8,128)(2,1)S(1)} %join_rows.4.first), channel_id=1, source_target_pairs={{0,4},{2,6},{4,0},{6,2},{8,12},{10,14},{12,8},{14,10},{1,5},{3,7},... | collective-permute-start | bytes 688136 | tf_op jit(solution)/shard_map/ppermute | solution.py:413
  17.3 4.7 %collective-permute-start.2 = (bf16[2,96,256]{2,1,0:T(8,128)(2,1)S(1)}, bf16[2,96,256]{2,1,0:T(8,128)(2,1)S(1)}, u32[]{:S(2)}, u32[]{:S(2)}) collective-permute-start(bf16[2,96,256]{2,1,0:T(8,128)(2,1)S(1)} %gather_means.4), channel_id=1, source_target_pairs={{0,2},{2,0},{4,6},{6,4},{8,10},{10,8},{12,14},{14,12},{1,3},{3,1},... | collective-permute-start | bytes 294920 | tf_op jit(solution)/shard_map/ppermute | solution.py:413
  22.0 24.2 %collective-permute-start.7 = (bf16[448,512]{1,0:T(8,128)(2,1)S(1)}, bf16[448,512]{1,0:T(8,128)(2,1)S(1)}, u32[]{:S(2)}, u32[]{:S(2)}) collective-permute-start(bf16[448,512]{1,0:T(8,128)(2,1)S(1)} %join_rows.5.near_ref.near), channel_id=1, source_target_pairs={{0,2},{2,0},{4,6},{6,4},{8,10},{10,8},{12,14},{14,12},{1,3},{3,1},... | collective-permute-start | bytes 1376264 | tf_op jit(solution)/shard_map/ppermute | solution.py:413
  22.6 11.7 %collective-permute-start.4 = (bf16[224,256]{1,0:T(8,128)(2,1)S(1)}, bf16[224,256]{1,0:T(8,128)(2,1)S(1)}, u32[]{:S(2)}, u32[]{:S(2)}) collective-permute-start(bf16[224,256]{1,0:T(8,128)(2,1)S(1)} %get-tuple-element.86), channel_id=1, source_target_pairs={{0,4},{2,6},{4,8},{6,10},{8,12},{10,14},{12,0},{14,2},{1,5},{3,7},... | collective-permute-start | bytes 344072 | tf_op jit(solution)/shard_map/ppermute | solution.py:409
  23.9 10.4 %collective-permute-start.5 = (bf16[224,256]{1,0:T(8,128)(2,1)S(1)}, bf16[224,256]{1,0:T(8,128)(2,1)S(1)}, u32[]{:S(2)}, u32[]{:S(2)}) collective-permute-start(bf16[224,256]{1,0:T(8,128)(2,1)S(1)} %get-tuple-element.87), channel_id=1, source_target_pairs={{0,8},{2,10},{4,12},{6,14},{8,0},{10,2},{12,4},{14,6},{1,9},{3,11}... | collective-permute-start | bytes 344072 | tf_op jit(solution)/shard_map/ppermute | solution.py:409
  25.4 21.4 %copy-start.6 = (s32[1,256]{1,0:T(1,128)S(1)}, s32[1,256]{1,0:T(1,128)}, u32[]{:S(2)}) copy-start(s32[1,256]{1,0:T(1,128)} %seed_degree_ref.3) | copy-start | bytes 3076
  25.4 23.3 %copy-start.3 = (bf16[512,153]{0,1:T(8,128)(2,1)S(1)}, bf16[512,153]{0,1:T(8,128)(2,1)}, u32[]{:S(2)}) copy-start(bf16[512,153]{0,1:T(8,128)(2,1)} %param.19) | copy-start | bytes 470020
  25.4 23.3 %copy-start.4 = (bf16[512,153]{0,1:T(8,128)(2,1)S(1)}, bf16[512,153]{0,1:T(8,128)(2,1)}, u32[]{:S(2)}) copy-start(bf16[512,153]{0,1:T(8,128)(2,1)} %param.20) | copy-start | bytes 470020
  25.4 23.3 %copy-start.5 = (bf16[1,32,153]{2,1,0:T(8,128)(2,1)S(1)}, bf16[1,32,153]{2,1,0:T(8,128)(2,1)}, u32[]{:S(2)}) copy-start(bf16[1,32,153]{2,1,0:T(8,128)(2,1)} %cot_ref.1) | copy-start | bytes 29380
  25.4 8.9 %collective-permute-start.6 = (bf16[224,256]{1,0:T(8,128)(2,1)S(1)}, bf16[224,256]{1,0:T(8,128)(2,1)S(1)}, u32[]{:S(2)}, u32[]{:S(2)}) collective-permute-start(bf16[224,256]{1,0:T(8,128)(2,1)S(1)} %get-tuple-element.88), channel_id=1, source_target_pairs={{0,12},{2,14},{4,0},{6,2},{8,4},{10,6},{12,8},{14,10},{1,13},{3,15... | collective-permute-start | bytes 344072 | tf_op jit(solution)/shard_map/ppermute | solution.py:409
  28.2 6.2 %collective-permute-start.8 = (bf16[2,96,256]{2,1,0:T(8,128)(2,1)S(1)}, bf16[2,96,256]{2,1,0:T(8,128)(2,1)S(1)}, u32[]{:S(2)}, u32[]{:S(2)}) collective-permute-start(bf16[2,96,256]{2,1,0:T(8,128)(2,1)S(1)} %gather_means.5), channel_id=1, source_target_pairs={{0,2},{2,0},{4,6},{6,4},{8,10},{10,8},{12,14},{14,12},{1,3},{3,1},... | collective-permute-start | bytes 294920 | tf_op jit(solution)/shard_map/ppermute | solution.py:413
  34.5 5.5 %collective-permute-start.11 = (bf16[192,256]{1,0:T(8,128)(2,1)S(1)}, bf16[192,256]{1,0:T(8,128)(2,1)S(1)}, u32[]{:S(2)}, u32[]{:S(2)}) collective-permute-start(bf16[192,256]{1,0:T(8,128)(2,1)S(1)} %get-tuple-element.99), channel_id=1, source_target_pairs={{0,12},{2,14},{4,0},{6,2},{8,4},{10,6},{12,8},{14,10},{1,13},{3,15... | collective-permute-start | bytes 294920 | tf_op jit(solution)/shard_map/ppermute | solution.py:409
  37.2 9.0 %collective-permute-start.10 = (bf16[192,256]{1,0:T(8,128)(2,1)S(1)}, bf16[192,256]{1,0:T(8,128)(2,1)S(1)}, u32[]{:S(2)}, u32[]{:S(2)}) collective-permute-start(bf16[192,256]{1,0:T(8,128)(2,1)S(1)} %get-tuple-element.98), channel_id=1, source_target_pairs={{0,8},{2,10},{4,12},{6,14},{8,0},{10,2},{12,4},{14,6},{1,9},{3,11}... | collective-permute-start | bytes 294920 | tf_op jit(solution)/shard_map/ppermute | solution.py:409
  37.6 8.6 %collective-permute-start.9 = (bf16[192,256]{1,0:T(8,128)(2,1)S(1)}, bf16[192,256]{1,0:T(8,128)(2,1)S(1)}, u32[]{:S(2)}, u32[]{:S(2)}) collective-permute-start(bf16[192,256]{1,0:T(8,128)(2,1)S(1)} %get-tuple-element.97), channel_id=1, source_target_pairs={{0,4},{2,6},{4,8},{6,10},{8,12},{10,14},{12,0},{14,2},{1,5},{3,7},... | collective-permute-start | bytes 294920 | tf_op jit(solution)/shard_map/ppermute | solution.py:409
  46.2 1.8 %collective-permute-start.12 = (bf16[448,512]{1,0:T(8,128)(2,1)S(1)}, bf16[448,512]{1,0:T(8,128)(2,1)S(1)}, u32[]{:S(2)}, u32[]{:S(2)}) collective-permute-start(bf16[448,512]{1,0:T(8,128)(2,1)S(1)} %join_rows.5.near_ref.near), channel_id=1, source_target_pairs={{0,1},{1,0},{2,3},{3,2},{4,5},{5,4},{6,7},{7,6},{8,9},{9,8},{10,11... | collective-permute-start | bytes 1376264 | tf_op jit(solution)/shard_map/ppermute | solution.py:405
  46.2 2.5 %collective-permute-start.13 = (bf16[448,512]{1,0:T(8,128)(2,1)S(1)}, bf16[448,512]{1,0:T(8,128)(2,1)S(1)}, u32[]{:S(2)}, u32[]{:S(2)}) collective-permute-start(bf16[448,512]{1,0:T(8,128)(2,1)S(1)} %collective-permute-done.7.far_ref.far), channel_id=1, source_target_pairs={{0,1},{1,0},{2,3},{3,2},{4,5},{5,4},{6,7},{7,6},{8,9},{9,8},{10,11... | collective-permute-start | bytes 1376264 | tf_op jit(solution)/shard_map/ppermute | solution.py:405
  47.1 5.3 %collective-permute-start.14 = (bf16[768,384]{1,0:T(8,128)(2,1)S(1)}, bf16[768,384]{1,0:T(8,128)(2,1)S(1)}, u32[]{:S(2)}, u32[]{:S(2)}) collective-permute-start(bf16[768,384]{1,0:T(8,128)(2,1)S(1)} %get-tuple-element.109), channel_id=1, source_target_pairs={{0,1},{1,0},{2,3},{3,2},{4,5},{5,4},{6,7},{7,6},{8,9},{9,8},{10,11... | collective-permute-start | bytes 1769480 | tf_op jit(solution)/shard_map/ppermute | solution.py:405
  50.6 1.8 %collective-permute-start.15 = (bf16[384,512]{1,0:T(8,128)(2,1)S(1)}, bf16[384,512]{1,0:T(8,128)(2,1)S(1)}, u32[]{:S(2)}, u32[]{:S(2)}) collective-permute-start(bf16[384,512]{1,0:T(8,128)(2,1)S(1)} %get-tuple-element.110.dpre_ref), channel_id=1, source_target_pairs={{0,1},{1,0},{2,3},{3,2},{4,5},{5,4},{6,7},{7,6},{8,9},{9,8},{10,11... | collective-permute-start | bytes 1179656 | tf_op jit(solution)/shard_map/ppermute | solution.py:405
  50.7 1.7 %collective-permute-start.16 = (bf16[2,32,512]{2,1,0:T(8,128)(2,1)S(1)}, bf16[2,32,512]{2,1,0:T(8,128)(2,1)S(1)}, u32[]{:S(2)}, u32[]{:S(2)}) collective-permute-start(bf16[2,32,512]{2,1,0:T(8,128)(2,1)S(1)} %get-tuple-element.111.hid_ref), channel_id=1, source_target_pairs={{0,1},{1,0},{2,3},{3,2},{4,5},{5,4},{6,7},{7,6},{8,9},{9,8},{10,11... | collective-permute-start | bytes 196616 | tf_op jit(solution)/shard_map/ppermute | solution.py:405
  53.4 12.8 %collective-permute-start.17 = (bf16[4,96,512]{2,1,0:T(8,128)(2,1)S(1)}, bf16[4,96,512]{2,1,0:T(8,128)(2,1)S(1)}, u32[]{:S(2)}, u32[]{:S(2)}) collective-permute-start(bf16[4,96,512]{2,1,0:T(8,128)(2,1)S(1)} %get-tuple-element.113), channel_id=1, source_target_pairs={{0,2},{2,0},{4,6},{6,4},{8,10},{10,8},{12,14},{14,12},{1,3},{3,1},... | collective-permute-start | bytes 1179656 | tf_op jit(solution)/shard_map/ppermute | solution.py:413
  53.8 5.5 %collective-permute-start.18 = (bf16[64,512]{1,0:T(8,128)(2,1)S(1)}, bf16[64,512]{1,0:T(8,128)(2,1)S(1)}, u32[]{:S(2)}, u32[]{:S(2)}) collective-permute-start(bf16[64,512]{1,0:T(8,128)(2,1)S(1)} %get-tuple-element.115.first), channel_id=1, source_target_pairs={{0,8},{2,10},{4,12},{6,14},{8,0},{10,2},{12,4},{14,6},{1,9},{3,11}... | collective-permute-start | bytes 196616 | tf_op jit(solution)/shard_map/ppermute | solution.py:413
  59.3 5.1 %collective-permute-start.19 = (bf16[128,512]{1,0:T(8,128)(2,1)S(1)}, bf16[128,512]{1,0:T(8,128)(2,1)S(1)}, u32[]{:S(2)}, u32[]{:S(2)}) collective-permute-start(bf16[128,512]{1,0:T(8,128)(2,1)S(1)} %join_rows.6.first), channel_id=1, source_target_pairs={{0,4},{2,6},{4,0},{6,2},{8,12},{10,14},{12,8},{14,10},{1,5},{3,7},... | collective-permute-start | bytes 393224 | tf_op jit(solution)/shard_map/ppermute | solution.py:413
  64.4 7.0 %collective-permute-start.20 = (bf16[256,512]{1,0:T(8,128)(2,1)S(1)}, bf16[256,512]{1,0:T(8,128)(2,1)S(1)}, u32[]{:S(2)}, u32[]{:S(2)}) collective-permute-start(bf16[256,512]{1,0:T(8,128)(2,1)S(1)} %join_rows.7.hid_near), channel_id=1, source_target_pairs={{0,2},{2,0},{4,6},{6,4},{8,10},{10,8},{12,14},{14,12},{1,3},{3,1},... | collective-permute-start | bytes 786440 | tf_op jit(solution)/shard_map/ppermute | solution.py:413
  66.3 5.2 %collective-permute-start.21 = (bf16[96,512]{1,0:T(8,128)(2,1)S(1)}, bf16[96,512]{1,0:T(8,128)(2,1)S(1)}, u32[]{:S(2)}, u32[]{:S(2)}) collective-permute-start(bf16[96,512]{1,0:T(8,128)(2,1)S(1)} %get-tuple-element.116), channel_id=1, source_target_pairs={{0,12},{2,14},{4,0},{6,2},{8,4},{10,6},{12,8},{14,10},{1,13},{3,15... | collective-permute-start | bytes 294920 | tf_op jit(solution)/shard_map/ppermute | solution.py:409
  68.4 7.4 %collective-permute-start.22 = (bf16[96,512]{1,0:T(8,128)(2,1)S(1)}, bf16[96,512]{1,0:T(8,128)(2,1)S(1)}, u32[]{:S(2)}, u32[]{:S(2)}) collective-permute-start(bf16[96,512]{1,0:T(8,128)(2,1)S(1)} %get-tuple-element.117), channel_id=1, source_target_pairs={{0,8},{2,10},{4,12},{6,14},{8,0},{10,2},{12,4},{14,6},{1,9},{3,11}... | collective-permute-start | bytes 294920 | tf_op jit(solution)/shard_map/ppermute | solution.py:409
  68.4 7.4 %collective-permute-start.23 = (bf16[96,512]{1,0:T(8,128)(2,1)S(1)}, bf16[96,512]{1,0:T(8,128)(2,1)S(1)}, u32[]{:S(2)}, u32[]{:S(2)}) collective-permute-start(bf16[96,512]{1,0:T(8,128)(2,1)S(1)} %get-tuple-element.118), channel_id=1, source_target_pairs={{0,4},{2,6},{4,8},{6,10},{8,12},{10,14},{12,0},{14,2},{1,5},{3,7},... | collective-permute-start | bytes 294920 | tf_op jit(solution)/shard_map/ppermute | solution.py:409
  76.2 2.0 %collective-permute-start.25 = (f32[153,512]{1,0:T(8,128)S(1)}, f32[153,512]{1,0:T(8,128)S(1)}, u32[]{:S(2)}, u32[]{:S(2)}) collective-permute-start(f32[153,512]{1,0:T(8,128)S(1)} %get-tuple-element.120.v_mine), channel_id=1, source_target_pairs={{0,1},{1,0},{2,3},{3,2},{4,5},{5,4},{6,7},{7,6},{8,9},{9,8},{10,11... | collective-permute-start | bytes 940040 | tf_op jit(solution)/shard_map/ppermute | solution.py:405
  76.3 1.9 %collective-permute-start.24 = (f32[96,512]{1,0:T(8,128)S(1)}, f32[96,512]{1,0:T(8,128)S(1)}, u32[]{:S(2)}, u32[]{:S(2)}) collective-permute-start(f32[96,512]{1,0:T(8,128)S(1)} %get-tuple-element.119.w_mine), channel_id=1, source_target_pairs={{0,1},{1,0},{2,3},{3,2},{4,5},{5,4},{6,7},{7,6},{8,9},{9,8},{10,11... | collective-permute-start | bytes 589832 | tf_op jit(solution)/shard_map/ppermute | solution.py:405

commit v7 on v6

--- a/solution.py
+++ b/solution.py
@@ -537,7 +537,7 @@
             shift_by(x, sign * 2 * k, owners) if k else x for k, x in zip(steps, blocks)
         ]
 
-    order = sorted(range(1, pairs), key=lambda k: (-min(k, pairs - k), k)) + [0]
+    order = sorted(range(1, pairs), key=lambda k: (-min(k, pairs - k), -k)) + [0]
     early, late = order[: pairs // 2], order[pairs // 2 :]
     early_passed = gather(True, early, live)
     passed, early_passed = lax.optimization_barrier((passed, early_passed))

time: 79.5 us -> 78.4 us (0.986)
  waiting for transfers between devices: 27.6 us -> 26.2 us
    ppermute x9, waiting for transfers between devices: 11.1 us -> 8.02 us  [shift_by(): lax.ppermute(x, 'feat', [(k, (k + step) % owners) for k in range(owners)])]
    ppermute x10, waiting for transfers between devices: 12.3 us -> 14.1 us  [across(): return lax.ppermute(x, 'feat', [(k, k ^ mask) for k in range(owners)])]
    ppermute x9, starting transfers between devices: 13.7 us -> 14.6 us  [shift_by(): lax.ppermute(x, 'feat', [(k, (k + step) % owners) for k in range(owners)])]
  transfers between devices with their start and end apart: 26 -> 26, of which waited for: 12 -> 13; matrix products, arithmetic and copies ran while one was open for 0% -> 0% of each run, Pallas kernels for 21% -> 22%
where the time goes in v7:
time: 78.4 us; the launch traced here: 78.1 us
  starting transfers between devices  28.7 us (37%)
  waiting for transfers between devices  26.2 us (33%)
  Pallas kernels  19.4 us (25%)
  local copies, waits for them, and re-layouts  2.02 us (3%)
  other arithmetic  0.92 us (1%)
  between operations  0.85 us (1%)
    ppermute x9, starting transfers between devices, shift_by(): lax.ppermute(x, 'feat', [(k, (k + step) % owners) for k in range(owners)])  14.6 us
    ppermute x10, waiting for transfers between devices, across(): return lax.ppermute(x, 'feat', [(k, k ^ mask) for k in range(owners)])  14.1 us
    ppermute x10, starting transfers between devices, across(): return lax.ppermute(x, 'feat', [(k, k ^ mask) for k in range(owners)])  12.4 us
    pallas_call x4, Pallas kernels, gather(): call(functools.partial(gather_means, (owners, seeds, fan, f, fp), across_...  11 us
    ppermute x9, waiting for transfers between devices, shift_by(): lax.ppermute(x, 'feat', [(k, (k + step) % owners) for k in range(owners)])  8.02 us
    ppermute x7, waiting for transfers between devices, swap(): return lax.ppermute(x, 'rep', [(0, 1), (1, 0)])  4.11 us
    pallas_call x1, Pallas kernels, on_device(): call(functools.partial(pack_features, (owners, seeds, fan, f, fp, nodes))...  2.34 us
    pallas_call x1, Pallas kernels, on_device(): call(functools.partial(forward, (owners, seeds, fan, fp, width, offsets_o...  1.88 us
  transfers between devices with their start and end apart: 26, of which 13 were waited for; matrix products, arithmetic and copies ran while one was open for 0% of the time, Pallas kernels for 22%

profile of v7, /device:TPU:0, one launch (start us, length us, event | category | flops | bytes accessed | tf_op | source)
XLA Modules:
  0.0 78.1 jit_solution(16507846347788984433)
XLA Ops:
  0.6 0.7 fusion
  1.4 0.9 %broadcast_select_fusion = bf16[96,512]{1,0:T(8,128)(2,1)S(1)} fusion(bf16[96,512]{1,0:T(8,128)(2,1)} %param.17, bf16[96,512]{1,0:T(8,128)(2,1)} %param.18, pred[]{:T(512)S(6)} %eq.3), kind=kLoop, calls=%fused_computation.1 | loop fusion | flops 49152 | bytes 294913 | tf_op jit(solution)/shard_map/jit(_where)/select_n | solution.py:464
  2.3 4.1 %collective-permute-start.1 = (bf16[112,512]{1,0:T(8,128)(2,1)S(1)}, bf16[112,512]{1,0:T(8,128)(2,1)S(1)}, u32[]{:S(2)}, u32[]{:S(2)}) collective-permute-start(bf16[112,512]{1,0:T(8,128)(2,1)S(1)} %maximum_maximum_fusion.first), channel_id=1, source_target_pairs={{0,8},{2,10},{4,12},{6,14},{8,0},{10,2},{12,4},{14,6},{1,9},{3,11}... | collective-permute-start | bytes 344072 | tf_op jit(solution)/shard_map/ppermute | solution.py:413
  6.4 2.3 %pack_features.1 = (bf16[4,112,256]{2,1,0:T(8,128)(2,1)}, bf16[4,112,256]{2,1,0:T(8,128)(2,1)}, s32[32,128]{1,0:T(8,128)}) custom-call(s32[1,4,8,256]{3,2,1,0:T(8,128)} %idx_ref.1, s32[1,8,256]{2,1,0:T(8,128)} %deg_ref.1, bf16[1,96,8,256]{3,2,1,0:T(8,128)(2,1)} %hop_ref.1, bf16[1,96,256]{2,1,0:T(8,128)(2,1)} %seed_ref.1), custom_call_target="tpu_custom_call" | custom-call | bytes 3000000 | tf_op jit(solution)/shard_map/pack_features/pallas_call | solution.py:476
  8.7 1.6 %collective-permute-start = (bf16[4,112,256]{2,1,0:T(8,128)(2,1)}, bf16[4,112,256]{2,1,0:T(8,128)(2,1)S(1)}, u32[]{:S(2)}, u32[]{:S(2)}) collective-permute-start(bf16[4,112,256]{2,1,0:T(8,128)(2,1)} %get-tuple-element.66), channel_id=1, source_target_pairs={{0,2},{2,0},{4,6},{6,4},{8,10},{10,8},{12,14},{14,12},{1,3},{3,1},... | collective-permute-start | bytes 688136 | tf_op jit(solution)/shard_map/ppermute | solution.py:413
  10.3 1.3 %copy-done = bf16[1,96,6144]{2,1,0:T(8,128)(2,1)S(1)} copy-done((bf16[1,96,6144]{2,1,0:T(8,128)(2,1)S(1)}, bf16[1,96,6144]{2,1,0:T(8,128)(2,1)}, u32[]{:S(2)}) %copy-start) | copy-done | bytes 1179672
  11.6 1.2 %turn_table.1.rows = f32[6152,128]{1,0:T(8,128)S(1)} custom-call(bf16[1,96,6144]{2,1,0:T(8,128)(2,1)S(1)} %copy-done), custom_call_target="tpu_custom_call" | custom-call | bytes 3000000 | tf_op jit(solution)/shard_map/turn_table/pallas_call | solution.py:497
  12.8 0.0 collective-permute-done.1.second
  12.9 1.6 %collective-permute-start.3 = (bf16[224,512]{1,0:T(8,128)(2,1)S(1)}, bf16[224,512]{1,0:T(8,128)(2,1)S(1)}, u32[]{:S(2)}, u32[]{:S(2)}) collective-permute-start(bf16[224,512]{1,0:T(8,128)(2,1)S(1)} %join_rows.4.first), channel_id=1, source_target_pairs={{0,4},{2,6},{4,0},{6,2},{8,12},{10,14},{12,8},{14,10},{1,5},{3,7},... | collective-permute-start | bytes 688136 | tf_op jit(solution)/shard_map/ppermute | solution.py:413
  14.5 2.7 %gather_means.4 = bf16[2,96,256]{2,1,0:T(8,128)(2,1)S(1)} custom-call(s32[4096]{0:T(1024)S(1)} %bitcast.10, f32[6152,128]{1,0:T(8,128)S(1)} %turn_table.1.rows), custom_call_target="tpu_custom_call" | custom-call | bytes 3000000 | tf_op jit(solution)/shard_map/gather_means/pallas_call | solution.py:516
  17.3 0.0 collective-permute-done.pass_ref
  17.3 0.6 collective-permute-start.2
  17.9 2.7 %gather_means.5 = bf16[2,96,256]{2,1,0:T(8,128)(2,1)S(1)} custom-call(s32[4096]{0:T(1024)S(1)} %bitcast.11, f32[6152,128]{1,0:T(8,128)S(1)} %turn_table.1.rows), custom_call_target="tpu_custom_call" | custom-call | bytes 3000000 | tf_op jit(solution)/shard_map/gather_means/pallas_call | solution.py:516
  20.6 1.3 %collective-permute-done.2.pass_ref = bf16[2,96,256]{2,1,0:T(8,128)(2,1)S(1)} collective-permute-done((bf16[2,96,256]{2,1,0:T(8,128)(2,1)S(1)}, bf16[2,96,256]{2,1,0:T(8,128)(2,1)S(1)}, u32[]{:S(2)}, u32[]{:S(2)}) %collective-permute-start.2) | collective-permute-done | bytes 98336 | tf_op jit(solution)/shard_map/ppermute | solution.py:413
  22.0 0.0 collective-permute-done.3.second
  22.0 0.6 collective-permute-start.7
  22.6 1.3 %collective-permute-start.4 = (bf16[224,256]{1,0:T(8,128)(2,1)S(1)}, bf16[224,256]{1,0:T(8,128)(2,1)S(1)}, u32[]{:S(2)}, u32[]{:S(2)}) collective-permute-start(bf16[224,256]{1,0:T(8,128)(2,1)S(1)} %get-tuple-element.86), channel_id=1, source_target_pairs={{0,4},{2,6},{4,8},{6,10},{8,12},{10,14},{12,0},{14,2},{1,5},{3,7},... | collective-permute-start | bytes 344072 | tf_op jit(solution)/shard_map/ppermute | solution.py:409
  23.9 1.5 %collective-permute-start.5 = (bf16[224,256]{1,0:T(8,128)(2,1)S(1)}, bf16[224,256]{1,0:T(8,128)(2,1)S(1)}, u32[]{:S(2)}, u32[]{:S(2)}) collective-permute-start(bf16[224,256]{1,0:T(8,128)(2,1)S(1)} %get-tuple-element.87), channel_id=1, source_target_pairs={{0,8},{2,10},{4,12},{6,14},{8,0},{10,2},{12,4},{14,6},{1,9},{3,11}... | collective-permute-start | bytes 344072 | tf_op jit(solution)/shard_map/ppermute | solution.py:409
  25.4 2.9 %collective-permute-start.6 = (bf16[224,256]{1,0:T(8,128)(2,1)S(1)}, bf16[224,256]{1,0:T(8,128)(2,1)S(1)}, u32[]{:S(2)}, u32[]{:S(2)}) collective-permute-start(bf16[224,256]{1,0:T(8,128)(2,1)S(1)} %get-tuple-element.88), channel_id=1, source_target_pairs={{0,12},{2,14},{4,0},{6,2},{8,4},{10,6},{12,8},{14,10},{1,13},{3,15... | collective-permute-start | bytes 344072 | tf_op jit(solution)/shard_map/ppermute | solution.py:409
  28.2 0.5 collective-permute-start.8
  28.7 2.7 %gather_means.6.keep_ref = bf16[2,96,256]{2,1,0:T(8,128)(2,1)S(1)} custom-call(s32[4096]{0:T(1024)S(1)} %bitcast.12, f32[6152,128]{1,0:T(8,128)S(1)} %turn_table.1.rows), custom_call_target="tpu_custom_call" | custom-call | bytes 3000000 | tf_op jit(solution)/shard_map/gather_means/pallas_call | solution.py:516
  31.5 2.7 %gather_means.7.keep_ref = bf16[2,96,256]{2,1,0:T(8,128)(2,1)S(1)} custom-call(s32[4096]{0:T(1024)S(1)} %bitcast.13, f32[6152,128]{1,0:T(8,128)S(1)} %turn_table.1.rows), custom_call_target="tpu_custom_call" | custom-call | bytes 3000000 | tf_op jit(solution)/shard_map/gather_means/pallas_call | solution.py:516
  34.3 0.0 collective-permute-done.4.rest_1_
  34.3 0.0 collective-permute-done.5.rest_2_
  34.3 0.0 collective-permute-done.6.rest_3_
  34.3 0.2 collective-permute-done.8.pass_ref
  34.5 0.8 %collective-permute-start.9 = (bf16[192,256]{1,0:T(8,128)(2,1)S(1)}, bf16[192,256]{1,0:T(8,128)(2,1)S(1)}, u32[]{:S(2)}, u32[]{:S(2)}) collective-permute-start(bf16[192,256]{1,0:T(8,128)(2,1)S(1)} %get-tuple-element.97), channel_id=1, source_target_pairs={{0,4},{2,6},{4,8},{6,10},{8,12},{10,14},{12,0},{14,2},{1,5},{3,7},... | collective-permute-start | bytes 294920 | tf_op jit(solution)/shard_map/ppermute | solution.py:409
  35.3 2.5 %collective-permute-start.10 = (bf16[192,256]{1,0:T(8,128)(2,1)S(1)}, bf16[192,256]{1,0:T(8,128)(2,1)S(1)}, u32[]{:S(2)}, u32[]{:S(2)}) collective-permute-start(bf16[192,256]{1,0:T(8,128)(2,1)S(1)} %get-tuple-element.98), channel_id=1, source_target_pairs={{0,8},{2,10},{4,12},{6,14},{8,0},{10,2},{12,4},{14,6},{1,9},{3,11}... | collective-permute-start | bytes 294920 | tf_op jit(solution)/shard_map/ppermute | solution.py:409
  37.8 2.6 %collective-permute-start.11 = (bf16[192,256]{1,0:T(8,128)(2,1)S(1)}, bf16[192,256]{1,0:T(8,128)(2,1)S(1)}, u32[]{:S(2)}, u32[]{:S(2)}) collective-permute-start(bf16[192,256]{1,0:T(8,128)(2,1)S(1)} %get-tuple-element.99), channel_id=1, source_target_pairs={{0,12},{2,14},{4,0},{6,2},{8,4},{10,6},{12,8},{14,10},{1,13},{3,15... | collective-permute-start | bytes 294920 | tf_op jit(solution)/shard_map/ppermute | solution.py:409
  40.4 1.6 %collective-permute-done.9.rest_5_ = bf16[192,256]{1,0:T(8,128)(2,1)S(1)} collective-permute-done((bf16[192,256]{1,0:T(8,128)(2,1)S(1)}, bf16[192,256]{1,0:T(8,128)(2,1)S(1)}, u32[]{:S(2)}, u32[]{:S(2)}) %collective-permute-start.9) | collective-permute-done | bytes 98336 | tf_op jit(solution)/shard_map/ppermute | solution.py:409
  42.1 2.0 %collective-permute-done.10.rest_6_ = bf16[192,256]{1,0:T(8,128)(2,1)S(1)} collective-permute-done((bf16[192,256]{1,0:T(8,128)(2,1)S(1)}, bf16[192,256]{1,0:T(8,128)(2,1)S(1)}, u32[]{:S(2)}, u32[]{:S(2)}) %collective-permute-start.10) | collective-permute-done | bytes 98336 | tf_op jit(solution)/shard_map/ppermute | solution.py:409
  44.0 0.0 collective-permute-done.11.rest_7_
  44.0 0.0 collective-permute-done.7.far_ref.far
  44.0 0.0 collective-permute-start.12
  44.0 0.5 collective-permute-start.13
  44.5 0.4 stack_features.1
  45.0 0.1 collective-permute-start.14
  45.1 0.7 collective-permute-done.12.near_other_ref.near_other
  45.8 0.7 collective-permute-done.13.far_other_ref.far_other
  46.5 1.9 %forward.1 = (bf16[1,32,153]{2,1,0:T(8,128)(2,1)}, bf16[2,32,512]{2,1,0:T(8,128)(2,1)S(1)}, bf16[384,512]{1,0:T(8,128)(2,1)S(1)}) custom-call(s32[1,256]{1,0:T(1,128)S(1)} %copy-done.6, bf16[768,384]{1,0:T(8,128)(2,1)S(1)} %get-tuple-element.104.own_ref, bf16[768,384]{1,0:T(8,128)(2,1)S(1)} %get-tuple-element.105.mean_ref, ...), custom_call_target="tpu_custom_call" | custom-call | bytes 9000000 | tf_op jit(solution)/shard_map/forward/pallas_call | solution.py:574
  48.4 0.1 collective-permute-start.15
  48.5 0.4 collective-permute-start.16
  48.9 1.3 %collective-permute-done.16.hid_other_ref = bf16[2,32,512]{2,1,0:T(8,128)(2,1)S(1)} collective-permute-done((bf16[2,32,512]{2,1,0:T(8,128)(2,1)S(1)}, bf16[2,32,512]{2,1,0:T(8,128)(2,1)S(1)}, u32[]{:S(2)}, u32[]{:S(2)}) %collective-permute-start.16) | collective-permute-done | bytes 65568 | tf_op jit(solution)/shard_map/ppermute | solution.py:405
  50.2 1.0 %products.1 = (f32[4,96,512]{2,1,0:T(8,128)S(1)}, bf16[4,96,512]{2,1,0:T(8,128)(2,1)S(1)}, bf16[64,512]{1,0:T(8,128)(2,1)S(1)}) custom-call(bf16[768,384]{1,0:T(8,128)(2,1)S(1)} %get-tuple-element.104.own_ref, bf16[768,384]{1,0:T(8,128)(2,1)S(1)} %get-tuple-element.105.mean_ref, bf16[768,384]{1,0:T(8,128)(2,1)S(1)} %collective-permute-done.14.x_ref, ...), custom_call_target="tpu_custom_call" | custom-call | bytes 6000000 | tf_op jit(solution)/shard_map/products/pallas_call | solution.py:597
  51.2 1.1 %collective-permute-start.17 = (bf16[4,96,512]{2,1,0:T(8,128)(2,1)S(1)}, bf16[4,96,512]{2,1,0:T(8,128)(2,1)S(1)}, u32[]{:S(2)}, u32[]{:S(2)}) collective-permute-start(bf16[4,96,512]{2,1,0:T(8,128)(2,1)S(1)} %get-tuple-element.113), channel_id=1, source_target_pairs={{0,2},{2,0},{4,6},{6,4},{8,10},{10,8},{12,14},{14,12},{1,3},{3,1},... | collective-permute-start | bytes 1179656 | tf_op jit(solution)/shard_map/ppermute | solution.py:413
  52.3 0.8 %collective-permute-start.18 = (bf16[64,512]{1,0:T(8,128)(2,1)S(1)}, bf16[64,512]{1,0:T(8,128)(2,1)S(1)}, u32[]{:S(2)}, u32[]{:S(2)}) collective-permute-start(bf16[64,512]{1,0:T(8,128)(2,1)S(1)} %get-tuple-element.115.first), channel_id=1, source_target_pairs={{0,8},{2,10},{4,12},{6,14},{8,0},{10,2},{12,4},{14,6},{1,9},{3,11}... | collective-permute-start | bytes 196616 | tf_op jit(solution)/shard_map/ppermute | solution.py:413
  53.1 5.8 %collective-permute-done.18.second = bf16[64,512]{1,0:T(8,128)(2,1)S(1)} collective-permute-done((bf16[64,512]{1,0:T(8,128)(2,1)S(1)}, bf16[64,512]{1,0:T(8,128)(2,1)S(1)}, u32[]{:S(2)}, u32[]{:S(2)}) %collective-permute-start.18) | collective-permute-done | bytes 65568 | tf_op jit(solution)/shard_map/ppermute | solution.py:413
  58.8 0.5 collective-permute-start.19
  59.4 4.5 %collective-permute-done.19.second = bf16[128,512]{1,0:T(8,128)(2,1)S(1)} collective-permute-done((bf16[128,512]{1,0:T(8,128)(2,1)S(1)}, bf16[128,512]{1,0:T(8,128)(2,1)S(1)}, u32[]{:S(2)}, u32[]{:S(2)}) %collective-permute-start.19) | collective-permute-done | bytes 131104 | tf_op jit(solution)/shard_map/ppermute | solution.py:413
  63.9 1.0 %collective-permute-start.20 = (bf16[256,512]{1,0:T(8,128)(2,1)S(1)}, bf16[256,512]{1,0:T(8,128)(2,1)S(1)}, u32[]{:S(2)}, u32[]{:S(2)}) collective-permute-start(bf16[256,512]{1,0:T(8,128)(2,1)S(1)} %join_rows.7.hid_near), channel_id=1, source_target_pairs={{0,2},{2,0},{4,6},{6,4},{8,10},{10,8},{12,14},{14,12},{1,3},{3,1},... | collective-permute-start | bytes 786440 | tf_op jit(solution)/shard_map/ppermute | solution.py:413
  64.9 0.0 collective-permute-done.17.passed_ref
  64.9 0.1 join_pairs.1
  65.0 2.4 %collective-permute-start.21 = (bf16[96,512]{1,0:T(8,128)(2,1)S(1)}, bf16[96,512]{1,0:T(8,128)(2,1)S(1)}, u32[]{:S(2)}, u32[]{:S(2)}) collective-permute-start(bf16[96,512]{1,0:T(8,128)(2,1)S(1)} %get-tuple-element.116), channel_id=1, source_target_pairs={{0,12},{2,14},{4,0},{6,2},{8,4},{10,6},{12,8},{14,10},{1,13},{3,15... | collective-permute-start | bytes 294920 | tf_op jit(solution)/shard_map/ppermute | solution.py:409
  67.4 0.0 collective-permute-start.22
  67.4 0.6 collective-permute-start.23
  68.0 2.3 %collective-permute-done.20.hid_far = bf16[256,512]{1,0:T(8,128)(2,1)S(1)} collective-permute-done((bf16[256,512]{1,0:T(8,128)(2,1)S(1)}, bf16[256,512]{1,0:T(8,128)(2,1)S(1)}, u32[]{:S(2)}, u32[]{:S(2)}) %collective-permute-start.20) | collective-permute-done | bytes 262176 | tf_op jit(solution)/shard_map/ppermute | solution.py:413
  70.3 1.0 %collective-permute-done.21.rest_0_ = bf16[96,512]{1,0:T(8,128)(2,1)S(1)} collective-permute-done((bf16[96,512]{1,0:T(8,128)(2,1)S(1)}, bf16[96,512]{1,0:T(8,128)(2,1)S(1)}, u32[]{:S(2)}, u32[]{:S(2)}) %collective-permute-start.21) | collective-permute-done | bytes 98336 | tf_op jit(solution)/shard_map/ppermute | solution.py:409
  71.4 3.4 %collective-permute-done.22.rest_1_ = bf16[96,512]{1,0:T(8,128)(2,1)S(1)} collective-permute-done((bf16[96,512]{1,0:T(8,128)(2,1)S(1)}, bf16[96,512]{1,0:T(8,128)(2,1)S(1)}, u32[]{:S(2)}, u32[]{:S(2)}) %collective-permute-start.22) | collective-permute-done | bytes 98336 | tf_op jit(solution)/shard_map/ppermute | solution.py:409
  74.8 0.3 total_gradients.1
  75.1 0.1 collective-permute-start.25
  75.2 0.5 collective-permute-start.24
  75.7 1.4 %collective-permute-done.24.w_other = f32[96,512]{1,0:T(8,128)S(1)} collective-permute-done((f32[96,512]{1,0:T(8,128)S(1)}, f32[96,512]{1,0:T(8,128)S(1)}, u32[]{:S(2)}, u32[]{:S(2)}) %collective-permute-start.24) | collective-permute-done | bytes 196640 | tf_op jit(solution)/shard_map/ppermute | solution.py:405
  77.1 0.0 collective-permute-done.25.v_other
  77.1 1.0 %place_gradients.1 = (f32[96,512]{1,0:T(8,128)}, f32[96,512]{1,0:T(8,128)}, f32[153,512]{1,0:T(8,128)}, f32[153,512]{1,0:T(8,128)}) custom-call(f32[96,512]{1,0:T(8,128)S(1)} %get-tuple-element.119.w_mine, f32[96,512]{1,0:T(8,128)S(1)} %collective-permute-done.24.w_other, f32[153,512]{1,0:T(8,128)S(1)} %get-tuple-element.120.v_mine, ...), custom_call_target="tpu_custom_call" | custom-call | bytes 3000000 | tf_op jit(solution)/shard_map/place_gradients/pallas_call | solution.py:624
  (24 shorter events, 0.2 us)
Async XLA Ops:
  2.3 10.6 %collective-permute-start.1 = (bf16[112,512]{1,0:T(8,128)(2,1)S(1)}, bf16[112,512]{1,0:T(8,128)(2,1)S(1)}, u32[]{:S(2)}, u32[]{:S(2)}) collective-permute-start(bf16[112,512]{1,0:T(8,128)(2,1)S(1)} %maximum_maximum_fusion.first), channel_id=1, source_target_pairs={{0,8},{2,10},{4,12},{6,14},{8,0},{10,2},{12,4},{14,6},{1,9},{3,11}... | collective-permute-start | bytes 344072 | tf_op jit(solution)/shard_map/ppermute | solution.py:413
  8.7 8.5 %collective-permute-start = (bf16[4,112,256]{2,1,0:T(8,128)(2,1)}, bf16[4,112,256]{2,1,0:T(8,128)(2,1)S(1)}, u32[]{:S(2)}, u32[]{:S(2)}) collective-permute-start(bf16[4,112,256]{2,1,0:T(8,128)(2,1)} %get-tuple-element.66), channel_id=1, source_target_pairs={{0,2},{2,0},{4,6},{6,4},{8,10},{10,8},{12,14},{14,12},{1,3},{3,1},... | collective-permute-start | bytes 688136 | tf_op jit(solution)/shard_map/ppermute | solution.py:413
  10.3 1.3 %copy-start = (bf16[1,96,6144]{2,1,0:T(8,128)(2,1)S(1)}, bf16[1,96,6144]{2,1,0:T(8,128)(2,1)}, u32[]{:S(2)}) copy-start(bf16[1,96,6144]{2,1,0:T(8,128)(2,1)} %table.1) | copy-start | bytes 3538948
  11.6 2.9 %copy-start.1 = (s32[32,128]{1,0:T(8,128)S(1)}, s32[32,128]{1,0:T(8,128)}, u32[]{:S(2)}) copy-start(s32[32,128]{1,0:T(8,128)} %get-tuple-element.67) | copy-start | bytes 49156
  11.6 6.3 %copy-start.2 = (bf16[4,112,256]{2,1,0:T(8,128)(2,1)S(1)}, bf16[4,112,256]{2,1,0:T(8,128)(2,1)}, u32[]{:S(2)}) copy-start(bf16[4,112,256]{2,1,0:T(8,128)(2,1)} %get-tuple-element.65.keep_ref) | copy-start | bytes 688132
  12.9 9.1 %collective-permute-start.3 = (bf16[224,512]{1,0:T(8,128)(2,1)S(1)}, bf16[224,512]{1,0:T(8,128)(2,1)S(1)}, u32[]{:S(2)}, u32[]{:S(2)}) collective-permute-start(bf16[224,512]{1,0:T(8,128)(2,1)S(1)} %join_rows.4.first), channel_id=1, source_target_pairs={{0,4},{2,6},{4,0},{6,2},{8,12},{10,14},{12,8},{14,10},{1,5},{3,7},... | collective-permute-start | bytes 688136 | tf_op jit(solution)/shard_map/ppermute | solution.py:413
  17.3 4.7 %collective-permute-start.2 = (bf16[2,96,256]{2,1,0:T(8,128)(2,1)S(1)}, bf16[2,96,256]{2,1,0:T(8,128)(2,1)S(1)}, u32[]{:S(2)}, u32[]{:S(2)}) collective-permute-start(bf16[2,96,256]{2,1,0:T(8,128)(2,1)S(1)} %gather_means.4), channel_id=1, source_target_pairs={{0,2},{2,0},{4,6},{6,4},{8,10},{10,8},{12,14},{14,12},{1,3},{3,1},... | collective-permute-start | bytes 294920 | tf_op jit(solution)/shard_map/ppermute | solution.py:413
  22.0 22.0 %collective-permute-start.7 = (bf16[448,512]{1,0:T(8,128)(2,1)S(1)}, bf16[448,512]{1,0:T(8,128)(2,1)S(1)}, u32[]{:S(2)}, u32[]{:S(2)}) collective-permute-start(bf16[448,512]{1,0:T(8,128)(2,1)S(1)} %join_rows.5.near_ref.near), channel_id=1, source_target_pairs={{0,2},{2,0},{4,6},{6,4},{8,10},{10,8},{12,14},{14,12},{1,3},{3,1},... | collective-permute-start | bytes 1376264 | tf_op jit(solution)/shard_map/ppermute | solution.py:413
  22.6 11.7 %collective-permute-start.4 = (bf16[224,256]{1,0:T(8,128)(2,1)S(1)}, bf16[224,256]{1,0:T(8,128)(2,1)S(1)}, u32[]{:S(2)}, u32[]{:S(2)}) collective-permute-start(bf16[224,256]{1,0:T(8,128)(2,1)S(1)} %get-tuple-element.86), channel_id=1, source_target_pairs={{0,4},{2,6},{4,8},{6,10},{8,12},{10,14},{12,0},{14,2},{1,5},{3,7},... | collective-permute-start | bytes 344072 | tf_op jit(solution)/shard_map/ppermute | solution.py:409
  23.9 10.4 %collective-permute-start.5 = (bf16[224,256]{1,0:T(8,128)(2,1)S(1)}, bf16[224,256]{1,0:T(8,128)(2,1)S(1)}, u32[]{:S(2)}, u32[]{:S(2)}) collective-permute-start(bf16[224,256]{1,0:T(8,128)(2,1)S(1)} %get-tuple-element.87), channel_id=1, source_target_pairs={{0,8},{2,10},{4,12},{6,14},{8,0},{10,2},{12,4},{14,6},{1,9},{3,11}... | collective-permute-start | bytes 344072 | tf_op jit(solution)/shard_map/ppermute | solution.py:409
  25.4 19.2 %copy-start.6 = (s32[1,256]{1,0:T(1,128)S(1)}, s32[1,256]{1,0:T(1,128)}, u32[]{:S(2)}) copy-start(s32[1,256]{1,0:T(1,128)} %seed_degree_ref.3) | copy-start | bytes 3076
  25.4 21.1 %copy-start.3 = (bf16[512,153]{0,1:T(8,128)(2,1)S(1)}, bf16[512,153]{0,1:T(8,128)(2,1)}, u32[]{:S(2)}) copy-start(bf16[512,153]{0,1:T(8,128)(2,1)} %param.19) | copy-start | bytes 470020
  25.4 21.1 %copy-start.4 = (bf16[512,153]{0,1:T(8,128)(2,1)S(1)}, bf16[512,153]{0,1:T(8,128)(2,1)}, u32[]{:S(2)}) copy-start(bf16[512,153]{0,1:T(8,128)(2,1)} %param.20) | copy-start | bytes 470020
  25.4 21.1 %copy-start.5 = (bf16[1,32,153]{2,1,0:T(8,128)(2,1)S(1)}, bf16[1,32,153]{2,1,0:T(8,128)(2,1)}, u32[]{:S(2)}) copy-start(bf16[1,32,153]{2,1,0:T(8,128)(2,1)} %cot_ref.1) | copy-start | bytes 29380
  25.4 8.9 %collective-permute-start.6 = (bf16[224,256]{1,0:T(8,128)(2,1)S(1)}, bf16[224,256]{1,0:T(8,128)(2,1)S(1)}, u32[]{:S(2)}, u32[]{:S(2)}) collective-permute-start(bf16[224,256]{1,0:T(8,128)(2,1)S(1)} %get-tuple-element.88), channel_id=1, source_target_pairs={{0,12},{2,14},{4,0},{6,2},{8,4},{10,6},{12,8},{14,10},{1,13},{3,15... | collective-permute-start | bytes 344072 | tf_op jit(solution)/shard_map/ppermute | solution.py:409
  28.2 6.2 %collective-permute-start.8 = (bf16[2,96,256]{2,1,0:T(8,128)(2,1)S(1)}, bf16[2,96,256]{2,1,0:T(8,128)(2,1)S(1)}, u32[]{:S(2)}, u32[]{:S(2)}) collective-permute-start(bf16[2,96,256]{2,1,0:T(8,128)(2,1)S(1)} %gather_means.5), channel_id=1, source_target_pairs={{0,2},{2,0},{4,6},{6,4},{8,10},{10,8},{12,14},{14,12},{1,3},{3,1},... | collective-permute-start | bytes 294920 | tf_op jit(solution)/shard_map/ppermute | solution.py:413
  34.5 7.6 %collective-permute-start.9 = (bf16[192,256]{1,0:T(8,128)(2,1)S(1)}, bf16[192,256]{1,0:T(8,128)(2,1)S(1)}, u32[]{:S(2)}, u32[]{:S(2)}) collective-permute-start(bf16[192,256]{1,0:T(8,128)(2,1)S(1)} %get-tuple-element.97), channel_id=1, source_target_pairs={{0,4},{2,6},{4,8},{6,10},{8,12},{10,14},{12,0},{14,2},{1,5},{3,7},... | collective-permute-start | bytes 294920 | tf_op jit(solution)/shard_map/ppermute | solution.py:409
  35.3 8.7 %collective-permute-start.10 = (bf16[192,256]{1,0:T(8,128)(2,1)S(1)}, bf16[192,256]{1,0:T(8,128)(2,1)S(1)}, u32[]{:S(2)}, u32[]{:S(2)}) collective-permute-start(bf16[192,256]{1,0:T(8,128)(2,1)S(1)} %get-tuple-element.98), channel_id=1, source_target_pairs={{0,8},{2,10},{4,12},{6,14},{8,0},{10,2},{12,4},{14,6},{1,9},{3,11}... | collective-permute-start | bytes 294920 | tf_op jit(solution)/shard_map/ppermute | solution.py:409
  37.8 6.2 %collective-permute-start.11 = (bf16[192,256]{1,0:T(8,128)(2,1)S(1)}, bf16[192,256]{1,0:T(8,128)(2,1)S(1)}, u32[]{:S(2)}, u32[]{:S(2)}) collective-permute-start(bf16[192,256]{1,0:T(8,128)(2,1)S(1)} %get-tuple-element.99), channel_id=1, source_target_pairs={{0,12},{2,14},{4,0},{6,2},{8,4},{10,6},{12,8},{14,10},{1,13},{3,15... | collective-permute-start | bytes 294920 | tf_op jit(solution)/shard_map/ppermute | solution.py:409
  44.0 1.8 %collective-permute-start.12 = (bf16[448,512]{1,0:T(8,128)(2,1)S(1)}, bf16[448,512]{1,0:T(8,128)(2,1)S(1)}, u32[]{:S(2)}, u32[]{:S(2)}) collective-permute-start(bf16[448,512]{1,0:T(8,128)(2,1)S(1)} %join_rows.5.near_ref.near), channel_id=1, source_target_pairs={{0,1},{1,0},{2,3},{3,2},{4,5},{5,4},{6,7},{7,6},{8,9},{9,8},{10,11... | collective-permute-start | bytes 1376264 | tf_op jit(solution)/shard_map/ppermute | solution.py:405
  44.0 2.5 %collective-permute-start.13 = (bf16[448,512]{1,0:T(8,128)(2,1)S(1)}, bf16[448,512]{1,0:T(8,128)(2,1)S(1)}, u32[]{:S(2)}, u32[]{:S(2)}) collective-permute-start(bf16[448,512]{1,0:T(8,128)(2,1)S(1)} %collective-permute-done.7.far_ref.far), channel_id=1, source_target_pairs={{0,1},{1,0},{2,3},{3,2},{4,5},{5,4},{6,7},{7,6},{8,9},{9,8},{10,11... | collective-permute-start | bytes 1376264 | tf_op jit(solution)/shard_map/ppermute | solution.py:405
  45.0 5.3 %collective-permute-start.14 = (bf16[768,384]{1,0:T(8,128)(2,1)S(1)}, bf16[768,384]{1,0:T(8,128)(2,1)S(1)}, u32[]{:S(2)}, u32[]{:S(2)}) collective-permute-start(bf16[768,384]{1,0:T(8,128)(2,1)S(1)} %get-tuple-element.109), channel_id=1, source_target_pairs={{0,1},{1,0},{2,3},{3,2},{4,5},{5,4},{6,7},{7,6},{8,9},{9,8},{10,11... | collective-permute-start | bytes 1769480 | tf_op jit(solution)/shard_map/ppermute | solution.py:405
  48.4 1.8 %collective-permute-start.15 = (bf16[384,512]{1,0:T(8,128)(2,1)S(1)}, bf16[384,512]{1,0:T(8,128)(2,1)S(1)}, u32[]{:S(2)}, u32[]{:S(2)}) collective-permute-start(bf16[384,512]{1,0:T(8,128)(2,1)S(1)} %get-tuple-element.110.dpre_ref), channel_id=1, source_target_pairs={{0,1},{1,0},{2,3},{3,2},{4,5},{5,4},{6,7},{7,6},{8,9},{9,8},{10,11... | collective-permute-start | bytes 1179656 | tf_op jit(solution)/shard_map/ppermute | solution.py:405
  48.5 1.7 %collective-permute-start.16 = (bf16[2,32,512]{2,1,0:T(8,128)(2,1)S(1)}, bf16[2,32,512]{2,1,0:T(8,128)(2,1)S(1)}, u32[]{:S(2)}, u32[]{:S(2)}) collective-permute-start(bf16[2,32,512]{2,1,0:T(8,128)(2,1)S(1)} %get-tuple-element.111.hid_ref), channel_id=1, source_target_pairs={{0,1},{1,0},{2,3},{3,2},{4,5},{5,4},{6,7},{7,6},{8,9},{9,8},{10,11... | collective-permute-start | bytes 196616 | tf_op jit(solution)/shard_map/ppermute | solution.py:405
  51.2 13.7 %collective-permute-start.17 = (bf16[4,96,512]{2,1,0:T(8,128)(2,1)S(1)}, bf16[4,96,512]{2,1,0:T(8,128)(2,1)S(1)}, u32[]{:S(2)}, u32[]{:S(2)}) collective-permute-start(bf16[4,96,512]{2,1,0:T(8,128)(2,1)S(1)} %get-tuple-element.113), channel_id=1, source_target_pairs={{0,2},{2,0},{4,6},{6,4},{8,10},{10,8},{12,14},{14,12},{1,3},{3,1},... | collective-permute-start | bytes 1179656 | tf_op jit(solution)/shard_map/ppermute | solution.py:413
  52.3 6.6 %collective-permute-start.18 = (bf16[64,512]{1,0:T(8,128)(2,1)S(1)}, bf16[64,512]{1,0:T(8,128)(2,1)S(1)}, u32[]{:S(2)}, u32[]{:S(2)}) collective-permute-start(bf16[64,512]{1,0:T(8,128)(2,1)S(1)} %get-tuple-element.115.first), channel_id=1, source_target_pairs={{0,8},{2,10},{4,12},{6,14},{8,0},{10,2},{12,4},{14,6},{1,9},{3,11}... | collective-permute-start | bytes 196616 | tf_op jit(solution)/shard_map/ppermute | solution.py:413
  58.8 5.0 %collective-permute-start.19 = (bf16[128,512]{1,0:T(8,128)(2,1)S(1)}, bf16[128,512]{1,0:T(8,128)(2,1)S(1)}, u32[]{:S(2)}, u32[]{:S(2)}) collective-permute-start(bf16[128,512]{1,0:T(8,128)(2,1)S(1)} %join_rows.6.first), channel_id=1, source_target_pairs={{0,4},{2,6},{4,0},{6,2},{8,12},{10,14},{12,8},{14,10},{1,5},{3,7},... | collective-permute-start | bytes 393224 | tf_op jit(solution)/shard_map/ppermute | solution.py:413
  63.9 6.4 %collective-permute-start.20 = (bf16[256,512]{1,0:T(8,128)(2,1)S(1)}, bf16[256,512]{1,0:T(8,128)(2,1)S(1)}, u32[]{:S(2)}, u32[]{:S(2)}) collective-permute-start(bf16[256,512]{1,0:T(8,128)(2,1)S(1)} %join_rows.7.hid_near), channel_id=1, source_target_pairs={{0,2},{2,0},{4,6},{6,4},{8,10},{10,8},{12,14},{14,12},{1,3},{3,1},... | collective-permute-start | bytes 786440 | tf_op jit(solution)/shard_map/ppermute | solution.py:413
  65.0 6.4 %collective-permute-start.21 = (bf16[96,512]{1,0:T(8,128)(2,1)S(1)}, bf16[96,512]{1,0:T(8,128)(2,1)S(1)}, u32[]{:S(2)}, u32[]{:S(2)}) collective-permute-start(bf16[96,512]{1,0:T(8,128)(2,1)S(1)} %get-tuple-element.116), channel_id=1, source_target_pairs={{0,12},{2,14},{4,0},{6,2},{8,4},{10,6},{12,8},{14,10},{1,13},{3,15... | collective-permute-start | bytes 294920 | tf_op jit(solution)/shard_map/ppermute | solution.py:409
  67.4 7.4 %collective-permute-start.22 = (bf16[96,512]{1,0:T(8,128)(2,1)S(1)}, bf16[96,512]{1,0:T(8,128)(2,1)S(1)}, u32[]{:S(2)}, u32[]{:S(2)}) collective-permute-start(bf16[96,512]{1,0:T(8,128)(2,1)S(1)} %get-tuple-element.117), channel_id=1, source_target_pairs={{0,8},{2,10},{4,12},{6,14},{8,0},{10,2},{12,4},{14,6},{1,9},{3,11}... | collective-permute-start | bytes 294920 | tf_op jit(solution)/shard_map/ppermute | solution.py:409
  67.4 7.4 %collective-permute-start.23 = (bf16[96,512]{1,0:T(8,128)(2,1)S(1)}, bf16[96,512]{1,0:T(8,128)(2,1)S(1)}, u32[]{:S(2)}, u32[]{:S(2)}) collective-permute-start(bf16[96,512]{1,0:T(8,128)(2,1)S(1)} %get-tuple-element.118), channel_id=1, source_target_pairs={{0,4},{2,6},{4,8},{6,10},{8,12},{10,14},{12,0},{14,2},{1,5},{3,7},... | collective-permute-start | bytes 294920 | tf_op jit(solution)/shard_map/ppermute | solution.py:409
  75.1 2.0 %collective-permute-start.25 = (f32[153,512]{1,0:T(8,128)S(1)}, f32[153,512]{1,0:T(8,128)S(1)}, u32[]{:S(2)}, u32[]{:S(2)}) collective-permute-start(f32[153,512]{1,0:T(8,128)S(1)} %get-tuple-element.120.v_mine), channel_id=1, source_target_pairs={{0,1},{1,0},{2,3},{3,2},{4,5},{5,4},{6,7},{7,6},{8,9},{9,8},{10,11... | collective-permute-start | bytes 940040 | tf_op jit(solution)/shard_map/ppermute | solution.py:405
  75.2 1.9 %collective-permute-start.24 = (f32[96,512]{1,0:T(8,128)S(1)}, f32[96,512]{1,0:T(8,128)S(1)}, u32[]{:S(2)}, u32[]{:S(2)}) collective-permute-start(f32[96,512]{1,0:T(8,128)S(1)} %get-tuple-element.119.w_mine), channel_id=1, source_target_pairs={{0,1},{1,0},{2,3},{3,2},{4,5},{5,4},{6,7},{7,6},{8,9},{9,8},{10,11... | collective-permute-start | bytes 589832 | tf_op jit(solution)/shard_map/ppermute | solution.py:405
